TPU v7x, 512 devices: a whole 4x8x8 slice. The times are simulated.
512 devices in a mesh: lead: 16 (over z, core), lat: 32 (over x, y).
Axes of the slice: x: 4, y: 8, z: 8, core: 2. Of those that a mesh axis runs over, the one named last changes fastest.
Arguments:
- window: bfloat16 [16, 96, 192, 768], P('lead', 'lat'), may hold values from -10 to 10
- noise_level: float32 [16], replicated, may hold values from 0.1 to 10
- keep_ratio: float32 [16], replicated, may hold values from 0.3 to 0.95
- norm_gains: float32 [3, 768], replicated, may hold values from 0.5 to 1.5
- w_qkv: bfloat16 [768, 1152], replicated, may hold values from -0.19921875 to 0.19921875
- w_out: bfloat16 [384, 768], replicated, may hold values from -0.3125 to 0.3125
- spectral_filter: bfloat16 [96, 768], replicated, may hold values from -2.5 to 2.5
- w_in: bfloat16 [1536, 768], P('lead'), may hold values from -0.21875 to 0.21875
- w_down: bfloat16 [1536, 768], P('lead'), may hold values from -0.15625 to 0.15625
Outputs:
- next_window: bfloat16 [16, 96, 192, 768], P('lead', 'lat')
All inputs are finite; a program needn't handle non-finite values.
Results may differ from a plain program's by a relative error of at most 0.011.
Values may be sent and summed in bfloat16 or wider, within the bound.
No kernel may reach another device: no remote copies, remote signals or barrier semaphores. Data moves between devices by JAX's collectives and lax.ppermute only.
A program may use at most 64 MiB of HBM per device.

v0:
```python
import jax
import jax.numpy as jnp
import ml_dtypes
import numpy as np
from jax import lax
from jax.experimental import pallas as pl
from jax.experimental.pallas import tpu as pltpu
from jax.sharding import PartitionSpec as P

F32, BF16 = jnp.float32, jnp.bfloat16
FRAMES, LATS, ROWS, NLON, NLAT, LMAX = 16, 32, 3, 192, 96, 96
POINTS, WIDTH, ATTN, FF = ROWS * NLON, 768, 384, 1536
ORDERS = LMAX // LATS
EPS = 1e-05
MIB = 1 << 20


def chunk_row(r):
    return r // 6, (r // 2) % 3, r % 2


def chunk_columns():
    listed = [(d,) + chunk_row(r) for d in range(LATS) for r in range(16)]
    for d in range(LATS):
        listed += [(d,) + chunk_row(16 + s % 2) if s < 6 else None for s in range(8)]
    return listed


def fourier_tables():
    forward = np.zeros((768, ROWS, NLON))
    inverse = np.zeros((768, ROWS, NLON))
    lon = np.arange(NLON)
    for at, entry in enumerate(chunk_columns()):
        if entry is None:
            continue
        owner, j, i, c = entry
        m = ORDERS * owner + i
        angle = 2 * np.pi * ((m * lon) % NLON) / NLON
        wave = np.cos(angle) if c == 0 else -np.sin(angle)
        forward[at, j] = wave
        inverse[at, j] = wave * (1.0 if m == 0 else 2.0)
    return (
        forward.reshape(768, POINTS).astype(ml_dtypes.bfloat16),
        np.ascontiguousarray(inverse.reshape(768, POINTS).T).astype(ml_dtypes.bfloat16),
    )


def placement_table():
    table = np.zeros((ORDERS, 2, NLAT, 768))
    for at, entry in enumerate(chunk_columns()):
        if entry is not None:
            source, j, i, c = entry
            table[i, c, ROWS * source + j, at] = 1.0
    return table.astype(ml_dtypes.bfloat16)


def legendre_tables():
    colatitude = np.pi * (np.arange(NLAT) + 0.5) / NLAT
    cosines = np.cos(colatitude)
    sine_rows = np.sin(colatitude)
    legendre = np.zeros((LMAX, LMAX, NLAT))
    for order_m in range(LMAX):
        counter = np.arange(1, order_m + 1)
        log_part = (
            0.5 * np.log((2 * order_m + 1) / (4 * np.pi))
            + 0.5 * np.sum(np.log((2 * counter - 1) / (2 * counter)))
            + order_m * np.log(sine_rows)
        )
        diagonal_value = (-1.0) ** order_m * np.exp(log_part)
        legendre[order_m, order_m] = diagonal_value
        if order_m + 1 < LMAX:
            legendre[order_m, order_m + 1] = cosines * np.sqrt(2 * order_m + 3) * diagonal_value
        for degree_l in range(order_m + 2, LMAX):
            factor_a = np.sqrt(
                (4.0 * degree_l * degree_l - 1) / (degree_l * degree_l - order_m * order_m)
            )
            factor_b = np.sqrt(
                ((degree_l - 1.0) ** 2 - order_m * order_m) / (4.0 * (degree_l - 1) ** 2 - 1)
            )
            legendre[order_m, degree_l] = factor_a * (
                cosines * legendre[order_m, degree_l - 1]
                - factor_b * legendre[order_m, degree_l - 2]
            )
    quadrature = sine_rows * (np.pi / NLAT) * (2 * np.pi / NLON)
    return legendre.astype(np.float32).astype(ml_dtypes.bfloat16), quadrature.astype(np.float32)


def swap4(first, second):
    low = lax.broadcasted_iota(jnp.int32, first.shape, 1) < 4
    rolled_first, rolled_second = pltpu.roll(first, 4, 1), pltpu.roll(second, 4, 1)
    return jnp.where(low, first, rolled_second), jnp.where(low, rolled_first, second)


def pairs(tiles):
    split = tiles.reshape(8, 2, 8, 128)
    return split[:, 0], split[:, 1]


def frame_scale(level):
    return lax.rsqrt(1.0 + level * level)


def row_scale(values):
    return lax.rsqrt(jnp.sum(values * values, axis=-1, keepdims=True) * (1.0 / WIDTH) + EPS)


def pack_window(window_ref, out_ref):
    for d in range(FRAMES):
        for block in range(2):
            for c in range(6):
                at = (block * 6 + c) * 16
                out_ref[d, at : at + 16, :] = window_ref[
                    32 * d + 16 * block : 32 * d + 16 * block + 16, 128 * c : 128 * c + 128
                ]
    for q in range(3):
        left = window_ref[512:576, 256 * q : 256 * q + 128].astype(F32).reshape(8, 8, 128)
        right = window_ref[512:576, 256 * q + 128 : 256 * q + 256].astype(F32).reshape(8, 8, 128)
        even, odd = swap4(left, right)
        at = 192 + 8 * q
        for i in range(8):
            out_ref[2 * i, at : at + 8, :] = even[i].astype(BF16)
            out_ref[2 * i + 1, at : at + 8, :] = odd[i].astype(BF16)


def attend(noise_ref, gains_ref, in_ref, w_ref, out_ref, x_ref, proj_ref):
    level = jnp.concatenate([jnp.full((1, 8, 128), noise_ref[f], F32) for f in range(FRAMES)], 0)
    scale = frame_scale(level)
    gain = [gains_ref[0:1, 128 * c : 128 * c + 128].reshape(1, 1, 128) for c in range(6)]
    for s in range(4):
        at = (s // 2) * 96 + 8 * (s % 2)
        parts = [in_ref[:, at + 16 * c : at + 16 * c + 8, :].astype(F32) * scale for c in range(6)]
        squares = sum(v * v for v in parts)
        r = lax.rsqrt(jnp.sum(squares, axis=-1, keepdims=True) * (1.0 / WIDTH) + EPS)
        for c in range(6):
            x_ref[128 * s : 128 * s + 128, 128 * c : 128 * c + 128] = (
                (parts[c] * r * gain[c]).reshape(128, 128).astype(BF16)
            )
    parts = [in_ref[:, 192 + 8 * q : 200 + 8 * q, :].astype(F32) * scale for q in range(3)]
    squares = sum(v * v for v in parts)
    total = jnp.broadcast_to(jnp.sum(squares, axis=-1, keepdims=True), squares.shape)
    r = lax.rsqrt((total + pltpu.roll(total, 4, 1)) * (1.0 / WIDTH) + EPS)
    low = lax.broadcasted_iota(jnp.int32, (1, 8, 128), 1) < 4
    for q in range(3):
        both = parts[q] * r * jnp.where(low, gain[2 * q], gain[2 * q + 1])
        left, right = swap4(*pairs(both))
        x_ref[512:576, 256 * q : 256 * q + 128] = left.reshape(64, 128).astype(BF16)
        x_ref[512:576, 256 * q + 128 : 256 * q + 256] = right.reshape(64, 128).astype(BF16)
    for b in range(3):
        proj_ref[:, ATTN * b : ATTN * (b + 1)] = jnp.dot(
            x_ref[...], w_ref[:, ATTN * b : ATTN * (b + 1)], preferred_element_type=F32
        ).astype(BF16)

    def mix(base, n):
        size = FRAMES * n
        row = lax.broadcasted_iota(jnp.int32, (1, size, size), 1)
        col = lax.broadcasted_iota(jnp.int32, (1, size, size), 2)
        kept = ((row & (n - 1)) == (col & (n - 1))) & (col // n <= row // n)
        lane = lax.broadcasted_iota(jnp.int32, (size, 128), 1) < 64
        one = jnp.where(lane, 1.0, 0.0).astype(BF16)
        other = jnp.where(lane, 0.0, 1.0).astype(BF16)
        results = []
        for h in range(3):
            q = proj_ref[base : base + size, 128 * h : 128 * h + 128]
            k = proj_ref[base : base + size, ATTN + 128 * h : ATTN + 128 * h + 128]
            v = proj_ref[base : base + size, 2 * ATTN + 128 * h : 2 * ATTN + 128 * h + 128]
            scores = lax.dot_general(
                jnp.concatenate([q * one, q * other], 0),
                k,
                (((1,), (1,)), ((), ())),
                preferred_element_type=F32,
            )
            scores = jnp.where(kept, scores.reshape(2, size, size) * 0.125, -1e30)
            expo = jnp.exp(scores - jnp.max(scores, axis=-1, keepdims=True))
            total = jnp.sum(expo, axis=-1, keepdims=True)
            weights = expo.reshape(2 * size, size).astype(BF16)
            mixed = jnp.dot(weights, v, preferred_element_type=F32).reshape(2, size, 128) / total
            results.append(jnp.where(lane, mixed[0], mixed[1]))
        return results

    for s in range(4):
        for h, mixed in enumerate(mix(128 * s, 8)):
            at = (s // 2) * 48 + 16 * h + 8 * (s % 2)
            mixed = mixed.reshape(FRAMES, 8, 128).astype(BF16)
            out_ref[0:15, at : at + 8, :] = mixed[1:16]
            out_ref[15:16, at : at + 8, :] = mixed[0:1]
    rest = [mixed.reshape(8, 8, 128) for mixed in mix(512, 4)]
    for at, (even, odd) in ((96, swap4(rest[0], rest[1])), (104, swap4(rest[2], rest[2]))):
        for i in range(8):
            out_ref[(2 * i - 1) % FRAMES, at : at + 8, :] = even[i].astype(BF16)
            out_ref[2 * i, at : at + 8, :] = odd[i].astype(BF16)


def put_chunks(values, out_ref):
    for c in range(6):
        block = values[:512, 128 * c : 128 * c + 128].reshape(LATS, 16, 128)
        out_ref[:, 16 * c : 16 * c + 16, :] = block.astype(BF16)
    slot = lax.broadcasted_iota(jnp.int32, (LATS, 8, 128), 1)
    for t in range(2):
        tile = None
        for q in range(3):
            at = 256 * q + 128 * t
            part = values[512:, at : at + 128].reshape(LATS, 8, 128)
            tile = part if tile is None else jnp.where(slot // 2 == q, part, tile)
        out_ref[:, 96 + 8 * t : 104 + 8 * t, :] = tile.astype(BF16)


def get_chunks(in_ref, rows_ref):
    for c in range(6):
        rows_ref[0:512, 128 * c : 128 * c + 128] = in_ref[:, 16 * c : 16 * c + 16, :].reshape(
            512, 128
        )
    slot = lax.broadcasted_iota(jnp.int32, (LATS, 8, 128), 1)
    for t in range(2):
        tile = in_ref[:, 96 + 8 * t : 104 + 8 * t, :].astype(F32)
        for q in range(3):
            at = 256 * q + 128 * t
            rows_ref[512:768, at : at + 128] = (
                jnp.where(slot // 2 == q, tile, 0.0).reshape(256, 128).astype(BF16)
            )


def to_spectra(
    where_ref, noise_ref, quad_ref, gains_ref, mixed_ref, window_ref, w_ref, table_ref,
    first_ref, out_ref, mixed_rows, base_rows,
):
    for block in range(2):
        for h in range(3):
            at = (block * 3 + h) * 16
            for d in range(FRAMES):
                mixed_rows[
                    32 * d + 16 * block : 32 * d + 16 * block + 16, 128 * h : 128 * h + 128
                ] = mixed_ref[d, at : at + 16, :]
    left, right = swap4(*pairs(mixed_ref[:, 96:104, :].astype(F32)))
    last, _ = swap4(*pairs(mixed_ref[:, 104:112, :].astype(F32)))
    for h, tile in enumerate((left, right, last)):
        mixed_rows[512:576, 128 * h : 128 * h + 128] = tile.reshape(64, 128).astype(BF16)
    scale = frame_scale(jnp.full((1, 1), noise_ref[where_ref[0]], F32))
    gain = gains_ref[1:2, :]
    for j in range(ROWS):
        rows = slice(NLON * j, NLON * (j + 1))
        first = window_ref[rows, :].astype(F32) * scale + jnp.dot(
            mixed_rows[rows, :], w_ref[...], preferred_element_type=F32
        )
        first_ref[rows, :] = first
        weight = quad_ref[ROWS * where_ref[1] + j]
        base_rows[rows, :] = (first * (row_scale(first) * weight) * gain).astype(BF16)
    put_chunks(jnp.dot(table_ref[...], base_rows[...], preferred_element_type=F32), out_ref)


def filter_orders(in_ref, down_ref, up_ref, filter_ref, out_ref, rows_ref, coeffs_ref):
    get_chunks(in_ref, rows_ref)
    factor = filter_ref[...].astype(F32)
    coeffs = jnp.dot(down_ref[...], rows_ref[...], preferred_element_type=F32)
    for b in range(2 * ORDERS):
        rows = slice(LMAX * b, LMAX * (b + 1))
        coeffs_ref[rows, :] = (coeffs[rows] * factor).astype(BF16)
    put_chunks(jnp.dot(up_ref[...], coeffs_ref[...], preferred_element_type=F32), out_ref)


def gelu(x):
    return 0.5 * x * (1.0 + jnp.tanh(np.float32(np.sqrt(2 / np.pi)) * (x + 0.044715 * (x * x * x))))


def feed_forward(
    where_ref, keep_ref, gains_ref, in_ref, table_ref, first_ref, window_ref, w_ref,
    out_ref, rows_ref, inner_ref, total_ref,
):
    get_chunks(in_ref, rows_ref)
    gain = gains_ref[2:3, :]
    second = first_ref[...] + jnp.dot(table_ref[...], rows_ref[...], preferred_element_type=F32)
    total_ref[...] = second
    inner_ref[...] = (second * row_scale(second) * gain).astype(BF16)
    for b in range(4):
        w_in = w_ref[4 * b : 4 * b + 4, 0:96, :].reshape(384, WIDTH)
        w_down = w_ref[4 * b : 4 * b + 4, 96:192, :].reshape(384, WIDTH)
        raised = lax.dot_general(
            inner_ref[...], w_in, (((1,), (1,)), ((), ())), preferred_element_type=F32
        )
        total_ref[...] += jnp.dot(
            gelu(raised).astype(BF16), w_down, preferred_element_type=F32
        )
    frame = where_ref[0]
    ratio = jnp.where(frame == 0, 0.0, keep_ref[frame])
    denoised = total_ref[...]
    out_ref[...] = (denoised + ratio * (window_ref[...].astype(F32) - denoised)).astype(BF16)


def call(kernel, out_shape, specs, scratch, args, flops=0, moved=0, limit=40):
    spaces = {"v": pltpu.VMEM, "s": pltpu.SMEM}
    outs = out_shape if isinstance(out_shape, list) else [out_shape]
    result = pl.pallas_call(
        kernel,
        out_shape=out_shape,
        in_specs=[pl.BlockSpec(memory_space=spaces[kind]) for kind in specs],
        out_specs=jax.tree.map(lambda _: pl.BlockSpec(memory_space=pltpu.VMEM), out_shape),
        scratch_shapes=[pltpu.VMEM(shape, dtype) for shape, dtype in scratch],
        compiler_params=pltpu.CompilerParams(vmem_limit_bytes=limit * MIB),
        cost_estimate=pl.CostEstimate(
            flops=flops,
            bytes_accessed=sum(a.size * a.dtype.itemsize for a in list(args) + outs),
            transcendentals=0,
        ),
    )(*args)
    return result


def exchange(chunks, axis):
    return lax.all_to_all(chunks, axis, split_axis=0, concat_axis=0, tiled=True)


def per_device(
    window, noise_level, keep_ratio, norm_gains, w_qkv, w_out, spectral_filter, w_in, w_down
):
    lead, lat = lax.axis_index("lead"), lax.axis_index("lat")
    frame = (lead + 1) % FRAMES
    here = jnp.stack([frame, lat]).astype(jnp.int32)
    forward, inverse = (jnp.asarray(table) for table in fourier_tables())
    legendre, quadrature = (jnp.asarray(table) for table in legendre_tables())
    placement = jnp.asarray(placement_table())
    shape = jax.ShapeDtypeStruct

    state = window.reshape(POINTS, WIDTH)
    packed = call(pack_window, shape((FRAMES, 216, 128), BF16), "v", [], [state])
    ahead = lax.ppermute(
        state, "lead", [(source, (source - 1) % FRAMES) for source in range(FRAMES)]
    )
    packed, legendre = lax.optimization_barrier((packed, legendre))
    local = lax.dynamic_slice_in_dim(legendre, ORDERS * lat, ORDERS, 0)
    down = jnp.einsum("ilj,icjn->icln", local, placement, preferred_element_type=F32)
    down = down.astype(BF16).reshape(2 * ORDERS * LMAX, 768)
    up = down.T

    mixed = call(
        attend,
        shape((FRAMES, 112, 128), BF16),
        "svvv",
        [((POINTS, WIDTH), BF16), ((POINTS, 3 * ATTN), BF16)],
        [noise_level, norm_gains, exchange(packed, "lead"), w_qkv],
        flops=2 * POINTS * WIDTH * 3 * ATTN,
    )
    mixed = exchange(mixed, "lead")
    weights = jnp.concatenate([w_in, w_down], 0)
    mixed, weights = lax.optimization_barrier((mixed, weights))
    weights = lax.all_gather(weights, "lead", axis=0, tiled=False)
    first, spectra = call(
        to_spectra,
        [shape((POINTS, WIDTH), F32), shape((LATS, 112, 128), BF16)],
        "sssvvvvv",
        [((POINTS, ATTN), BF16), ((POINTS, WIDTH), BF16)],
        [here, noise_level, quadrature, norm_gains, mixed, ahead, w_out, forward],
        flops=2 * POINTS * WIDTH * (ATTN + 768),
    )
    back = call(
        filter_orders,
        shape((LATS, 112, 128), BF16),
        "vvvv",
        [((768, WIDTH), BF16), ((2 * ORDERS * LMAX, WIDTH), BF16)],
        [exchange(spectra, "lat"), down, up, spectral_filter],
        flops=4 * POINTS * WIDTH * 768,
    )
    stepped = call(
        feed_forward,
        shape((POINTS, WIDTH), BF16),
        "ssvvvvvv",
        [((768, WIDTH), BF16), ((POINTS, WIDTH), BF16), ((POINTS, WIDTH), F32)],
        [here, keep_ratio, norm_gains, exchange(back, "lat"), inverse, first, ahead, weights],
        flops=2 * POINTS * WIDTH * (2 * FF + 768),
    )
    return stepped.reshape(1, ROWS, NLON, WIDTH)


def solution(mesh):
    return jax.shard_map(
        per_device,
        mesh=mesh,
        in_specs=(
            P("lead", "lat", None, None),
            P(),
            P(),
            P(),
            P(),
            P(),
            P(),
            P("lead", None),
            P("lead", None),
        ),
        out_specs=P("lead", "lat", None, None),
        check_vma=False,
    )
```

profile of v0, /device:TPU:1, one launch (start us, length us, event | category | flops | bytes accessed | tf_op | source)
XLA Modules:
  0.0 170.7 jit_solution(15878161016348375640)
XLA Ops:
  6.5 0.0 copy-start.9
  6.5 0.0 copy-start
  6.5 1.2 copy-done
  7.7 0.0 copy-start.3
  7.7 0.0 copy-start.8
  7.7 0.2 shard_map.136
  7.9 36.8 %all_to_all.20.in_ref = bf16[16,216,128]{2,1,0:T(8,128)(2,1)S(1)} all-to-all(bf16[16,216,128]{2,1,0:T(8,128)(2,1)S(1)} %shard_map.136), channel_id=1, replica_groups=mesh['lead'=16,'lat'=32] {'lead'}, dimensions={0} | all-to-all | bytes 1769472 | tf_op jit(solution)/shard_map/all_to_all | solution.py:308
  44.7 0.0 copy-done.9
  44.7 0.0 copy-done.3
  44.7 0.0 copy-done.8
  44.7 0.0 copy-start.16
  44.7 0.0 copy-start.17
  44.7 0.0 copy-start.1
  44.7 0.0 copy-start.6
  44.7 0.0 copy-start.13
  44.8 4.1 %shard_map.137 = bf16[16,112,128]{2,1,0:T(8,128)(2,1)} custom-call(f32[16]{0:T(128)S(1)} %copy-done.9, f32[3,768]{1,0:T(4,128)S(1)} %copy-done.8, bf16[16,216,128]{2,1,0:T(8,128)(2,1)S(1)} %all_to_all.20.in_ref, bf16[768,1152]{1,0:T(8,128)(2,1)S(1)} %copy-done.3), custom_call_target="tpu_custom_call" | custom-call | flops 1019215872 | bytes 3122240 | tf_op jit(solution)/shard_map/pallas_call | solution.py:291
  48.9 3.5 %all-to-all-start.1 = ((bf16[16,112,128]{2,1,0:T(8,128)(2,1)}), bf16[16,112,128]{2,1,0:T(8,128)(2,1)S(1)}, u32[]{:S(2)}, u32[]{:S(2)}) async-start(bf16[16,112,128]{2,1,0:T(8,128)(2,1)} %shard_map.137), calls=%async_computation.1 | async-start | bytes 917504 | tf_op jit(solution)/shard_map/all_to_all | solution.py:308
  52.3 0.0 all-gather.3.cloned.1.call-start
  52.4 0.0 copy-done.16
  52.4 0.0 copy-done.17
  52.4 0.7 pad_maximum_fusion
  53.1 14.5 %all-to-all-done.1.mixed_ref = bf16[16,112,128]{2,1,0:T(8,128)(2,1)S(1)} async-done(((bf16[16,112,128]{2,1,0:T(8,128)(2,1)}), bf16[16,112,128]{2,1,0:T(8,128)(2,1)S(1)}, u32[]{:S(2)}, u32[]{:S(2)}) %all-to-all-start.1) | async-done | bytes 458784 | tf_op jit(solution)/shard_map/all_to_all | solution.py:308
  67.7 0.0 all-gather.3.cloned.1.call-update
  67.7 0.0 copy-done.1
  67.7 0.0 collective-permute-start
  67.7 0.1 pad_add_fusion.where_ref
  67.8 12.4 %collective-permute-done.window_ref = bf16[576,768]{1,0:T(8,128)(2,1)S(1)} collective-permute-done((bf16[576,768]{1,0:T(8,128)(2,1)S(1)}, bf16[576,768]{1,0:T(8,128)(2,1)S(1)}, u32[]{:S(2)}, u32[]{:S(2)}) %collective-permute-start) | collective-permute-done | bytes 884768 | tf_op jit(solution)/shard_map/ppermute | solution.py:324
  80.2 0.0 copy-done.6
  80.2 0.0 copy-done.13
  80.2 0.0 copy-start.11
  80.2 1.2 copy-done.11
  81.4 0.0 copy-start.4
  81.4 3.5 %shard_map.138 = (f32[576,768]{1,0:T(8,128)S(1)}, bf16[32,112,128]{2,1,0:T(8,128)(2,1)}) custom-call(s32[2]{0:T(128)S(1)} %pad_add_fusion.where_ref, f32[16]{0:T(128)S(1)} %copy-done.9, f32[96]{0:T(128)S(1)} %copy-done.13, f32[3,768]{1,0:T(4,128)S(1)} %copy-done.8, bf16[16,112,128]{2,1,0:T(8,128)(2,1)S(1)} %all-to-all-done.1.mixed_ref, ...), custom_call_target="tpu_custom_call" | custom-call | flops 1019215872 | bytes 5514696 | tf_op jit(solution)/shard_map/pallas_call | solution.py:291
  84.9 1.3 copy-done.14
  86.1 0.0 copy-done.4
  86.2 9.9 %all-to-all-start.2 = ((bf16[32,112,128]{2,1,0:T(8,128)(2,1)}), bf16[32,112,128]{2,1,0:T(8,128)(2,1)S(1)}, u32[]{:S(2)}, u32[]{:S(2)}) async-start(bf16[32,112,128]{2,1,0:T(8,128)(2,1)} %get-tuple-element.13), calls=%async_computation.2 | async-start | bytes 1835008 | tf_op jit(solution)/shard_map/all_to_all | solution.py:308
  96.1 1.6 convolution_convert_fusion
  97.7 0.6 copy.17
  98.3 22.1 %all-to-all-done.2.in_ref = bf16[32,112,128]{2,1,0:T(8,128)(2,1)S(1)} async-done(((bf16[32,112,128]{2,1,0:T(8,128)(2,1)}), bf16[32,112,128]{2,1,0:T(8,128)(2,1)S(1)}, u32[]{:S(2)}, u32[]{:S(2)}) %all-to-all-start.2) | async-done | bytes 917536 | tf_op jit(solution)/shard_map/all_to_all | solution.py:308
  120.4 0.0 copy-done.7
  120.4 2.0 %shard_map.139 = bf16[32,112,128]{2,1,0:T(8,128)(2,1)S(1)} custom-call(bf16[32,112,128]{2,1,0:T(8,128)(2,1)S(1)} %all-to-all-done.2.in_ref, bf16[576,768]{1,0:T(8,128)(2,1)S(1)} %bitcast.16, bf16[768,576]{1,0:T(8,128)(2,1)S(1)} %bitcast.17, bf16[96,768]{1,0:T(8,128)(2,1)S(1)} %copy-done.7), custom_call_target="tpu_custom_call" | custom-call | flops 1358954496 | bytes 3751936 | tf_op jit(solution)/shard_map/pallas_call | solution.py:291
  122.4 28.3 %all_to_all.21.in_ref = bf16[32,112,128]{2,1,0:T(8,128)(2,1)S(1)} all-to-all(bf16[32,112,128]{2,1,0:T(8,128)(2,1)S(1)} %shard_map.139), channel_id=1, replica_groups=mesh['lead'=16,'lat'=32] {'lat'}, dimensions={0} | all-to-all | bytes 1835008 | tf_op jit(solution)/shard_map/all_to_all | solution.py:308
  150.7 0.0 copy-done.10
  150.7 2.3 %copy-done.2 = bf16[3072,768]{1,0:T(8,128)(2,1)S(1)} copy-done((bf16[3072,768]{1,0:T(8,128)(2,1)S(1)}, bf16[3072,768]{1,0:T(8,128)(2,1)}, u32[]{:S(2)}) %copy-start.2) | copy-done | bytes 4718616
  153.1 1.2 copy-done.5
  154.2 1.2 copy-done.12
  155.4 1.5 copy-done.15
  156.9 6.9 %shard_map.140 = bf16[576,768]{1,0:T(8,128)(2,1)} custom-call(s32[2]{0:T(128)S(1)} %pad_add_fusion.where_ref, f32[16]{0:T(128)S(1)} %copy-done.10, f32[3,768]{1,0:T(4,128)S(1)} %copy-done.8, bf16[32,112,128]{2,1,0:T(8,128)(2,1)S(1)} %all_to_all.21.in_ref, bf16[576,768]{1,0:T(8,128)(2,1)S(1)} %copy-done.12, f32[576,768]{1,0:T(8,128)S(1)} %copy-done.15, ...), custom_call_target="tpu_custom_call" | custom-call | flops 3397386240 | bytes 10069064 | tf_op jit(solution)/shard_map/pallas_call | solution.py:291
  (8 shorter events, 0.0 us)
Async XLA Ops:
  6.5 38.1 %copy-start.9 = (f32[16]{0:T(128)S(1)}, f32[16]{0:T(128)}, u32[]{:S(2)}) copy-start(f32[16]{0:T(128)} %noise_ref.3) | copy-start | bytes 196
  6.5 1.2 copy-start
  7.7 37.0 %copy-start.3 = (bf16[768,1152]{1,0:T(8,128)(2,1)S(1)}, bf16[768,1152]{1,0:T(8,128)(2,1)}, u32[]{:S(2)}) copy-start(bf16[768,1152]{1,0:T(8,128)(2,1)} %w_ref.2) | copy-start | bytes 5308420
  7.7 37.0 %copy-start.8 = (f32[3,768]{1,0:T(4,128)S(1)}, f32[3,768]{1,0:T(4,128)}, u32[]{:S(2)}) copy-start(f32[3,768]{1,0:T(4,128)} %gains_ref.5) | copy-start | bytes 27652
  44.7 7.7 %copy-start.16 = (bf16[96,768]{1,0:T(8,128)(2,1)S(1)}, bf16[96,768]{1,0:T(8,128)(2,1)}, u32[]{:S(2)}) copy-start(bf16[96,768]{1,0:T(8,128)(2,1)} %param.22) | copy-start | bytes 442372
  44.7 7.7 %copy-start.17 = (bf16[96,768]{1,0:T(8,128)(2,1)S(1)}, bf16[96,768]{1,0:T(8,128)(2,1)}, u32[]{:S(2)}) copy-start(bf16[96,768]{1,0:T(8,128)(2,1)} %param.21) | copy-start | bytes 442372
  44.7 23.0 %copy-start.1 = (bf16[1,3,192,768]{3,2,1,0:T(8,128)(2,1)S(1)}, bf16[1,3,192,768]{3,2,1,0:T(8,128)(2,1)}, u32[]{:S(2)}) copy-start(bf16[1,3,192,768]{3,2,1,0:T(8,128)(2,1)} %param.14) | copy-start | bytes 2654212
  44.7 35.5 %copy-start.6 = (bf16[384,768]{1,0:T(8,128)(2,1)S(1)}, bf16[384,768]{1,0:T(8,128)(2,1)}, u32[]{:S(2)}) copy-start(bf16[384,768]{1,0:T(8,128)(2,1)} %w_ref.3) | copy-start | bytes 1769476
  44.7 35.4 %copy-start.13 = (f32[96]{0:T(128)S(1)}, f32[96]{0:T(128)}, u32[]{:S(2)}) copy-start(f32[96]{0:T(128)} %constant.42.clone.quad_ref) | copy-start | bytes 1156
  48.9 18.8 %all-to-all-start.1 = ((bf16[16,112,128]{2,1,0:T(8,128)(2,1)}), bf16[16,112,128]{2,1,0:T(8,128)(2,1)S(1)}, u32[]{:S(2)}, u32[]{:S(2)}) async-start(bf16[16,112,128]{2,1,0:T(8,128)(2,1)} %shard_map.137), calls=%async_computation.1 | async-start | bytes 917504 | tf_op jit(solution)/shard_map/all_to_all | solution.py:308
  52.3 98.4 %all-gather.3.cloned.1.call-start = ((), (), s32[]{:S(2)}) async-start(), calls=%async_computation.4 | async-start | bytes 5013504 | tf_op jit(solution)/shard_map/all_gather | solution.py:344
  67.7 12.5 %collective-permute-start = (bf16[576,768]{1,0:T(8,128)(2,1)S(1)}, bf16[576,768]{1,0:T(8,128)(2,1)S(1)}, u32[]{:S(2)}, u32[]{:S(2)}) collective-permute-start(bf16[576,768]{1,0:T(8,128)(2,1)S(1)} %bitcast.19), channel_id=1, source_target_pairs={{0,480},{32,0},{64,32},{96,64},{128,96},{160,128},{192,160},{224,1... | collective-permute-start | bytes 2654216 | tf_op jit(solution)/shard_map/ppermute | solution.py:324
  80.2 1.2 copy-start.11
  81.4 4.8 %copy-start.4 = (bf16[576,768]{1,0:T(8,128)(2,1)}, bf16[576,768]{1,0:T(8,128)(2,1)S(1)}, u32[]{:S(2)}) copy-start(bf16[576,768]{1,0:T(8,128)(2,1)S(1)} %collective-permute-done.window_ref) | copy-start | bytes 2654212
  84.9 1.3 copy-start.14
  86.1 34.3 %copy-start.7 = (bf16[96,768]{1,0:T(8,128)(2,1)S(1)}, bf16[96,768]{1,0:T(8,128)(2,1)}, u32[]{:S(2)}) copy-start(bf16[96,768]{1,0:T(8,128)(2,1)} %filter_ref.1) | copy-start | bytes 442372
  86.2 34.2 %all-to-all-start.2 = ((bf16[32,112,128]{2,1,0:T(8,128)(2,1)}), bf16[32,112,128]{2,1,0:T(8,128)(2,1)S(1)}, u32[]{:S(2)}, u32[]{:S(2)}) async-start(bf16[32,112,128]{2,1,0:T(8,128)(2,1)} %get-tuple-element.13), calls=%async_computation.2 | async-start | bytes 1835008 | tf_op jit(solution)/shard_map/all_to_all | solution.py:308
  120.4 30.3 %copy-start.10 = (f32[16]{0:T(128)S(1)}, f32[16]{0:T(128)}, u32[]{:S(2)}) copy-start(f32[16]{0:T(128)} %keep_ref.1) | copy-start | bytes 196
  150.7 2.3 %copy-start.2 = (bf16[3072,768]{1,0:T(8,128)(2,1)S(1)}, bf16[3072,768]{1,0:T(8,128)(2,1)}, u32[]{:S(2)}) copy-start(bf16[3072,768]{1,0:T(8,128)(2,1)} %all-gather.3.cloned.1.call-done) | copy-start | bytes 14155780
  153.1 1.2 copy-start.5
  154.2 1.2 copy-start.12
  155.4 1.5 copy-start.15
Sparse Core Ops, SparseCore 0:
  67.8 43.1 all-gather.2
where the time goes:
time: 172 us; the launch traced here: 171 us
  blocking collectives  65.1 us (38%)
  waiting for transfers between devices  49 us (28%)
  Pallas kernels  16.7 us (10%)
  between operations  13.5 us (8%)
  starting transfers between devices  13.4 us (8%)
  local copies, waits for them, and re-layouts  10.5 us (6%)
    all_to_all x2, blocking collectives, exchange(): return lax.all_to_all(chunks, axis, split_axis=0, concat_axis=0, tiled=True)  65.1 us
    all_to_all x2, waiting for transfers between devices, exchange(): return lax.all_to_all(chunks, axis, split_axis=0, concat_axis=0, tiled=True)  36.6 us
    pallas_call x5, Pallas kernels, call(): pl.pallas_call(kernel, out_shape=out_shape, in_specs=[pl.BlockSpec(memory...  16.7 us
    all_to_all x2, starting transfers between devices, exchange(): return lax.all_to_all(chunks, axis, split_axis=0, concat_axis=0, tiled=True)  13.4 us
    ppermute x1, waiting for transfers between devices, per_device(): lax.ppermute(state, 'lead', [(source, (source - 1) % FRAMES) for source i...  12.4 us
    unnamed x36, local copies, waits for them, and re-layouts  9.86 us
  transfers between devices with their start and end apart: 4, of which 3 were waited for; matrix products, arithmetic and copies ran while one was open for 2% of the time, Pallas kernels for 3%

commit v1 on v0

--- a/solution.py
+++ b/solution.py
@@ -13,6 +13,7 @@
 ORDERS = LMAX // LATS
 EPS = 1e-05
 MIB = 1 << 20
+LIMITS = (60, 51, 52, 45, 51)
 
 
 def chunk_row(r):
@@ -39,10 +40,10 @@
         wave = np.cos(angle) if c == 0 else -np.sin(angle)
         forward[at, j] = wave
         inverse[at, j] = wave * (1.0 if m == 0 else 2.0)
-    return (
-        forward.reshape(768, POINTS).astype(ml_dtypes.bfloat16),
-        np.ascontiguousarray(inverse.reshape(768, POINTS).T).astype(ml_dtypes.bfloat16),
-    )
+    tables = np.zeros((2, 768, 768))
+    tables[0, :, :POINTS] = forward.reshape(768, POINTS)
+    tables[1, :POINTS] = inverse.reshape(768, POINTS).T
+    return tables.astype(ml_dtypes.bfloat16)
 
 
 def placement_table():
@@ -82,7 +83,7 @@
                 - factor_b * legendre[order_m, degree_l - 2]
             )
     quadrature = sine_rows * (np.pi / NLAT) * (2 * np.pi / NLON)
-    return legendre.astype(np.float32).astype(ml_dtypes.bfloat16), quadrature.astype(np.float32)
+    return np.stack([legendre * quadrature, legendre]).astype(ml_dtypes.bfloat16)
 
 
 def swap4(first, second):
@@ -96,6 +97,12 @@
     return split[:, 0], split[:, 1]
 
 
+def fetch(source, target, sem):
+    copy = pltpu.make_async_copy(source, target, sem)
+    copy.start()
+    return copy
+
+
 def frame_scale(level):
     return lax.rsqrt(1.0 + level * level)
 
@@ -104,22 +111,27 @@
     return lax.rsqrt(jnp.sum(values * values, axis=-1, keepdims=True) * (1.0 / WIDTH) + EPS)
 
 
-def pack_window(window_ref, out_ref):
-    for d in range(FRAMES):
-        for block in range(2):
-            for c in range(6):
-                at = (block * 6 + c) * 16
-                out_ref[d, at : at + 16, :] = window_ref[
-                    32 * d + 16 * block : 32 * d + 16 * block + 16, 128 * c : 128 * c + 128
-                ]
-    for q in range(3):
-        left = window_ref[512:576, 256 * q : 256 * q + 128].astype(F32).reshape(8, 8, 128)
-        right = window_ref[512:576, 256 * q + 128 : 256 * q + 256].astype(F32).reshape(8, 8, 128)
-        even, odd = swap4(left, right)
-        at = 192 + 8 * q
+def pack_window(window_any, out_any, last_ref, packed_ref, sems):
+    last = fetch(window_any.at[16:18], last_ref, sems.at[0])
+    copies = [
+        fetch(
+            window_any.at[0:16, :, :, ATTN * h : ATTN * h + ATTN],
+            out_any.at[:, 4 * h : 4 * h + 4],
+            sems.at[1 + h],
+        )
+        for h in range(2)
+    ]
+    last.wait()
+    for c in range(3):
+        left = last_ref[:, :, :, 128 * c : 128 * c + 128].astype(F32).reshape(8, 8, 128)
+        right = last_ref[:, :, :, ATTN + 128 * c : ATTN + 128 * c + 128].astype(F32)
+        even, odd = swap4(left, right.reshape(8, 8, 128))
         for i in range(8):
-            out_ref[2 * i, at : at + 8, :] = even[i].astype(BF16)
-            out_ref[2 * i + 1, at : at + 8, :] = odd[i].astype(BF16)
+            packed_ref[2 * i, :, 128 * c : 128 * c + 128] = even[i].astype(BF16)
+            packed_ref[2 * i + 1, :, 128 * c : 128 * c + 128] = odd[i].astype(BF16)
+    copies.append(fetch(packed_ref, out_any.at[:, 8], sems.at[3]))
+    for copy in copies:
+        copy.wait()
 
 
 def attend(noise_ref, gains_ref, in_ref, w_ref, out_ref, x_ref, proj_ref):
@@ -127,24 +139,26 @@
     scale = frame_scale(level)
     gain = [gains_ref[0:1, 128 * c : 128 * c + 128].reshape(1, 1, 128) for c in range(6)]
     for s in range(4):
-        at = (s // 2) * 96 + 8 * (s % 2)
-        parts = [in_ref[:, at + 16 * c : at + 16 * c + 8, :].astype(F32) * scale for c in range(6)]
+        parts = [
+            in_ref[:, 4 * (c // 3) + s, :, 128 * (c % 3) : 128 * (c % 3) + 128].astype(F32) * scale
+            for c in range(6)
+        ]
         squares = sum(v * v for v in parts)
         r = lax.rsqrt(jnp.sum(squares, axis=-1, keepdims=True) * (1.0 / WIDTH) + EPS)
         for c in range(6):
             x_ref[128 * s : 128 * s + 128, 128 * c : 128 * c + 128] = (
                 (parts[c] * r * gain[c]).reshape(128, 128).astype(BF16)
             )
-    parts = [in_ref[:, 192 + 8 * q : 200 + 8 * q, :].astype(F32) * scale for q in range(3)]
+    parts = [in_ref[:, 8, :, 128 * c : 128 * c + 128].astype(F32) * scale for c in range(3)]
     squares = sum(v * v for v in parts)
     total = jnp.broadcast_to(jnp.sum(squares, axis=-1, keepdims=True), squares.shape)
     r = lax.rsqrt((total + pltpu.roll(total, 4, 1)) * (1.0 / WIDTH) + EPS)
     low = lax.broadcasted_iota(jnp.int32, (1, 8, 128), 1) < 4
-    for q in range(3):
-        both = parts[q] * r * jnp.where(low, gain[2 * q], gain[2 * q + 1])
+    for c in range(3):
+        both = parts[c] * r * jnp.where(low, gain[c], gain[c + 3])
         left, right = swap4(*pairs(both))
-        x_ref[512:576, 256 * q : 256 * q + 128] = left.reshape(64, 128).astype(BF16)
-        x_ref[512:576, 256 * q + 128 : 256 * q + 256] = right.reshape(64, 128).astype(BF16)
+        x_ref[512:576, 128 * c : 128 * c + 128] = left.reshape(64, 128).astype(BF16)
+        x_ref[512:576, ATTN + 128 * c : ATTN + 128 * c + 128] = right.reshape(64, 128).astype(BF16)
     for b in range(3):
         proj_ref[:, ATTN * b : ATTN * (b + 1)] = jnp.dot(
             x_ref[...], w_ref[:, ATTN * b : ATTN * (b + 1)], preferred_element_type=F32
@@ -220,9 +234,12 @@
 
 
 def to_spectra(
-    where_ref, noise_ref, quad_ref, gains_ref, mixed_ref, window_ref, w_ref, table_ref,
-    first_ref, out_ref, mixed_rows, base_rows,
+    frame_ref, noise_ref, gains_ref, mixed_ref, window_any, w_any, tables_any,
+    first_any, out_ref, mixed_rows, base_rows, first_ref, window_ref, w_ref, table_ref, sems,
 ):
+    w_copy = fetch(w_any, w_ref, sems.at[0])
+    window_copy = fetch(window_any, window_ref, sems.at[1])
+    table_copy = fetch(tables_any.at[0, :, 0:640], table_ref, sems.at[2])
     for block in range(2):
         for h in range(3):
             at = (block * 3 + h) * 16
@@ -234,17 +251,20 @@
     last, _ = swap4(*pairs(mixed_ref[:, 104:112, :].astype(F32)))
     for h, tile in enumerate((left, right, last)):
         mixed_rows[512:576, 128 * h : 128 * h + 128] = tile.reshape(64, 128).astype(BF16)
-    scale = frame_scale(jnp.full((1, 1), noise_ref[where_ref[0]], F32))
+    scale = frame_scale(jnp.full((1, 1), noise_ref[frame_ref[0]], F32))
     gain = gains_ref[1:2, :]
-    for j in range(ROWS):
-        rows = slice(NLON * j, NLON * (j + 1))
-        first = window_ref[rows, :].astype(F32) * scale + jnp.dot(
-            mixed_rows[rows, :], w_ref[...], preferred_element_type=F32
-        )
-        first_ref[rows, :] = first
-        weight = quad_ref[ROWS * where_ref[1] + j]
-        base_rows[rows, :] = (first * (row_scale(first) * weight) * gain).astype(BF16)
+    w_copy.wait()
+    window_copy.wait()
+    first = window_ref[...].astype(F32) * scale + jnp.dot(
+        mixed_rows[...], w_ref[...], preferred_element_type=F32
+    )
+    first_ref[...] = first
+    first_copy = fetch(first_ref, first_any, sems.at[3])
+    base_rows[0:POINTS, :] = (first * row_scale(first) * gain).astype(BF16)
+    base_rows[POINTS:640, :] = jnp.zeros((640 - POINTS, WIDTH), BF16)
+    table_copy.wait()
     put_chunks(jnp.dot(table_ref[...], base_rows[...], preferred_element_type=F32), out_ref)
+    first_copy.wait()
 
 
 def filter_orders(in_ref, down_ref, up_ref, filter_ref, out_ref, rows_ref, coeffs_ref):
@@ -262,46 +282,71 @@
 
 
 def feed_forward(
-    where_ref, keep_ref, gains_ref, in_ref, table_ref, first_ref, window_ref, w_ref,
-    out_ref, rows_ref, inner_ref, total_ref,
+    frame_ref, keep_ref, gains_ref, in_ref, tables_any, first_any, window_any, weights_any,
+    out_any, rows_ref, inner_ref, hidden_ref, out_ref, table_ref, first_ref, window_ref,
+    w_in_ref, w_down_ref, sems,
 ):
+    table_copy = fetch(tables_any.at[1, 0:POINTS], table_ref, sems.at[0])
+    first_copy = fetch(first_any, first_ref, sems.at[1])
     get_chunks(in_ref, rows_ref)
+    in_copy = fetch(weights_any.at[:, 0:96, :], w_in_ref, sems.at[2])
     gain = gains_ref[2:3, :]
+    table_copy.wait()
+    first_copy.wait()
+    down_copy = fetch(weights_any.at[:, 96:192, :], w_down_ref, sems.at[3])
+    window_copy = fetch(window_any, window_ref, sems.at[4])
     second = first_ref[...] + jnp.dot(table_ref[...], rows_ref[...], preferred_element_type=F32)
-    total_ref[...] = second
+    first_ref[...] = second
     inner_ref[...] = (second * row_scale(second) * gain).astype(BF16)
-    for b in range(4):
-        w_in = w_ref[4 * b : 4 * b + 4, 0:96, :].reshape(384, WIDTH)
-        w_down = w_ref[4 * b : 4 * b + 4, 96:192, :].reshape(384, WIDTH)
+    in_copy.wait()
+    for b in range(2):
+        units = slice(8 * b, 8 * b + 8)
         raised = lax.dot_general(
-            inner_ref[...], w_in, (((1,), (1,)), ((), ())), preferred_element_type=F32
+            inner_ref[...],
+            w_in_ref[units].reshape(FF // 2, WIDTH),
+            (((1,), (1,)), ((), ())),
+            preferred_element_type=F32,
         )
-        total_ref[...] += jnp.dot(
-            gelu(raised).astype(BF16), w_down, preferred_element_type=F32
+        hidden_ref[:, FF // 2 * b : FF // 2 * (b + 1)] = gelu(raised).astype(BF16)
+    frame = frame_ref[0]
+    ratio = jnp.where(frame == 0, 0.0, keep_ref[frame])
+    down_copy.wait()
+    window_copy.wait()
+    w_down = w_down_ref[...].reshape(FF, WIDTH)
+    copies = []
+    for j in range(2):
+        rows = slice(POINTS // 2 * j, POINTS // 2 * (j + 1))
+        denoised = first_ref[rows, :] + jnp.dot(
+            hidden_ref[rows, :], w_down, preferred_element_type=F32
         )
-    frame = where_ref[0]
-    ratio = jnp.where(frame == 0, 0.0, keep_ref[frame])
-    denoised = total_ref[...]
-    out_ref[...] = (denoised + ratio * (window_ref[...].astype(F32) - denoised)).astype(BF16)
-
-
-def call(kernel, out_shape, specs, scratch, args, flops=0, moved=0, limit=40):
-    spaces = {"v": pltpu.VMEM, "s": pltpu.SMEM}
-    outs = out_shape if isinstance(out_shape, list) else [out_shape]
-    result = pl.pallas_call(
+        state = window_ref[rows, :].astype(F32)
+        out_ref[rows, :] = (denoised + ratio * (state - denoised)).astype(BF16)
+        copies.append(fetch(out_ref.at[rows], out_any.at[rows], sems.at[5 + j]))
+    for copy in copies:
+        copy.wait()
+
+
+SPACES = {"v": pltpu.VMEM, "s": pltpu.SMEM, "h": pltpu.HBM}
+
+
+def call(kernel, outs, kinds, scratch, args, flops, limit):
+    specs = [pl.BlockSpec(memory_space=SPACES[kind]) for kind in kinds]
+    return pl.pallas_call(
         kernel,
-        out_shape=out_shape,
-        in_specs=[pl.BlockSpec(memory_space=spaces[kind]) for kind in specs],
-        out_specs=jax.tree.map(lambda _: pl.BlockSpec(memory_space=pltpu.VMEM), out_shape),
-        scratch_shapes=[pltpu.VMEM(shape, dtype) for shape, dtype in scratch],
-        compiler_params=pltpu.CompilerParams(vmem_limit_bytes=limit * MIB),
+        out_shape=outs,
+        in_specs=specs[: len(args)],
+        out_specs=specs[len(args) :],
+        scratch_shapes=[
+            pltpu.VMEM(*entry) if isinstance(entry, tuple) else pltpu.SemaphoreType.DMA((entry,))
+            for entry in scratch
+        ],
+        compiler_params=pltpu.CompilerParams(vmem_limit_bytes=int(limit * MIB)),
         cost_estimate=pl.CostEstimate(
             flops=flops,
             bytes_accessed=sum(a.size * a.dtype.itemsize for a in list(args) + outs),
             transcendentals=0,
         ),
     )(*args)
-    return result
 
 
 def exchange(chunks, axis):
@@ -312,32 +357,42 @@
     window, noise_level, keep_ratio, norm_gains, w_qkv, w_out, spectral_filter, w_in, w_down
 ):
     lead, lat = lax.axis_index("lead"), lax.axis_index("lat")
-    frame = (lead + 1) % FRAMES
-    here = jnp.stack([frame, lat]).astype(jnp.int32)
-    forward, inverse = (jnp.asarray(table) for table in fourier_tables())
-    legendre, quadrature = (jnp.asarray(table) for table in legendre_tables())
+    frame = ((lead + 1) & (FRAMES - 1)).astype(jnp.int32).reshape(1)
+    tables = jnp.asarray(fourier_tables())
+    legendre = jnp.asarray(legendre_tables())
     placement = jnp.asarray(placement_table())
     shape = jax.ShapeDtypeStruct
 
     state = window.reshape(POINTS, WIDTH)
-    packed = call(pack_window, shape((FRAMES, 216, 128), BF16), "v", [], [state])
+    (packed,) = call(
+        pack_window,
+        [shape((FRAMES, 9, 8, ATTN), BF16)],
+        "hh",
+        [((2, 4, 8, WIDTH), BF16), ((FRAMES, 8, ATTN), BF16), 4],
+        [window.reshape(18, 4, 8, WIDTH)],
+        0,
+        LIMITS[0],
+    )
     ahead = lax.ppermute(
         state, "lead", [(source, (source - 1) % FRAMES) for source in range(FRAMES)]
     )
     packed, legendre = lax.optimization_barrier((packed, legendre))
-    local = lax.dynamic_slice_in_dim(legendre, ORDERS * lat, ORDERS, 0)
-    down = jnp.einsum("ilj,icjn->icln", local, placement, preferred_element_type=F32)
+    local = lax.dynamic_slice_in_dim(legendre, ORDERS * lat, ORDERS, 1)
+    down = jnp.einsum("ilj,icjn->icln", local[0], placement, preferred_element_type=F32)
     down = down.astype(BF16).reshape(2 * ORDERS * LMAX, 768)
-    up = down.T
-
-    mixed = call(
+    up = jnp.einsum("ilj,icjn->nicl", local[1], placement, preferred_element_type=F32)
+    up = up.astype(BF16).reshape(768, 2 * ORDERS * LMAX)
+
+    (mixed,) = call(
         attend,
-        shape((FRAMES, 112, 128), BF16),
-        "svvv",
+        [shape((FRAMES, 112, 128), BF16)],
+        "svvvv",
         [((POINTS, WIDTH), BF16), ((POINTS, 3 * ATTN), BF16)],
         [noise_level, norm_gains, exchange(packed, "lead"), w_qkv],
-        flops=2 * POINTS * WIDTH * 3 * ATTN,
-    )
+        2 * POINTS * WIDTH * 3 * ATTN,
+        LIMITS[1],
+    )
+    mixed, ahead = lax.optimization_barrier((mixed, ahead))
     mixed = exchange(mixed, "lead")
     weights = jnp.concatenate([w_in, w_down], 0)
     mixed, weights = lax.optimization_barrier((mixed, weights))
@@ -345,26 +400,48 @@
     first, spectra = call(
         to_spectra,
         [shape((POINTS, WIDTH), F32), shape((LATS, 112, 128), BF16)],
-        "sssvvvvv",
-        [((POINTS, ATTN), BF16), ((POINTS, WIDTH), BF16)],
-        [here, noise_level, quadrature, norm_gains, mixed, ahead, w_out, forward],
-        flops=2 * POINTS * WIDTH * (ATTN + 768),
-    )
-    back = call(
+        "ssvvhhhhv",
+        [
+            ((POINTS, ATTN), BF16),
+            ((640, WIDTH), BF16),
+            ((POINTS, WIDTH), F32),
+            ((POINTS, WIDTH), BF16),
+            ((ATTN, WIDTH), BF16),
+            ((768, 640), BF16),
+            4,
+        ],
+        [frame, noise_level, norm_gains, mixed, ahead, w_out, tables],
+        2 * POINTS * WIDTH * (ATTN + 768),
+        LIMITS[2],
+    )
+    (back,) = call(
         filter_orders,
-        shape((LATS, 112, 128), BF16),
-        "vvvv",
+        [shape((LATS, 112, 128), BF16)],
+        "vvvvv",
         [((768, WIDTH), BF16), ((2 * ORDERS * LMAX, WIDTH), BF16)],
         [exchange(spectra, "lat"), down, up, spectral_filter],
-        flops=4 * POINTS * WIDTH * 768,
-    )
-    stepped = call(
+        4 * POINTS * WIDTH * 768,
+        LIMITS[3],
+    )
+    (stepped,) = call(
         feed_forward,
-        shape((POINTS, WIDTH), BF16),
-        "ssvvvvvv",
-        [((768, WIDTH), BF16), ((POINTS, WIDTH), BF16), ((POINTS, WIDTH), F32)],
-        [here, keep_ratio, norm_gains, exchange(back, "lat"), inverse, first, ahead, weights],
-        flops=2 * POINTS * WIDTH * (2 * FF + 768),
+        [shape((POINTS, WIDTH), BF16)],
+        "ssvvhhhhh",
+        [
+            ((768, WIDTH), BF16),
+            ((POINTS, WIDTH), BF16),
+            ((POINTS, FF), BF16),
+            ((POINTS, WIDTH), BF16),
+            ((POINTS, 768), BF16),
+            ((POINTS, WIDTH), F32),
+            ((POINTS, WIDTH), BF16),
+            ((FRAMES, 96, WIDTH), BF16),
+            ((FRAMES, 96, WIDTH), BF16),
+            7,
+        ],
+        [frame, keep_ratio, norm_gains, exchange(back, "lat"), tables, first, ahead, weights],
+        2 * POINTS * WIDTH * (2 * FF + 768),
+        LIMITS[4],
     )
     return stepped.reshape(1, ROWS, NLON, WIDTH)
 

time: 172 us -> 185 us (1.076)
  the two profiles are of different devices: /device:TPU:1 before, /device:TPU:8 now
where the time goes in v1:
time: 185 us
  waiting for transfers between devices  57 us (31%)
  Pallas kernels  44.4 us (24%)
  blocking collectives  31.5 us (17%)
  starting transfers between devices  31 us (17%)
  between operations  13.6 us (7%)
  local copies, waits for them, and re-layouts  3.2 us (2%)
  matrix products  3.2 us (2%)
    all_to_all x3, waiting for transfers between devices, exchange(): return lax.all_to_all(chunks, axis, split_axis=0, concat_axis=0, tiled=True)  56.4 us
    pallas_call x5, Pallas kernels, call(): pl.pallas_call(kernel, out_shape=outs, in_specs=specs[:len(args)], out_sp...  44.4 us
    all_to_all x1, blocking collectives, exchange(): return lax.all_to_all(chunks, axis, split_axis=0, concat_axis=0, tiled=True)  31.5 us
    all_to_all x3, starting transfers between devices, exchange(): return lax.all_to_all(chunks, axis, split_axis=0, concat_axis=0, tiled=True)  28 us
  transfers between devices with their start and end apart: 5, of which 4 were waited for; matrix products, arithmetic and copies ran while one was open for 2% of the time, Pallas kernels for 6%

profile of v1, /device:TPU:8, one launch (start us, length us, event | category | flops | bytes accessed | tf_op | source)
XLA Modules:
  0.0 184.6 jit_solution(4455571121795992480)
XLA Ops:
  6.5 0.0 copy-start.6
  6.5 0.0 copy-start.4
  6.5 0.0 copy-start.10
  6.5 0.0 copy-start.9
  6.5 0.0 copy-start.2
  6.5 25.0 %shard_map.118 = bf16[16,9,8,384]{3,2,1,0:T(8,128)(2,1)} custom-call(bf16[18,4,8,768]{3,2,1,0:T(8,128)(2,1)} %bitcast.27), custom_call_target="tpu_custom_call" | custom-call | bytes 1769472 | tf_op jit(solution)/shard_map/pallas_call | solution.py:334
  31.5 10.4 %all-to-all-start = ((bf16[16,9,8,384]{3,2,1,0:T(8,128)(2,1)}), bf16[16,9,8,384]{3,2,1,0:T(8,128)(2,1)S(1)}, u32[]{:S(2)}, u32[]{:S(2)}) async-start(bf16[16,9,8,384]{3,2,1,0:T(8,128)(2,1)} %shard_map.118), calls=%async_computation | async-start | bytes 1769472 | tf_op jit(solution)/shard_map/all_to_all | solution.py:353
  42.0 2.9 %collective-permute-start = (bf16[576,768]{1,0:T(8,128)(2,1)}, bf16[576,768]{1,0:T(8,128)(2,1)S(1)}, u32[]{:S(2)}, u32[]{:S(2)}) collective-permute-start(bf16[576,768]{1,0:T(8,128)(2,1)} %bitcast.28), channel_id=1, source_target_pairs={{0,480},{32,0},{64,32},{96,64},{128,96},{160,128},{192,160},{224,1... | collective-permute-start | bytes 2654216 | tf_op jit(solution)/shard_map/ppermute | solution.py:376
  44.9 19.7 %all-to-all-done.in_ref = bf16[16,9,8,384]{3,2,1,0:T(8,128)(2,1)S(1)} async-done(((bf16[16,9,8,384]{3,2,1,0:T(8,128)(2,1)}), bf16[16,9,8,384]{3,2,1,0:T(8,128)(2,1)S(1)}, u32[]{:S(2)}, u32[]{:S(2)}) %all-to-all-start) | async-done | bytes 884768 | tf_op jit(solution)/shard_map/all_to_all | solution.py:353
  64.5 0.0 copy-start.3
  64.5 0.7 copy-done.3
  65.2 0.0 copy-start.5
  65.2 0.7 copy-done.5
  65.9 5.1 %shard_map.119 = bf16[16,112,128]{2,1,0:T(8,128)(2,1)} custom-call(f32[16]{0:T(128)S(1)} %copy-done.5, f32[3,768]{1,0:T(4,128)S(1)} %copy-done.3, bf16[16,9,8,384]{3,2,1,0:T(8,128)(2,1)S(1)} %all-to-all-done.in_ref, bf16[768,1152]{1,0:T(8,128)(2,1)} %w_ref.1), custom_call_target="tpu_custom_call" | custom-call | flops 1019215872 | bytes 3122240 | tf_op jit(solution)/shard_map/pallas_call | solution.py:334
  70.9 0.6 collective-permute-done.window_any
  71.5 0.0 copy-start
  71.5 7.3 %all-to-all-start.1 = ((bf16[16,112,128]{2,1,0:T(8,128)(2,1)}), bf16[16,112,128]{2,1,0:T(8,128)(2,1)S(1)}, u32[]{:S(2)}, u32[]{:S(2)}) async-start(bf16[16,112,128]{2,1,0:T(8,128)(2,1)} %shard_map.119), calls=%async_computation.1 | async-start | bytes 917504 | tf_op jit(solution)/shard_map/all_to_all | solution.py:353
  78.8 0.0 all-gather.3.cloned.1.call-start
  78.9 0.0 copy-done.10
  78.9 0.0 copy-done.9
  78.9 0.7 pad_maximum_fusion
  79.6 14.0 %all-to-all-done.1.mixed_ref = bf16[16,112,128]{2,1,0:T(8,128)(2,1)S(1)} async-done(((bf16[16,112,128]{2,1,0:T(8,128)(2,1)}), bf16[16,112,128]{2,1,0:T(8,128)(2,1)S(1)}, u32[]{:S(2)}, u32[]{:S(2)}) %all-to-all-start.1) | async-done | bytes 458784 | tf_op jit(solution)/shard_map/all_to_all | solution.py:353
  93.6 0.0 all-gather.3.cloned.1.call-update
  93.7 0.0 copy-done.6
  93.7 0.0 copy-done.4
  93.7 0.0 copy-done.2
  93.7 4.4 %shard_map.120 = (f32[576,768]{1,0:T(8,128)}, bf16[32,112,128]{2,1,0:T(8,128)(2,1)}) custom-call(s32[1]{0:T(128)} %bitcast.frame_ref, f32[16]{0:T(128)S(1)} %copy-done.6, f32[3,768]{1,0:T(4,128)S(1)} %copy-done.4, bf16[16,112,128]{2,1,0:T(8,128)(2,1)S(1)} %all-to-all-done.1.mixed_ref, bf16[576,768]{1,0:T(8,128)(2,1)S(1)} %collective-permute-done.window_any, ...), custom_call_target="tpu_custom_call" | custom-call | flops 1019215872 | bytes 6988868 | tf_op jit(solution)/shard_map/pallas_call | solution.py:334
  98.1 0.0 copy-start.7
  98.1 0.0 copy-done
  98.1 10.3 %all-to-all-start.2 = ((bf16[32,112,128]{2,1,0:T(8,128)(2,1)}), bf16[32,112,128]{2,1,0:T(8,128)(2,1)S(1)}, u32[]{:S(2)}, u32[]{:S(2)}) async-start(bf16[32,112,128]{2,1,0:T(8,128)(2,1)} %get-tuple-element.17), calls=%async_computation.2 | async-start | bytes 1835008 | tf_op jit(solution)/shard_map/all_to_all | solution.py:353
  108.4 1.6 convolution_convert_fusion
  110.0 0.6 copy.14.up_ref
  110.7 0.0 copy-start.8
  110.7 1.6 convolution_convert_fusion.1
  112.3 22.8 %all-to-all-done.2.in_ref = bf16[32,112,128]{2,1,0:T(8,128)(2,1)S(1)} async-done(((bf16[32,112,128]{2,1,0:T(8,128)(2,1)}), bf16[32,112,128]{2,1,0:T(8,128)(2,1)S(1)}, u32[]{:S(2)}, u32[]{:S(2)}) %all-to-all-start.2) | async-done | bytes 917536 | tf_op jit(solution)/shard_map/all_to_all | solution.py:353
  135.1 0.0 copy-done.7
  135.1 2.0 %shard_map.121 = bf16[32,112,128]{2,1,0:T(8,128)(2,1)S(1)} custom-call(bf16[32,112,128]{2,1,0:T(8,128)(2,1)S(1)} %all-to-all-done.2.in_ref, bf16[576,768]{1,0:T(8,128)(2,1)S(1)} %bitcast.25, bf16[768,576]{1,0:T(8,128)(2,1)S(1)} %copy.14.up_ref, bf16[96,768]{1,0:T(8,128)(2,1)S(1)} %copy-done.7), custom_call_target="tpu_custom_call" | custom-call | flops 1358954496 | bytes 3751936 | tf_op jit(solution)/shard_map/pallas_call | solution.py:334
  137.1 31.5 %all_to_all.20.in_ref = bf16[32,112,128]{2,1,0:T(8,128)(2,1)S(1)} all-to-all(bf16[32,112,128]{2,1,0:T(8,128)(2,1)S(1)} %shard_map.121), channel_id=1, replica_groups=mesh['lead'=16,'lat'=32] {'lat'}, dimensions={0} | all-to-all | bytes 1835008 | tf_op jit(solution)/shard_map/all_to_all | solution.py:353
  168.6 0.0 all-gather.3.cloned.1.call-done
  168.6 0.0 copy-done.8
  168.6 0.0 copy-start.1
  168.6 1.2 copy-done.1
  169.8 8.0 %shard_map.122 = bf16[576,768]{1,0:T(8,128)(2,1)} custom-call(s32[1]{0:T(128)} %bitcast.frame_ref, f32[16]{0:T(128)S(1)} %copy-done.8, f32[3,768]{1,0:T(4,128)S(1)} %copy-done.4, bf16[32,112,128]{2,1,0:T(8,128)(2,1)S(1)} %all_to_all.20.in_ref, bf16[2,768,768]{2,1,0:T(8,128)(2,1)} %constant.25.clone.tables_any, f32[576,768]{1,0:T(8,128)} %get-tuple-element.19.first_any, ...), custom_call_target="tpu_custom_call" | custom-call | flops 3397386240 | bytes 11543620 | tf_op jit(solution)/shard_map/pallas_call | solution.py:334
Async XLA Ops:
  6.5 87.1 %copy-start.6 = (f32[16]{0:T(128)S(1)}, f32[16]{0:T(128)}, u32[]{:S(2)}) copy-start(f32[16]{0:T(128)} %noise_ref.3) | copy-start | bytes 196
  6.5 87.1 %copy-start.4 = (f32[3,768]{1,0:T(4,128)S(1)}, f32[3,768]{1,0:T(4,128)}, u32[]{:S(2)}) copy-start(f32[3,768]{1,0:T(4,128)} %gains_ref.5) | copy-start | bytes 27652
  6.5 72.3 %copy-start.10 = (bf16[96,768]{1,0:T(8,128)(2,1)S(1)}, bf16[96,768]{1,0:T(8,128)(2,1)}, u32[]{:S(2)}) copy-start(bf16[96,768]{1,0:T(8,128)(2,1)} %param.19) | copy-start | bytes 442372
  6.5 72.3 %copy-start.9 = (bf16[96,768]{1,0:T(8,128)(2,1)S(1)}, bf16[96,768]{1,0:T(8,128)(2,1)}, u32[]{:S(2)}) copy-start(bf16[96,768]{1,0:T(8,128)(2,1)} %param.20) | copy-start | bytes 442372
  6.5 87.1 %copy-start.2 = (bf16[384,768]{1,0:T(8,128)(2,1)S(1)}, bf16[384,768]{1,0:T(8,128)(2,1)}, u32[]{:S(2)}) copy-start(bf16[384,768]{1,0:T(8,128)(2,1)} %w_any.1) | copy-start | bytes 1769476
  31.5 33.0 %all-to-all-start = ((bf16[16,9,8,384]{3,2,1,0:T(8,128)(2,1)}), bf16[16,9,8,384]{3,2,1,0:T(8,128)(2,1)S(1)}, u32[]{:S(2)}, u32[]{:S(2)}) async-start(bf16[16,9,8,384]{3,2,1,0:T(8,128)(2,1)} %shard_map.118), calls=%async_computation | async-start | bytes 1769472 | tf_op jit(solution)/shard_map/all_to_all | solution.py:353
  42.0 29.6 %collective-permute-start = (bf16[576,768]{1,0:T(8,128)(2,1)}, bf16[576,768]{1,0:T(8,128)(2,1)S(1)}, u32[]{:S(2)}, u32[]{:S(2)}) collective-permute-start(bf16[576,768]{1,0:T(8,128)(2,1)} %bitcast.28), channel_id=1, source_target_pairs={{0,480},{32,0},{64,32},{96,64},{128,96},{160,128},{192,160},{224,1... | collective-permute-start | bytes 2654216 | tf_op jit(solution)/shard_map/ppermute | solution.py:376
  64.5 0.7 copy-start.3
  65.2 0.7 copy-start.5
  71.5 26.6 %copy-start = (bf16[576,768]{1,0:T(8,128)(2,1)}, bf16[576,768]{1,0:T(8,128)(2,1)S(1)}, u32[]{:S(2)}) copy-start(bf16[576,768]{1,0:T(8,128)(2,1)S(1)} %collective-permute-done.window_any) | copy-start | bytes 2654212
  71.5 22.1 %all-to-all-start.1 = ((bf16[16,112,128]{2,1,0:T(8,128)(2,1)}), bf16[16,112,128]{2,1,0:T(8,128)(2,1)S(1)}, u32[]{:S(2)}, u32[]{:S(2)}) async-start(bf16[16,112,128]{2,1,0:T(8,128)(2,1)} %shard_map.119), calls=%async_computation.1 | async-start | bytes 917504 | tf_op jit(solution)/shard_map/all_to_all | solution.py:353
  78.8 89.8 %all-gather.3.cloned.1.call-start = ((), (), s32[]{:S(2)}) async-start(), calls=%async_computation.4 | async-start | bytes 5013504 | tf_op jit(solution)/shard_map/all_gather | solution.py:399
  98.1 37.0 %copy-start.7 = (bf16[96,768]{1,0:T(8,128)(2,1)S(1)}, bf16[96,768]{1,0:T(8,128)(2,1)}, u32[]{:S(2)}) copy-start(bf16[96,768]{1,0:T(8,128)(2,1)} %filter_ref.1) | copy-start | bytes 442372
  98.1 37.0 %all-to-all-start.2 = ((bf16[32,112,128]{2,1,0:T(8,128)(2,1)}), bf16[32,112,128]{2,1,0:T(8,128)(2,1)S(1)}, u32[]{:S(2)}, u32[]{:S(2)}) async-start(bf16[32,112,128]{2,1,0:T(8,128)(2,1)} %get-tuple-element.17), calls=%async_computation.2 | async-start | bytes 1835008 | tf_op jit(solution)/shard_map/all_to_all | solution.py:353
  110.7 57.9 %copy-start.8 = (f32[16]{0:T(128)S(1)}, f32[16]{0:T(128)}, u32[]{:S(2)}) copy-start(f32[16]{0:T(128)} %keep_ref.1) | copy-start | bytes 196
  168.6 1.2 copy-start.1
Sparse Core Ops, SparseCore 0:
  93.8 44.2 all-gather.2

commit v2 on v1

--- a/solution.py
+++ b/solution.py
@@ -12,8 +12,10 @@
 POINTS, WIDTH, ATTN, FF = ROWS * NLON, 768, 384, 1536
 ORDERS = LMAX // LATS
 EPS = 1e-05
+SHARDS = 9
+BLOCKS = tuple((b, slice(ATTN * b, ATTN * (b + 1))) for b in range(3))
 MIB = 1 << 20
-LIMITS = (60, 51, 52, 45, 51)
+LIMITS = (60, 51, 52, 16, 49)
 
 
 def chunk_row(r):
@@ -103,41 +105,39 @@
     return copy
 
 
-def frame_scale(level):
-    return lax.rsqrt(1.0 + level * level)
-
-
 def row_scale(values):
     return lax.rsqrt(jnp.sum(values * values, axis=-1, keepdims=True) * (1.0 / WIDTH) + EPS)
 
 
-def pack_window(window_any, out_any, last_ref, packed_ref, sems):
-    last = fetch(window_any.at[16:18], last_ref, sems.at[0])
-    copies = [
-        fetch(
-            window_any.at[0:16, :, :, ATTN * h : ATTN * h + ATTN],
-            out_any.at[:, 4 * h : 4 * h + 4],
-            sems.at[1 + h],
-        )
-        for h in range(2)
-    ]
-    last.wait()
+def pack_window(noise_ref, keep_ref, gains_ref, window_ref, out_ref, params_ref):
+    for f in range(FRAMES):
+        level = jnp.full((8, 128), noise_ref[f], F32)
+        params_ref[f] = lax.rsqrt(1.0 + level * level)
+        params_ref[FRAMES + f] = jnp.full((8, 128), 0.0 if f == 0 else keep_ref[f], F32)
+    for norm in range(3):
+        for c in range(6):
+            params_ref[2 * FRAMES + norm, c : c + 1, :] = gains_ref[
+                norm : norm + 1, 128 * c : 128 * c + 128
+            ]
+    for h in range(2):
+        out_ref[:, 4 * h : 4 * h + 4] = window_ref[0:16, :, :, ATTN * h : ATTN * h + ATTN]
     for c in range(3):
-        left = last_ref[:, :, :, 128 * c : 128 * c + 128].astype(F32).reshape(8, 8, 128)
-        right = last_ref[:, :, :, ATTN + 128 * c : ATTN + 128 * c + 128].astype(F32)
+        left = window_ref[16:18, :, :, 128 * c : 128 * c + 128].astype(F32).reshape(8, 8, 128)
+        right = window_ref[16:18, :, :, ATTN + 128 * c : ATTN + 128 * c + 128].astype(F32)
         even, odd = swap4(left, right.reshape(8, 8, 128))
         for i in range(8):
-            packed_ref[2 * i, :, 128 * c : 128 * c + 128] = even[i].astype(BF16)
-            packed_ref[2 * i + 1, :, 128 * c : 128 * c + 128] = odd[i].astype(BF16)
-    copies.append(fetch(packed_ref, out_any.at[:, 8], sems.at[3]))
-    for copy in copies:
-        copy.wait()
-
-
-def attend(noise_ref, gains_ref, in_ref, w_ref, out_ref, x_ref, proj_ref):
-    level = jnp.concatenate([jnp.full((1, 8, 128), noise_ref[f], F32) for f in range(FRAMES)], 0)
-    scale = frame_scale(level)
-    gain = [gains_ref[0:1, 128 * c : 128 * c + 128].reshape(1, 1, 128) for c in range(6)]
+            out_ref[2 * i, 8, :, 128 * c : 128 * c + 128] = even[i].astype(BF16)
+            out_ref[2 * i + 1, 8, :, 128 * c : 128 * c + 128] = odd[i].astype(BF16)
+
+
+def gain_row(params_ref, norm):
+    return jnp.concatenate([params_ref[2 * FRAMES + norm, c : c + 1, :] for c in range(6)], 1)
+
+
+def attend(params_ref, in_ref, w_any, out_ref, x_ref, proj_ref, w_ref, sems):
+    w_copies = [fetch(w_any.at[:, cols], w_ref.at[:, cols], sems.at[b]) for b, cols in BLOCKS]
+    scale = params_ref[0:FRAMES]
+    gain = [params_ref[2 * FRAMES, c : c + 1, :].reshape(1, 1, 128) for c in range(6)]
     for s in range(4):
         parts = [
             in_ref[:, 4 * (c // 3) + s, :, 128 * (c % 3) : 128 * (c % 3) + 128].astype(F32) * scale
@@ -159,9 +159,10 @@
         left, right = swap4(*pairs(both))
         x_ref[512:576, 128 * c : 128 * c + 128] = left.reshape(64, 128).astype(BF16)
         x_ref[512:576, ATTN + 128 * c : ATTN + 128 * c + 128] = right.reshape(64, 128).astype(BF16)
-    for b in range(3):
-        proj_ref[:, ATTN * b : ATTN * (b + 1)] = jnp.dot(
-            x_ref[...], w_ref[:, ATTN * b : ATTN * (b + 1)], preferred_element_type=F32
+    for b, cols in BLOCKS:
+        w_copies[b].wait()
+        proj_ref[:, cols] = jnp.dot(
+            x_ref[...], w_ref[:, cols], preferred_element_type=F32
         ).astype(BF16)
 
     def mix(base, n):
@@ -234,8 +235,8 @@
 
 
 def to_spectra(
-    frame_ref, noise_ref, gains_ref, mixed_ref, window_any, w_any, tables_any,
-    first_any, out_ref, mixed_rows, base_rows, first_ref, window_ref, w_ref, table_ref, sems,
+    frame_ref, params_ref, mixed_ref, window_any, w_any, tables_any,
+    carry_any, out_ref, mixed_rows, base_rows, split_ref, window_ref, w_ref, table_ref, sems,
 ):
     w_copy = fetch(w_any, w_ref, sems.at[0])
     window_copy = fetch(window_any, window_ref, sems.at[1])
@@ -251,20 +252,26 @@
     last, _ = swap4(*pairs(mixed_ref[:, 104:112, :].astype(F32)))
     for h, tile in enumerate((left, right, last)):
         mixed_rows[512:576, 128 * h : 128 * h + 128] = tile.reshape(64, 128).astype(BF16)
-    scale = frame_scale(jnp.full((1, 1), noise_ref[frame_ref[0]], F32))
-    gain = gains_ref[1:2, :]
+    scale = params_ref[frame_ref[0], 0:1, 0:1]
+    gain = gain_row(params_ref, 1)
     w_copy.wait()
     window_copy.wait()
     first = window_ref[...].astype(F32) * scale + jnp.dot(
         mixed_rows[...], w_ref[...], preferred_element_type=F32
     )
-    first_ref[...] = first
-    first_copy = fetch(first_ref, first_any, sems.at[3])
+    high = first.astype(BF16)
+    split_ref[0] = high
+    split_ref[1] = (first - high.astype(F32)).astype(BF16)
+    carries = [
+        fetch(split_ref, carry_any.at[0:2], sems.at[3]),
+        fetch(window_ref, carry_any.at[2], sems.at[4]),
+    ]
     base_rows[0:POINTS, :] = (first * row_scale(first) * gain).astype(BF16)
     base_rows[POINTS:640, :] = jnp.zeros((640 - POINTS, WIDTH), BF16)
     table_copy.wait()
     put_chunks(jnp.dot(table_ref[...], base_rows[...], preferred_element_type=F32), out_ref)
-    first_copy.wait()
+    for copy in carries:
+        copy.wait()
 
 
 def filter_orders(in_ref, down_ref, up_ref, filter_ref, out_ref, rows_ref, coeffs_ref):
@@ -282,44 +289,51 @@
 
 
 def feed_forward(
-    frame_ref, keep_ref, gains_ref, in_ref, tables_any, first_any, window_any, weights_any,
-    out_any, rows_ref, inner_ref, hidden_ref, out_ref, table_ref, first_ref, window_ref,
-    w_in_ref, w_down_ref, sems,
+    frame_ref, params_ref, in_any, tables_any, carry_any, *refs
 ):
+    shards, refs = refs[:SHARDS], refs[SHARDS:]
+    (
+        out_any, rows_ref, inner_ref, hidden_ref, out_ref, table_ref, carry_ref, second_ref,
+        w_ref, in_ref, sems, w_sems,
+    ) = refs
+    in_copy = fetch(in_any, in_ref, sems.at[2])
     table_copy = fetch(tables_any.at[1, 0:POINTS], table_ref, sems.at[0])
-    first_copy = fetch(first_any, first_ref, sems.at[1])
+    first_copy = fetch(carry_any.at[0:2], carry_ref.at[0:2], sems.at[1])
+    in_copy.wait()
     get_chunks(in_ref, rows_ref)
-    in_copy = fetch(weights_any.at[:, 0:96, :], w_in_ref, sems.at[2])
-    gain = gains_ref[2:3, :]
+    w_copies, at = [], 0
+    for i, shard in enumerate(shards):
+        w_copies.append(fetch(shard, w_ref.at[at : at + shard.shape[0]], w_sems.at[i]))
+        at += shard.shape[0]
+    gain = gain_row(params_ref, 2)
     table_copy.wait()
+    second_ref[...] = jnp.dot(table_ref[...], rows_ref[...], preferred_element_type=F32)
     first_copy.wait()
-    down_copy = fetch(weights_any.at[:, 96:192, :], w_down_ref, sems.at[3])
-    window_copy = fetch(window_any, window_ref, sems.at[4])
-    second = first_ref[...] + jnp.dot(table_ref[...], rows_ref[...], preferred_element_type=F32)
-    first_ref[...] = second
+    window_copy = fetch(carry_any.at[2], carry_ref.at[2], sems.at[4])
+    second = carry_ref[0].astype(F32) + carry_ref[1].astype(F32) + second_ref[...]
+    second_ref[...] = second
     inner_ref[...] = (second * row_scale(second) * gain).astype(BF16)
-    in_copy.wait()
     for b in range(2):
         units = slice(8 * b, 8 * b + 8)
+        for copy in w_copies[4 * b : 4 * b + 4] if b == 0 else w_copies[4:]:
+            copy.wait()
         raised = lax.dot_general(
             inner_ref[...],
-            w_in_ref[units].reshape(FF // 2, WIDTH),
+            w_ref[units, 0:96, :].reshape(FF // 2, WIDTH),
             (((1,), (1,)), ((), ())),
             preferred_element_type=F32,
         )
         hidden_ref[:, FF // 2 * b : FF // 2 * (b + 1)] = gelu(raised).astype(BF16)
-    frame = frame_ref[0]
-    ratio = jnp.where(frame == 0, 0.0, keep_ref[frame])
-    down_copy.wait()
+    ratio = params_ref[FRAMES + frame_ref[0], 0:1, 0:1]
     window_copy.wait()
-    w_down = w_down_ref[...].reshape(FF, WIDTH)
+    w_down = w_ref[:, 96:192, :].reshape(FF, WIDTH)
     copies = []
     for j in range(2):
         rows = slice(POINTS // 2 * j, POINTS // 2 * (j + 1))
-        denoised = first_ref[rows, :] + jnp.dot(
+        denoised = second_ref[rows, :] + jnp.dot(
             hidden_ref[rows, :], w_down, preferred_element_type=F32
         )
-        state = window_ref[rows, :].astype(F32)
+        state = carry_ref[2, rows, :].astype(F32)
         out_ref[rows, :] = (denoised + ratio * (state - denoised)).astype(BF16)
         copies.append(fetch(out_ref.at[rows], out_any.at[rows], sems.at[5 + j]))
     for copy in copies:
@@ -353,6 +367,20 @@
     return lax.all_to_all(chunks, axis, split_axis=0, concat_axis=0, tiled=True)
 
 
+def shift(value, steps):
+    hops = [(source, (source + steps) % FRAMES) for source in range(FRAMES)]
+    return lax.ppermute(value, "lead", hops)
+
+
+def swap_cores(value):
+    return lax.ppermute(value, "lead", [(source, source ^ 1) for source in range(FRAMES)])
+
+
+def round_chips(value, chips):
+    hops = [(s, (s + (2 * chips if s % 2 == 0 else -2 * chips)) % FRAMES) for s in range(FRAMES)]
+    return lax.ppermute(value, "lead", hops)
+
+
 def per_device(
     window, noise_level, keep_ratio, norm_gains, w_qkv, w_out, spectral_filter, w_in, w_down
 ):
@@ -364,19 +392,22 @@
     shape = jax.ShapeDtypeStruct
 
     state = window.reshape(POINTS, WIDTH)
-    (packed,) = call(
+    packed, params = call(
         pack_window,
-        [shape((FRAMES, 9, 8, ATTN), BF16)],
-        "hh",
-        [((2, 4, 8, WIDTH), BF16), ((FRAMES, 8, ATTN), BF16), 4],
-        [window.reshape(18, 4, 8, WIDTH)],
+        [shape((FRAMES, 9, 8, ATTN), BF16), shape((2 * FRAMES + 3, 8, 128), F32)],
+        "ssvvvv",
+        [],
+        [noise_level, keep_ratio, norm_gains, window.reshape(18, 4, 8, WIDTH)],
         0,
         LIMITS[0],
     )
-    ahead = lax.ppermute(
-        state, "lead", [(source, (source - 1) % FRAMES) for source in range(FRAMES)]
-    )
-    packed, legendre = lax.optimization_barrier((packed, legendre))
+    ahead = shift(state, -1)
+    packed, legendre, w_in, w_down = lax.optimization_barrier((packed, legendre, w_in, w_down))
+    own = jnp.concatenate([w_in, w_down], 0)[None]
+    other = swap_cores(own)
+    pair = jnp.where(
+        lead % 2 == 0, jnp.concatenate([own, other], 0), jnp.concatenate([other, own], 0)
+    )
     local = lax.dynamic_slice_in_dim(legendre, ORDERS * lat, ORDERS, 1)
     down = jnp.einsum("ilj,icjn->icln", local[0], placement, preferred_element_type=F32)
     down = down.astype(BF16).reshape(2 * ORDERS * LMAX, 768)
@@ -386,60 +417,68 @@
     (mixed,) = call(
         attend,
         [shape((FRAMES, 112, 128), BF16)],
-        "svvvv",
-        [((POINTS, WIDTH), BF16), ((POINTS, 3 * ATTN), BF16)],
-        [noise_level, norm_gains, exchange(packed, "lead"), w_qkv],
+        "vvhv",
+        [((POINTS, WIDTH), BF16), ((POINTS, 3 * ATTN), BF16), ((WIDTH, 3 * ATTN), BF16), 3],
+        [params, exchange(packed, "lead"), w_qkv],
         2 * POINTS * WIDTH * 3 * ATTN,
         LIMITS[1],
     )
-    mixed, ahead = lax.optimization_barrier((mixed, ahead))
+    mixed, ahead, pair = lax.optimization_barrier((mixed, ahead, pair))
     mixed = exchange(mixed, "lead")
-    weights = jnp.concatenate([w_in, w_down], 0)
-    mixed, weights = lax.optimization_barrier((mixed, weights))
-    weights = lax.all_gather(weights, "lead", axis=0, tiled=False)
-    first, spectra = call(
+    carry, spectra = call(
         to_spectra,
-        [shape((POINTS, WIDTH), F32), shape((LATS, 112, 128), BF16)],
-        "ssvvhhhhv",
+        [shape((3, POINTS, WIDTH), BF16), shape((LATS, 112, 128), BF16)],
+        "svvhhhhv",
         [
             ((POINTS, ATTN), BF16),
             ((640, WIDTH), BF16),
-            ((POINTS, WIDTH), F32),
+            ((2, POINTS, WIDTH), BF16),
             ((POINTS, WIDTH), BF16),
             ((ATTN, WIDTH), BF16),
             ((768, 640), BF16),
-            4,
+            5,
         ],
-        [frame, noise_level, norm_gains, mixed, ahead, w_out, tables],
+        [frame, params, mixed, ahead, w_out, tables],
         2 * POINTS * WIDTH * (ATTN + 768),
         LIMITS[2],
     )
+    spectra, pair = lax.optimization_barrier((spectra, pair))
+    first_pair, second_pair = round_chips(pair, 1), round_chips(pair, 2)
+    swapped = swap_cores(first_pair)
+    by_order = exchange(spectra, "lat")
+    by_order, second_pair, swapped = lax.optimization_barrier((by_order, second_pair, swapped))
+    shards = [pair, first_pair, swapped, second_pair]
     (back,) = call(
         filter_orders,
         [shape((LATS, 112, 128), BF16)],
         "vvvvv",
         [((768, WIDTH), BF16), ((2 * ORDERS * LMAX, WIDTH), BF16)],
-        [exchange(spectra, "lat"), down, up, spectral_filter],
+        [by_order, down, up, spectral_filter],
         4 * POINTS * WIDTH * 768,
         LIMITS[3],
     )
+    back, second_pair = lax.optimization_barrier((back, second_pair))
+    third_pair = round_chips(second_pair, 1)
+    last = round_chips(jnp.where(lead % 2 == 0, second_pair[0:1], second_pair[1:2]), 2)
+    shards += [third_pair, swap_cores(second_pair), swap_cores(third_pair), last, swap_cores(last)]
     (stepped,) = call(
         feed_forward,
         [shape((POINTS, WIDTH), BF16)],
-        "ssvvhhhhh",
+        "svhhh" + "h" * SHARDS + "h",
         [
             ((768, WIDTH), BF16),
             ((POINTS, WIDTH), BF16),
             ((POINTS, FF), BF16),
             ((POINTS, WIDTH), BF16),
             ((POINTS, 768), BF16),
+            ((3, POINTS, WIDTH), BF16),
             ((POINTS, WIDTH), F32),
-            ((POINTS, WIDTH), BF16),
-            ((FRAMES, 96, WIDTH), BF16),
-            ((FRAMES, 96, WIDTH), BF16),
+            ((FRAMES, 192, WIDTH), BF16),
+            ((LATS, 112, 128), BF16),
             7,
+            SHARDS,
         ],
-        [frame, keep_ratio, norm_gains, exchange(back, "lat"), tables, first, ahead, weights],
+        [frame, params, exchange(back, "lat"), tables, carry, *shards],
         2 * POINTS * WIDTH * (2 * FF + 768),
         LIMITS[4],
     )

time: 185 us -> 152 us (0.82)
  the two profiles are of different devices: /device:TPU:8 before, /device:TPU:1 now
where the time goes in v2:
time: 152 us; the launch traced here: 151 us
  starting transfers between devices  63.7 us (42%)
  waiting for transfers between devices  54.7 us (36%)
  Pallas kernels  22.9 us (15%)
  other arithmetic  3.25 us (2%)
  matrix products  3.2 us (2%)
  local copies, waits for them, and re-layouts  2.46 us (2%)
    all_to_all x4, waiting for transfers between devices, exchange(): return lax.all_to_all(chunks, axis, split_axis=0, concat_axis=0, tiled=True)  35.2 us
    all_to_all x4, starting transfers between devices, exchange(): return lax.all_to_all(chunks, axis, split_axis=0, concat_axis=0, tiled=True)  33.7 us
    pallas_call x5, Pallas kernels, call(): pl.pallas_call(kernel, out_shape=outs, in_specs=specs[:len(args)], out_sp...  22.9 us
    ppermute x5, starting transfers between devices, swap_cores(): lax.ppermute(value, 'lead', [(source, source ^ 1) for source in range(FRA...  17.7 us
    ppermute x4, waiting for transfers between devices, round_chips(): return lax.ppermute(value, 'lead', hops)  16.6 us
    ppermute x4, starting transfers between devices, round_chips(): return lax.ppermute(value, 'lead', hops)  12.2 us
  transfers between devices with their start and end apart: 14, of which 10 were waited for; matrix products, arithmetic and copies ran while one was open for 5% of the time, Pallas kernels for 3%

profile of v2, /device:TPU:1, one launch (start us, length us, event | category | flops | bytes accessed | tf_op | source)
XLA Modules:
  0.0 150.6 jit_solution(6295557356295969658)
XLA Ops:
  0.0 0.0 copy-start
  0.0 2.3 %shard_map.118 = (bf16[16,9,8,384]{3,2,1,0:T(8,128)(2,1)}, f32[35,8,128]{2,1,0:T(8,128)}) custom-call(f32[16]{0:T(128)} %noise_ref.1, f32[16]{0:T(128)} %keep_ref.1, f32[3,768]{1,0:T(4,128)} %gains_ref.1, bf16[18,4,8,768]{3,2,1,0:T(8,128)(2,1)} %bitcast.28), custom_call_target="tpu_custom_call" | custom-call | bytes 1922176 | tf_op jit(solution)/shard_map/pallas_call | solution.py:348
  2.3 0.0 copy-start.2
  2.3 12.0 %all-to-all-start = ((bf16[16,9,8,384]{3,2,1,0:T(8,128)(2,1)}), bf16[16,9,8,384]{3,2,1,0:T(8,128)(2,1)S(1)}, u32[]{:S(2)}, u32[]{:S(2)}) async-start(bf16[16,9,8,384]{3,2,1,0:T(8,128)(2,1)} %get-tuple-element.25), calls=%async_computation | async-start | bytes 1769472 | tf_op jit(solution)/shard_map/all_to_all | solution.py:367
  14.2 0.1 collective-permute-start
  14.4 1.0 maximum_bitcast_fusion
  15.4 4.8 %collective-permute-start.1 = (bf16[1,192,768]{2,1,0:T(8,128)(2,1)S(1)}, bf16[1,192,768]{2,1,0:T(8,128)(2,1)}, u32[]{:S(2)}, u32[]{:S(2)}) collective-permute-start(bf16[1,192,768]{2,1,0:T(8,128)(2,1)S(1)} %maximum_bitcast_fusion), channel_id=1, source_target_pairs={{0,32},{32,0},{64,96},{96,64},{128,160},{160,128},{192,224},{224,1... | collective-permute-start | bytes 884744 | tf_op jit(solution)/shard_map/ppermute | solution.py:376
  20.2 1.3 collective-permute-done.1
  21.5 1.2 maximum_select_fusion.refs_0_
  22.6 16.2 %all-to-all-done.in_ref = bf16[16,9,8,384]{3,2,1,0:T(8,128)(2,1)S(1)} async-done(((bf16[16,9,8,384]{3,2,1,0:T(8,128)(2,1)}), bf16[16,9,8,384]{3,2,1,0:T(8,128)(2,1)S(1)}, u32[]{:S(2)}, u32[]{:S(2)}) %all-to-all-start) | async-done | bytes 884768 | tf_op jit(solution)/shard_map/all_to_all | solution.py:367
  38.9 0.0 copy-start.1
  38.9 0.9 copy-done.1
  39.8 4.8 %shard_map.119 = bf16[16,112,128]{2,1,0:T(8,128)(2,1)} custom-call(f32[35,8,128]{2,1,0:T(8,128)S(1)} %copy-done.1, bf16[16,9,8,384]{3,2,1,0:T(8,128)(2,1)S(1)} %all-to-all-done.in_ref, bf16[768,1152]{1,0:T(8,128)(2,1)} %w_any.2), custom_call_target="tpu_custom_call" | custom-call | flops 1019215872 | bytes 3256320 | tf_op jit(solution)/shard_map/pallas_call | solution.py:348
  44.6 0.7 collective-permute-done.window_any
  45.3 0.0 copy-start.4
  45.3 5.8 %all-to-all-start.1 = ((bf16[16,112,128]{2,1,0:T(8,128)(2,1)}), bf16[16,112,128]{2,1,0:T(8,128)(2,1)S(1)}, u32[]{:S(2)}, u32[]{:S(2)}) async-start(bf16[16,112,128]{2,1,0:T(8,128)(2,1)} %shard_map.119), calls=%async_computation.1 | async-start | bytes 917504 | tf_op jit(solution)/shard_map/all_to_all | solution.py:367
  51.1 16.0 %all-to-all-done.1.mixed_ref = bf16[16,112,128]{2,1,0:T(8,128)(2,1)S(1)} async-done(((bf16[16,112,128]{2,1,0:T(8,128)(2,1)}), bf16[16,112,128]{2,1,0:T(8,128)(2,1)S(1)}, u32[]{:S(2)}, u32[]{:S(2)}) %all-to-all-start.1) | async-done | bytes 458784 | tf_op jit(solution)/shard_map/all_to_all | solution.py:367
  67.1 0.0 copy-done.4
  67.1 0.0 copy-done
  67.1 0.0 copy-done.2
  67.1 4.8 %shard_map.120 = (bf16[3,576,768]{2,1,0:T(8,128)(2,1)}, bf16[32,112,128]{2,1,0:T(8,128)(2,1)}) custom-call(s32[1]{0:T(128)} %bitcast.frame_ref, f32[35,8,128]{2,1,0:T(8,128)S(1)} %copy-done.2, bf16[16,112,128]{2,1,0:T(8,128)(2,1)S(1)} %all-to-all-done.1.mixed_ref, bf16[576,768]{1,0:T(8,128)(2,1)} %copy-done.4, bf16[384,768]{1,0:T(8,128)(2,1)S(1)} %copy-done, ...), custom_call_target="tpu_custom_call" | custom-call | flops 1019215872 | bytes 8007684 | tf_op jit(solution)/shard_map/pallas_call | solution.py:348
  71.9 9.7 %all-to-all-start.2 = ((bf16[32,112,128]{2,1,0:T(8,128)(2,1)}), bf16[32,112,128]{2,1,0:T(8,128)(2,1)S(1)}, u32[]{:S(2)}, u32[]{:S(2)}) async-start(bf16[32,112,128]{2,1,0:T(8,128)(2,1)} %get-tuple-element.32), calls=%async_computation.2 | async-start | bytes 1835008 | tf_op jit(solution)/shard_map/all_to_all | solution.py:367
  81.6 1.9 %collective-permute-start.3 = (bf16[2,192,768]{2,1,0:T(8,128)(2,1)S(1)}, bf16[2,192,768]{2,1,0:T(8,128)(2,1)}, u32[]{:S(2)}, u32[]{:S(2)}) collective-permute-start(bf16[2,192,768]{2,1,0:T(8,128)(2,1)S(1)} %maximum_select_fusion.refs_0_), channel_id=1, source_target_pairs={{0,64},{32,480},{64,128},{96,32},{128,192},{160,96},{192,256},{224... | collective-permute-start | bytes 1769480 | tf_op jit(solution)/shard_map/ppermute | solution.py:381
  83.5 2.4 %collective-permute-start.2 = (bf16[2,192,768]{2,1,0:T(8,128)(2,1)S(1)}, bf16[2,192,768]{2,1,0:T(8,128)(2,1)}, u32[]{:S(2)}, u32[]{:S(2)}) collective-permute-start(bf16[2,192,768]{2,1,0:T(8,128)(2,1)S(1)} %maximum_select_fusion.refs_0_), channel_id=1, source_target_pairs={{0,128},{32,416},{64,192},{96,480},{128,256},{160,32},{192,320},{2... | collective-permute-start | bytes 1769480 | tf_op jit(solution)/shard_map/ppermute | solution.py:381
  85.9 7.9 %collective-permute-done.3.refs_1_ = bf16[2,192,768]{2,1,0:T(8,128)(2,1)} collective-permute-done((bf16[2,192,768]{2,1,0:T(8,128)(2,1)S(1)}, bf16[2,192,768]{2,1,0:T(8,128)(2,1)}, u32[]{:S(2)}, u32[]{:S(2)}) %collective-permute-start.3) | collective-permute-done | bytes 589856 | tf_op jit(solution)/shard_map/ppermute | solution.py:381
  93.8 4.7 %collective-permute-start.4 = (bf16[2,192,768]{2,1,0:T(8,128)(2,1)}, bf16[2,192,768]{2,1,0:T(8,128)(2,1)}, u32[]{:S(2)}, u32[]{:S(2)}) collective-permute-start(bf16[2,192,768]{2,1,0:T(8,128)(2,1)} %collective-permute-done.3.refs_1_), channel_id=1, source_target_pairs={{0,32},{32,0},{64,96},{96,64},{128,160},{160,128},{192,224},{224,1... | collective-permute-start | bytes 1769480 | tf_op jit(solution)/shard_map/ppermute | solution.py:376
  98.6 1.6 %convolution_convert_fusion = bf16[3,96,2,768]{3,1,2,0:T(8,128)(2,1)S(1)} fusion(bf16[3,2,96,768]{3,2,1,0:T(8,128)(2,1)} %constant.40.clone, bf16[2,96,96,96]{3,2,1,0:T(8,128)(2,1)} %constant.39.clone, s32[]{:T(128)S(6)} %add.14, s32[]{:T(128)S(6)} %select_n.31), kind=kOutput, calls=%fused_computation | convolution fusion | flops 85377024 | bytes 1843208 | tf_op jit(solution)/shard_map/ilj,icjn->nicl/dot_general | solution.py:414
  100.2 0.6 copy.14.up_ref
  100.8 1.6 %convolution_convert_fusion.1 = bf16[3,96,2,768]{3,1,2,0:T(8,128)(2,1)S(1)} fusion(bf16[3,2,96,768]{3,2,1,0:T(8,128)(2,1)} %constant.40.clone, bf16[2,96,96,96]{3,2,1,0:T(8,128)(2,1)} %constant.39.clone, s32[]{:T(128)S(6)} %select_n.31), kind=kOutput, calls=%fused_computation.1 | convolution fusion | flops 85377024 | bytes 1843204 | tf_op jit(solution)/shard_map/ilj,icjn->icln/dot_general | solution.py:412
  102.4 1.3 collective-permute-done.2.refs_3_
  103.8 0.0 collective-permute-done.4.refs_2_
  103.8 3.0 %all-to-all-done.2.in_ref = bf16[32,112,128]{2,1,0:T(8,128)(2,1)S(1)} async-done(((bf16[32,112,128]{2,1,0:T(8,128)(2,1)}), bf16[32,112,128]{2,1,0:T(8,128)(2,1)S(1)}, u32[]{:S(2)}, u32[]{:S(2)}) %all-to-all-start.2) | async-done | bytes 917536 | tf_op jit(solution)/shard_map/all_to_all | solution.py:367
  106.7 0.9 copy-done.3
  107.7 3.0 %shard_map.121 = bf16[32,112,128]{2,1,0:T(8,128)(2,1)} custom-call(bf16[32,112,128]{2,1,0:T(8,128)(2,1)S(1)} %all-to-all-done.2.in_ref, bf16[576,768]{1,0:T(8,128)(2,1)S(1)} %bitcast.26, bf16[768,576]{1,0:T(8,128)(2,1)S(1)} %copy.14.up_ref, bf16[96,768]{1,0:T(8,128)(2,1)S(1)} %copy-done.3), custom_call_target="tpu_custom_call" | custom-call | flops 1358954496 | bytes 3751936 | tf_op jit(solution)/shard_map/pallas_call | solution.py:348
  110.6 6.2 %all-to-all-start.3 = ((bf16[32,112,128]{2,1,0:T(8,128)(2,1)}), bf16[32,112,128]{2,1,0:T(8,128)(2,1)}, u32[]{:S(2)}, u32[]{:S(2)}) async-start(bf16[32,112,128]{2,1,0:T(8,128)(2,1)} %shard_map.121), calls=%async_computation.3 | async-start | bytes 1835008 | tf_op jit(solution)/shard_map/all_to_all | solution.py:367
  116.8 5.7 %collective-permute-start.5 = (bf16[2,192,768]{2,1,0:T(8,128)(2,1)}, bf16[2,192,768]{2,1,0:T(8,128)(2,1)S(1)}, u32[]{:S(2)}, u32[]{:S(2)}) collective-permute-start(bf16[2,192,768]{2,1,0:T(8,128)(2,1)} %collective-permute-done.2.refs_3_), channel_id=1, source_target_pairs={{0,64},{32,480},{64,128},{96,32},{128,192},{160,96},{192,256},{224... | collective-permute-start | bytes 1769480 | tf_op jit(solution)/shard_map/ppermute | solution.py:381
  122.5 3.0 %collective-permute-start.6 = (bf16[2,192,768]{2,1,0:T(8,128)(2,1)}, bf16[2,192,768]{2,1,0:T(8,128)(2,1)S(1)}, u32[]{:S(2)}, u32[]{:S(2)}) collective-permute-start(bf16[2,192,768]{2,1,0:T(8,128)(2,1)} %collective-permute-done.2.refs_3_), channel_id=1, source_target_pairs={{0,32},{32,0},{64,96},{96,64},{128,160},{160,128},{192,224},{224,1... | collective-permute-start | bytes 1769480 | tf_op jit(solution)/shard_map/ppermute | solution.py:376
  125.6 1.1 slice_select_fusion
  126.7 2.1 %collective-permute-start.8 = (bf16[1,192,768]{2,1,0:T(8,128)(2,1)S(1)}, bf16[1,192,768]{2,1,0:T(8,128)(2,1)S(1)}, u32[]{:S(2)}, u32[]{:S(2)}) collective-permute-start(bf16[1,192,768]{2,1,0:T(8,128)(2,1)S(1)} %slice_select_fusion), channel_id=1, source_target_pairs={{0,128},{32,416},{64,192},{96,480},{128,256},{160,32},{192,320},{2... | collective-permute-start | bytes 884744 | tf_op jit(solution)/shard_map/ppermute | solution.py:381
  128.8 4.1 %collective-permute-done.5.refs_4_ = bf16[2,192,768]{2,1,0:T(8,128)(2,1)S(1)} collective-permute-done((bf16[2,192,768]{2,1,0:T(8,128)(2,1)}, bf16[2,192,768]{2,1,0:T(8,128)(2,1)S(1)}, u32[]{:S(2)}, u32[]{:S(2)}) %collective-permute-start.5) | collective-permute-done | bytes 589856 | tf_op jit(solution)/shard_map/ppermute | solution.py:381
  132.9 1.9 %collective-permute-start.7 = (bf16[2,192,768]{2,1,0:T(8,128)(2,1)S(1)}, bf16[2,192,768]{2,1,0:T(8,128)(2,1)S(1)}, u32[]{:S(2)}, u32[]{:S(2)}) collective-permute-start(bf16[2,192,768]{2,1,0:T(8,128)(2,1)S(1)} %collective-permute-done.5.refs_4_), channel_id=1, source_target_pairs={{0,32},{32,0},{64,96},{96,64},{128,160},{160,128},{192,224},{224,1... | collective-permute-start | bytes 1769480 | tf_op jit(solution)/shard_map/ppermute | solution.py:376
  134.8 3.3 %collective-permute-done.8.refs_7_ = bf16[1,192,768]{2,1,0:T(8,128)(2,1)S(1)} collective-permute-done((bf16[1,192,768]{2,1,0:T(8,128)(2,1)S(1)}, bf16[1,192,768]{2,1,0:T(8,128)(2,1)S(1)}, u32[]{:S(2)}, u32[]{:S(2)}) %collective-permute-start.8) | collective-permute-done | bytes 294944 | tf_op jit(solution)/shard_map/ppermute | solution.py:381
  138.0 3.2 %collective-permute-start.9 = (bf16[1,192,768]{2,1,0:T(8,128)(2,1)S(1)}, bf16[1,192,768]{2,1,0:T(8,128)(2,1)S(1)}, u32[]{:S(2)}, u32[]{:S(2)}) collective-permute-start(bf16[1,192,768]{2,1,0:T(8,128)(2,1)S(1)} %collective-permute-done.8.refs_7_), channel_id=1, source_target_pairs={{0,32},{32,0},{64,96},{96,64},{128,160},{160,128},{192,224},{224,1... | collective-permute-start | bytes 884744 | tf_op jit(solution)/shard_map/ppermute | solution.py:376
  141.3 0.0 collective-permute-done.6.refs_5_
  141.3 1.0 collective-permute-done.9.refs_8_
  142.3 0.0 collective-permute-done.7.refs_6_
  142.3 0.0 all-to-all-done.3.in_any
  142.3 8.1 %shard_map.122 = bf16[576,768]{1,0:T(8,128)(2,1)} custom-call(s32[1]{0:T(128)} %bitcast.frame_ref, f32[35,8,128]{2,1,0:T(8,128)S(1)} %copy-done.2, bf16[32,112,128]{2,1,0:T(8,128)(2,1)} %all-to-all-done.3.in_any, bf16[2,768,768]{2,1,0:T(8,128)(2,1)} %constant.38.clone.tables_any, bf16[3,576,768]{2,1,0:T(8,128)(2,1)} %get-tuple-element.38.carry_any, ...), custom_call_target="tpu_custom_call" | custom-call | flops 3397386240 | bytes 11677700 | tf_op jit(solution)/shard_map/pallas_call | solution.py:348
  (1 shorter events, 0.0 us)
Async XLA Ops:
  0.0 67.1 %copy-start = (bf16[384,768]{1,0:T(8,128)(2,1)S(1)}, bf16[384,768]{1,0:T(8,128)(2,1)}, u32[]{:S(2)}) copy-start(bf16[384,768]{1,0:T(8,128)(2,1)} %w_any.3) | copy-start | bytes 1769476
  2.3 64.8 %copy-start.2 = (f32[35,8,128]{2,1,0:T(8,128)S(1)}, f32[35,8,128]{2,1,0:T(8,128)}, u32[]{:S(2)}) copy-start(f32[35,8,128]{2,1,0:T(8,128)} %get-tuple-element.23.params_ref) | copy-start | bytes 430084
  2.3 36.6 %all-to-all-start = ((bf16[16,9,8,384]{3,2,1,0:T(8,128)(2,1)}), bf16[16,9,8,384]{3,2,1,0:T(8,128)(2,1)S(1)}, u32[]{:S(2)}, u32[]{:S(2)}) async-start(bf16[16,9,8,384]{3,2,1,0:T(8,128)(2,1)} %get-tuple-element.25), calls=%async_computation | async-start | bytes 1769472 | tf_op jit(solution)/shard_map/all_to_all | solution.py:367
  14.2 31.0 %collective-permute-start = (bf16[576,768]{1,0:T(8,128)(2,1)}, bf16[576,768]{1,0:T(8,128)(2,1)S(1)}, u32[]{:S(2)}, u32[]{:S(2)}) collective-permute-start(bf16[576,768]{1,0:T(8,128)(2,1)} %bitcast.29), channel_id=1, source_target_pairs={{0,480},{32,0},{64,32},{96,64},{128,96},{160,128},{192,160},{224,1... | collective-permute-start | bytes 2654216 | tf_op jit(solution)/shard_map/ppermute | solution.py:372
  15.4 6.1 %collective-permute-start.1 = (bf16[1,192,768]{2,1,0:T(8,128)(2,1)S(1)}, bf16[1,192,768]{2,1,0:T(8,128)(2,1)}, u32[]{:S(2)}, u32[]{:S(2)}) collective-permute-start(bf16[1,192,768]{2,1,0:T(8,128)(2,1)S(1)} %maximum_bitcast_fusion), channel_id=1, source_target_pairs={{0,32},{32,0},{64,96},{96,64},{128,160},{160,128},{192,224},{224,1... | collective-permute-start | bytes 884744 | tf_op jit(solution)/shard_map/ppermute | solution.py:376
  38.9 0.9 copy-start.1
  45.3 21.8 %copy-start.4 = (bf16[576,768]{1,0:T(8,128)(2,1)}, bf16[576,768]{1,0:T(8,128)(2,1)S(1)}, u32[]{:S(2)}) copy-start(bf16[576,768]{1,0:T(8,128)(2,1)S(1)} %collective-permute-done.window_any) | copy-start | bytes 2654212
  45.3 21.8 %all-to-all-start.1 = ((bf16[16,112,128]{2,1,0:T(8,128)(2,1)}), bf16[16,112,128]{2,1,0:T(8,128)(2,1)S(1)}, u32[]{:S(2)}, u32[]{:S(2)}) async-start(bf16[16,112,128]{2,1,0:T(8,128)(2,1)} %shard_map.119), calls=%async_computation.1 | async-start | bytes 917504 | tf_op jit(solution)/shard_map/all_to_all | solution.py:367
  71.9 34.9 %all-to-all-start.2 = ((bf16[32,112,128]{2,1,0:T(8,128)(2,1)}), bf16[32,112,128]{2,1,0:T(8,128)(2,1)S(1)}, u32[]{:S(2)}, u32[]{:S(2)}) async-start(bf16[32,112,128]{2,1,0:T(8,128)(2,1)} %get-tuple-element.32), calls=%async_computation.2 | async-start | bytes 1835008 | tf_op jit(solution)/shard_map/all_to_all | solution.py:367
  81.6 12.3 %collective-permute-start.3 = (bf16[2,192,768]{2,1,0:T(8,128)(2,1)S(1)}, bf16[2,192,768]{2,1,0:T(8,128)(2,1)}, u32[]{:S(2)}, u32[]{:S(2)}) collective-permute-start(bf16[2,192,768]{2,1,0:T(8,128)(2,1)S(1)} %maximum_select_fusion.refs_0_), channel_id=1, source_target_pairs={{0,64},{32,480},{64,128},{96,32},{128,192},{160,96},{192,256},{224... | collective-permute-start | bytes 1769480 | tf_op jit(solution)/shard_map/ppermute | solution.py:381
  83.5 20.3 %collective-permute-start.2 = (bf16[2,192,768]{2,1,0:T(8,128)(2,1)S(1)}, bf16[2,192,768]{2,1,0:T(8,128)(2,1)}, u32[]{:S(2)}, u32[]{:S(2)}) collective-permute-start(bf16[2,192,768]{2,1,0:T(8,128)(2,1)S(1)} %maximum_select_fusion.refs_0_), channel_id=1, source_target_pairs={{0,128},{32,416},{64,192},{96,480},{128,256},{160,32},{192,320},{2... | collective-permute-start | bytes 1769480 | tf_op jit(solution)/shard_map/ppermute | solution.py:381
  93.8 9.9 %collective-permute-start.4 = (bf16[2,192,768]{2,1,0:T(8,128)(2,1)}, bf16[2,192,768]{2,1,0:T(8,128)(2,1)}, u32[]{:S(2)}, u32[]{:S(2)}) collective-permute-start(bf16[2,192,768]{2,1,0:T(8,128)(2,1)} %collective-permute-done.3.refs_1_), channel_id=1, source_target_pairs={{0,32},{32,0},{64,96},{96,64},{128,160},{160,128},{192,224},{224,1... | collective-permute-start | bytes 1769480 | tf_op jit(solution)/shard_map/ppermute | solution.py:376
  106.7 0.9 copy-start.3
  110.6 31.7 %all-to-all-start.3 = ((bf16[32,112,128]{2,1,0:T(8,128)(2,1)}), bf16[32,112,128]{2,1,0:T(8,128)(2,1)}, u32[]{:S(2)}, u32[]{:S(2)}) async-start(bf16[32,112,128]{2,1,0:T(8,128)(2,1)} %shard_map.121), calls=%async_computation.3 | async-start | bytes 1835008 | tf_op jit(solution)/shard_map/all_to_all | solution.py:367
  116.8 16.0 %collective-permute-start.5 = (bf16[2,192,768]{2,1,0:T(8,128)(2,1)}, bf16[2,192,768]{2,1,0:T(8,128)(2,1)S(1)}, u32[]{:S(2)}, u32[]{:S(2)}) collective-permute-start(bf16[2,192,768]{2,1,0:T(8,128)(2,1)} %collective-permute-done.2.refs_3_), channel_id=1, source_target_pairs={{0,64},{32,480},{64,128},{96,32},{128,192},{160,96},{192,256},{224... | collective-permute-start | bytes 1769480 | tf_op jit(solution)/shard_map/ppermute | solution.py:381
  122.5 18.7 %collective-permute-start.6 = (bf16[2,192,768]{2,1,0:T(8,128)(2,1)}, bf16[2,192,768]{2,1,0:T(8,128)(2,1)S(1)}, u32[]{:S(2)}, u32[]{:S(2)}) collective-permute-start(bf16[2,192,768]{2,1,0:T(8,128)(2,1)} %collective-permute-done.2.refs_3_), channel_id=1, source_target_pairs={{0,32},{32,0},{64,96},{96,64},{128,160},{160,128},{192,224},{224,1... | collective-permute-start | bytes 1769480 | tf_op jit(solution)/shard_map/ppermute | solution.py:376
  126.7 11.4 %collective-permute-start.8 = (bf16[1,192,768]{2,1,0:T(8,128)(2,1)S(1)}, bf16[1,192,768]{2,1,0:T(8,128)(2,1)S(1)}, u32[]{:S(2)}, u32[]{:S(2)}) collective-permute-start(bf16[1,192,768]{2,1,0:T(8,128)(2,1)S(1)} %slice_select_fusion), channel_id=1, source_target_pairs={{0,128},{32,416},{64,192},{96,480},{128,256},{160,32},{192,320},{2... | collective-permute-start | bytes 884744 | tf_op jit(solution)/shard_map/ppermute | solution.py:381
  132.9 9.4 %collective-permute-start.7 = (bf16[2,192,768]{2,1,0:T(8,128)(2,1)S(1)}, bf16[2,192,768]{2,1,0:T(8,128)(2,1)S(1)}, u32[]{:S(2)}, u32[]{:S(2)}) collective-permute-start(bf16[2,192,768]{2,1,0:T(8,128)(2,1)S(1)} %collective-permute-done.5.refs_4_), channel_id=1, source_target_pairs={{0,32},{32,0},{64,96},{96,64},{128,160},{160,128},{192,224},{224,1... | collective-permute-start | bytes 1769480 | tf_op jit(solution)/shard_map/ppermute | solution.py:376
  138.0 4.2 %collective-permute-start.9 = (bf16[1,192,768]{2,1,0:T(8,128)(2,1)S(1)}, bf16[1,192,768]{2,1,0:T(8,128)(2,1)S(1)}, u32[]{:S(2)}, u32[]{:S(2)}) collective-permute-start(bf16[1,192,768]{2,1,0:T(8,128)(2,1)S(1)} %collective-permute-done.8.refs_7_), channel_id=1, source_target_pairs={{0,32},{32,0},{64,96},{96,64},{128,160},{160,128},{192,224},{224,1... | collective-permute-start | bytes 884744 | tf_op jit(solution)/shard_map/ppermute | solution.py:376

commit v3 on v2

--- a/solution.py
+++ b/solution.py
@@ -109,7 +109,7 @@
     return lax.rsqrt(jnp.sum(values * values, axis=-1, keepdims=True) * (1.0 / WIDTH) + EPS)
 
 
-def pack_window(noise_ref, keep_ref, gains_ref, window_ref, out_ref, params_ref):
+def bundle(noise_ref, keep_ref, gains_ref, params_ref):
     for f in range(FRAMES):
         level = jnp.full((8, 128), noise_ref[f], F32)
         params_ref[f] = lax.rsqrt(1.0 + level * level)
@@ -119,6 +119,9 @@
             params_ref[2 * FRAMES + norm, c : c + 1, :] = gains_ref[
                 norm : norm + 1, 128 * c : 128 * c + 128
             ]
+
+
+def pack_window(window_ref, out_ref):
     for h in range(2):
         out_ref[:, 4 * h : 4 * h + 4] = window_ref[0:16, :, :, ATTN * h : ATTN * h + ATTN]
     for c in range(3):
@@ -205,18 +208,23 @@
             out_ref[2 * i, at : at + 8, :] = odd[i].astype(BF16)
 
 
-def put_chunks(values, out_ref):
-    for c in range(6):
-        block = values[:512, 128 * c : 128 * c + 128].reshape(LATS, 16, 128)
-        out_ref[:, 16 * c : 16 * c + 16, :] = block.astype(BF16)
+def put_chunks(columns, out_ref, out_any, sems):
     slot = lax.broadcasted_iota(jnp.int32, (LATS, 8, 128), 1)
-    for t in range(2):
-        tile = None
-        for q in range(3):
-            at = 256 * q + 128 * t
-            part = values[512:, at : at + 128].reshape(LATS, 8, 128)
-            tile = part if tile is None else jnp.where(slot // 2 == q, part, tile)
-        out_ref[:, 96 + 8 * t : 104 + 8 * t, :] = tile.astype(BF16)
+    tiles, copies = [None, None], []
+    for q in range(3):
+        values = columns(q)
+        for t in range(2):
+            at = 32 * q + 16 * t
+            block = values[:512, 128 * t : 128 * t + 128].reshape(LATS, 16, 128)
+            out_ref[:, at : at + 16, :] = block.astype(BF16)
+            part = values[512:, 128 * t : 128 * t + 128].reshape(LATS, 8, 128)
+            tiles[t] = part if q == 0 else jnp.where(slot // 2 == q, part, tiles[t])
+        if q == 2:
+            for t in range(2):
+                out_ref[:, 96 + 8 * t : 104 + 8 * t, :] = tiles[t].astype(BF16)
+        rows = slice(32 * q, 32 * q + (32 if q < 2 else 48))
+        copies.append(fetch(out_ref.at[:, rows, :], out_any.at[:, rows, :], sems.at[q]))
+    return copies
 
 
 def get_chunks(in_ref, rows_ref):
@@ -236,7 +244,7 @@
 
 def to_spectra(
     frame_ref, params_ref, mixed_ref, window_any, w_any, tables_any,
-    carry_any, out_ref, mixed_rows, base_rows, split_ref, window_ref, w_ref, table_ref, sems,
+    carry_any, out_any, out_ref, mixed_rows, base_rows, kept_ref, window_ref, w_ref, table_ref, sems, out_sems,
 ):
     w_copy = fetch(w_any, w_ref, sems.at[0])
     window_copy = fetch(window_any, window_ref, sems.at[1])
@@ -259,29 +267,34 @@
     first = window_ref[...].astype(F32) * scale + jnp.dot(
         mixed_rows[...], w_ref[...], preferred_element_type=F32
     )
-    high = first.astype(BF16)
-    split_ref[0] = high
-    split_ref[1] = (first - high.astype(F32)).astype(BF16)
+    kept_ref[...] = first.astype(BF16)
     carries = [
-        fetch(split_ref, carry_any.at[0:2], sems.at[3]),
-        fetch(window_ref, carry_any.at[2], sems.at[4]),
+        fetch(kept_ref, carry_any.at[0], sems.at[3]),
+        fetch(window_ref, carry_any.at[1], sems.at[4]),
     ]
     base_rows[0:POINTS, :] = (first * row_scale(first) * gain).astype(BF16)
     base_rows[POINTS:640, :] = jnp.zeros((640 - POINTS, WIDTH), BF16)
     table_copy.wait()
-    put_chunks(jnp.dot(table_ref[...], base_rows[...], preferred_element_type=F32), out_ref)
-    for copy in carries:
+
+    def columns(q):
+        cols = slice(256 * q, 256 * q + 256)
+        return jnp.dot(table_ref[...], base_rows[:, cols], preferred_element_type=F32)
+
+    for copy in carries + put_chunks(columns, out_ref, out_any, out_sems):
         copy.wait()
 
 
-def filter_orders(in_ref, down_ref, up_ref, filter_ref, out_ref, rows_ref, coeffs_ref):
+def filter_orders(in_ref, down_ref, up_ref, out_any, out_ref, rows_ref, coeffs_ref, sems):
     get_chunks(in_ref, rows_ref)
-    factor = filter_ref[...].astype(F32)
-    coeffs = jnp.dot(down_ref[...], rows_ref[...], preferred_element_type=F32)
+    degrees = 2 * ORDERS * LMAX
+    factor = down_ref[degrees : degrees + LMAX, :].astype(F32)
+    coeffs = jnp.dot(down_ref[0:degrees, :], rows_ref[...], preferred_element_type=F32)
     for b in range(2 * ORDERS):
         rows = slice(LMAX * b, LMAX * (b + 1))
         coeffs_ref[rows, :] = (coeffs[rows] * factor).astype(BF16)
-    put_chunks(jnp.dot(up_ref[...], coeffs_ref[...], preferred_element_type=F32), out_ref)
+    values = jnp.dot(up_ref[...], coeffs_ref[...], preferred_element_type=F32)
+    for copy in put_chunks(lambda q: values[:, 256 * q : 256 * q + 256], out_ref, out_any, sems):
+        copy.wait()
 
 
 def gelu(x):
@@ -298,7 +311,7 @@
     ) = refs
     in_copy = fetch(in_any, in_ref, sems.at[2])
     table_copy = fetch(tables_any.at[1, 0:POINTS], table_ref, sems.at[0])
-    first_copy = fetch(carry_any.at[0:2], carry_ref.at[0:2], sems.at[1])
+    first_copy = fetch(carry_any.at[0], carry_ref.at[0], sems.at[1])
     in_copy.wait()
     get_chunks(in_ref, rows_ref)
     w_copies, at = [], 0
@@ -309,8 +322,8 @@
     table_copy.wait()
     second_ref[...] = jnp.dot(table_ref[...], rows_ref[...], preferred_element_type=F32)
     first_copy.wait()
-    window_copy = fetch(carry_any.at[2], carry_ref.at[2], sems.at[4])
-    second = carry_ref[0].astype(F32) + carry_ref[1].astype(F32) + second_ref[...]
+    window_copy = fetch(carry_any.at[1], carry_ref.at[1], sems.at[4])
+    second = carry_ref[0].astype(F32) + second_ref[...]
     second_ref[...] = second
     inner_ref[...] = (second * row_scale(second) * gain).astype(BF16)
     for b in range(2):
@@ -333,7 +346,7 @@
         denoised = second_ref[rows, :] + jnp.dot(
             hidden_ref[rows, :], w_down, preferred_element_type=F32
         )
-        state = carry_ref[2, rows, :].astype(F32)
+        state = carry_ref[1, rows, :].astype(F32)
         out_ref[rows, :] = (denoised + ratio * (state - denoised)).astype(BF16)
         copies.append(fetch(out_ref.at[rows], out_any.at[rows], sems.at[5 + j]))
     for copy in copies:
@@ -392,17 +405,28 @@
     shape = jax.ShapeDtypeStruct
 
     state = window.reshape(POINTS, WIDTH)
-    packed, params = call(
+    (packed,) = call(
         pack_window,
-        [shape((FRAMES, 9, 8, ATTN), BF16), shape((2 * FRAMES + 3, 8, 128), F32)],
-        "ssvvvv",
+        [shape((FRAMES, 9, 8, ATTN), BF16)],
+        "vv",
         [],
-        [noise_level, keep_ratio, norm_gains, window.reshape(18, 4, 8, WIDTH)],
+        [window.reshape(18, 4, 8, WIDTH)],
         0,
         LIMITS[0],
     )
     ahead = shift(state, -1)
-    packed, legendre, w_in, w_down = lax.optimization_barrier((packed, legendre, w_in, w_down))
+    packed, legendre, w_in, w_down, norm_gains = lax.optimization_barrier(
+        (packed, legendre, w_in, w_down, norm_gains)
+    )
+    (params,) = call(
+        bundle,
+        [shape((2 * FRAMES + 3, 8, 128), F32)],
+        "ssvv",
+        [],
+        [noise_level, keep_ratio, norm_gains],
+        0,
+        4,
+    )
     own = jnp.concatenate([w_in, w_down], 0)[None]
     other = swap_cores(own)
     pair = jnp.where(
@@ -411,6 +435,7 @@
     local = lax.dynamic_slice_in_dim(legendre, ORDERS * lat, ORDERS, 1)
     down = jnp.einsum("ilj,icjn->icln", local[0], placement, preferred_element_type=F32)
     down = down.astype(BF16).reshape(2 * ORDERS * LMAX, 768)
+    down = jnp.concatenate([down, spectral_filter], 0)
     up = jnp.einsum("ilj,icjn->nicl", local[1], placement, preferred_element_type=F32)
     up = up.astype(BF16).reshape(768, 2 * ORDERS * LMAX)
 
@@ -427,16 +452,18 @@
     mixed = exchange(mixed, "lead")
     carry, spectra = call(
         to_spectra,
-        [shape((3, POINTS, WIDTH), BF16), shape((LATS, 112, 128), BF16)],
-        "svvhhhhv",
+        [shape((2, POINTS, WIDTH), BF16), shape((LATS, 112, 128), BF16)],
+        "svvhhhhh",
         [
+            ((LATS, 112, 128), BF16),
             ((POINTS, ATTN), BF16),
             ((640, WIDTH), BF16),
-            ((2, POINTS, WIDTH), BF16),
+            ((POINTS, WIDTH), BF16),
             ((POINTS, WIDTH), BF16),
             ((ATTN, WIDTH), BF16),
             ((768, 640), BF16),
             5,
+            3,
         ],
         [frame, params, mixed, ahead, w_out, tables],
         2 * POINTS * WIDTH * (ATTN + 768),
@@ -451,9 +478,14 @@
     (back,) = call(
         filter_orders,
         [shape((LATS, 112, 128), BF16)],
-        "vvvvv",
-        [((768, WIDTH), BF16), ((2 * ORDERS * LMAX, WIDTH), BF16)],
-        [by_order, down, up, spectral_filter],
+        "vvvh",
+        [
+            ((LATS, 112, 128), BF16),
+            ((768, WIDTH), BF16),
+            ((2 * ORDERS * LMAX, WIDTH), BF16),
+            3,
+        ],
+        [by_order, down, up],
         4 * POINTS * WIDTH * 768,
         LIMITS[3],
     )
@@ -471,7 +503,7 @@
             ((POINTS, FF), BF16),
             ((POINTS, WIDTH), BF16),
             ((POINTS, 768), BF16),
-            ((3, POINTS, WIDTH), BF16),
+            ((2, POINTS, WIDTH), BF16),
             ((POINTS, WIDTH), F32),
             ((FRAMES, 192, WIDTH), BF16),
             ((LATS, 112, 128), BF16),

time: 152 us -> 151 us (level)
  waiting for transfers between devices: 54.7 us -> 56.5 us
    all_to_all x4, waiting for transfers between devices: 35.2 us -> 37.3 us  [exchange(): return lax.all_to_all(chunks, axis, split_axis=0, concat_axis=0, tiled=True)]
    pallas_call x5 -> x6, Pallas kernels: 22.9 us -> 22.4 us  [call(): pl.pallas_call(kernel, out_shape=outs, in_specs=specs[:len(args)], out_sp...]
  transfers between devices with their start and end apart: 14 -> 14, of which waited for: 10 -> 10; matrix products, arithmetic and copies ran while one was open for 5% -> 4% of each run, Pallas kernels for 3% -> 4%
where the time goes in v3:
time: 151 us; the launch traced here: 150 us
  starting transfers between devices  63.9 us (42%)
  waiting for transfers between devices  56.5 us (37%)
  Pallas kernels  22.4 us (15%)
  matrix products  2.87 us (2%)
  other arithmetic  2.18 us (1%)
  local copies, waits for them, and re-layouts  1.59 us (1%)
    all_to_all x4, waiting for transfers between devices, exchange(): return lax.all_to_all(chunks, axis, split_axis=0, concat_axis=0, tiled=True)  37.3 us
    all_to_all x4, starting transfers between devices, exchange(): return lax.all_to_all(chunks, axis, split_axis=0, concat_axis=0, tiled=True)  33.8 us
    pallas_call x6, Pallas kernels, call(): pl.pallas_call(kernel, out_shape=outs, in_specs=specs[:len(args)], out_sp...  22.4 us
    ppermute x5, starting transfers between devices, swap_cores(): lax.ppermute(value, 'lead', [(source, source ^ 1) for source in range(FRA...  17.7 us
    ppermute x4, waiting for transfers between devices, round_chips(): return lax.ppermute(value, 'lead', hops)  15.9 us
    ppermute x4, starting transfers between devices, round_chips(): return lax.ppermute(value, 'lead', hops)  12.2 us
  transfers between devices with their start and end apart: 14, of which 10 were waited for; matrix products, arithmetic and copies ran while one was open for 4% of the time, Pallas kernels for 4%

profile of v3, /device:TPU:1, one launch (start us, length us, event | category | flops | bytes accessed | tf_op | source)
XLA Modules:
  0.0 149.8 jit_solution(20981537565868350)
XLA Ops:
  0.0 0.0 copy-start.4
  0.0 0.0 copy-start.5
  0.0 0.0 copy-start.6
  0.0 2.3 %shard_map.118 = bf16[16,9,8,384]{3,2,1,0:T(8,128)(2,1)} custom-call(bf16[18,4,8,768]{3,2,1,0:T(8,128)(2,1)} %bitcast.28), custom_call_target="tpu_custom_call" | custom-call | bytes 1769472 | tf_op jit(solution)/shard_map/pallas_call | solution.py:361
  2.3 11.8 %all-to-all-start = ((bf16[16,9,8,384]{3,2,1,0:T(8,128)(2,1)}), bf16[16,9,8,384]{3,2,1,0:T(8,128)(2,1)S(1)}, u32[]{:S(2)}, u32[]{:S(2)}) async-start(bf16[16,9,8,384]{3,2,1,0:T(8,128)(2,1)} %shard_map.118), calls=%async_computation | async-start | bytes 1769472 | tf_op jit(solution)/shard_map/all_to_all | solution.py:380
  14.1 0.0 copy-done.8
  14.1 0.1 collective-permute-start
  14.3 0.0 copy-done.9
  14.3 4.8 %collective-permute-start.1 = (bf16[1,192,768]{2,1,0:T(8,128)(2,1)S(1)}, bf16[1,192,768]{2,1,0:T(8,128)(2,1)S(1)}, u32[]{:S(2)}, u32[]{:S(2)}) collective-permute-start(bf16[1,192,768]{2,1,0:T(8,128)(2,1)S(1)} %maximum_bitcast_fusion), channel_id=1, source_target_pairs={{0,32},{32,0},{64,96},{96,64},{128,160},{160,128},{192,224},{224,1... | collective-permute-start | bytes 884744 | tf_op jit(solution)/shard_map/ppermute | solution.py:389
  19.1 0.6 shard_map.119.params_ref
  19.7 0.6 collective-permute-done.1
  20.3 0.1 maximum_select_fusion.refs_0_
  20.4 0.0 copy-start.1
  20.4 18.4 %all-to-all-done.in_ref = bf16[16,9,8,384]{3,2,1,0:T(8,128)(2,1)S(1)} async-done(((bf16[16,9,8,384]{3,2,1,0:T(8,128)(2,1)}), bf16[16,9,8,384]{3,2,1,0:T(8,128)(2,1)S(1)}, u32[]{:S(2)}, u32[]{:S(2)}) %all-to-all-start) | async-done | bytes 884768 | tf_op jit(solution)/shard_map/all_to_all | solution.py:380
  38.8 4.8 %shard_map.120 = bf16[16,112,128]{2,1,0:T(8,128)(2,1)} custom-call(f32[35,8,128]{2,1,0:T(8,128)S(1)} %shard_map.119.params_ref, bf16[16,9,8,384]{3,2,1,0:T(8,128)(2,1)S(1)} %all-to-all-done.in_ref, bf16[768,1152]{1,0:T(8,128)(2,1)} %w_any.2), custom_call_target="tpu_custom_call" | custom-call | flops 1019215872 | bytes 3256320 | tf_op jit(solution)/shard_map/pallas_call | solution.py:361
  43.6 1.7 %collective-permute-done.window_any = bf16[576,768]{1,0:T(8,128)(2,1)} collective-permute-done((bf16[576,768]{1,0:T(8,128)(2,1)S(1)}, bf16[576,768]{1,0:T(8,128)(2,1)}, u32[]{:S(2)}, u32[]{:S(2)}) %collective-permute-start) | collective-permute-done | bytes 884768 | tf_op jit(solution)/shard_map/ppermute | solution.py:385
  45.3 5.8 %all-to-all-start.1 = ((bf16[16,112,128]{2,1,0:T(8,128)(2,1)}), bf16[16,112,128]{2,1,0:T(8,128)(2,1)S(1)}, u32[]{:S(2)}, u32[]{:S(2)}) async-start(bf16[16,112,128]{2,1,0:T(8,128)(2,1)} %shard_map.120), calls=%async_computation.1 | async-start | bytes 917504 | tf_op jit(solution)/shard_map/all_to_all | solution.py:380
  51.1 16.0 %all-to-all-done.1.mixed_ref = bf16[16,112,128]{2,1,0:T(8,128)(2,1)S(1)} async-done(((bf16[16,112,128]{2,1,0:T(8,128)(2,1)}), bf16[16,112,128]{2,1,0:T(8,128)(2,1)S(1)}, u32[]{:S(2)}, u32[]{:S(2)}) %all-to-all-start.1) | async-done | bytes 458784 | tf_op jit(solution)/shard_map/all_to_all | solution.py:380
  67.1 4.6 %shard_map.121 = (bf16[2,576,768]{2,1,0:T(8,128)(2,1)}, bf16[32,112,128]{2,1,0:T(8,128)(2,1)}) custom-call(s32[1]{0:T(128)} %bitcast.frame_ref, f32[35,8,128]{2,1,0:T(8,128)S(1)} %shard_map.119.params_ref, bf16[16,112,128]{2,1,0:T(8,128)(2,1)S(1)} %all-to-all-done.1.mixed_ref, bf16[576,768]{1,0:T(8,128)(2,1)} %collective-permute-done.window_any, ...), custom_call_target="tpu_custom_call" | custom-call | flops 1019215872 | bytes 7122948 | tf_op jit(solution)/shard_map/pallas_call | solution.py:361
  71.7 0.0 copy-start.7
  71.7 9.8 %all-to-all-start.2 = ((bf16[32,112,128]{2,1,0:T(8,128)(2,1)}), bf16[32,112,128]{2,1,0:T(8,128)(2,1)S(1)}, u32[]{:S(2)}, u32[]{:S(2)}) async-start(bf16[32,112,128]{2,1,0:T(8,128)(2,1)} %get-tuple-element.30), calls=%async_computation.2 | async-start | bytes 1835008 | tf_op jit(solution)/shard_map/all_to_all | solution.py:380
  81.5 1.9 %collective-permute-start.3 = (bf16[2,192,768]{2,1,0:T(8,128)(2,1)S(1)}, bf16[2,192,768]{2,1,0:T(8,128)(2,1)}, u32[]{:S(2)}, u32[]{:S(2)}) collective-permute-start(bf16[2,192,768]{2,1,0:T(8,128)(2,1)S(1)} %maximum_select_fusion.refs_0_), channel_id=1, source_target_pairs={{0,64},{32,480},{64,128},{96,32},{128,192},{160,96},{192,256},{224... | collective-permute-start | bytes 1769480 | tf_op jit(solution)/shard_map/ppermute | solution.py:394
  83.5 2.4 %collective-permute-start.2 = (bf16[2,192,768]{2,1,0:T(8,128)(2,1)S(1)}, bf16[2,192,768]{2,1,0:T(8,128)(2,1)}, u32[]{:S(2)}, u32[]{:S(2)}) collective-permute-start(bf16[2,192,768]{2,1,0:T(8,128)(2,1)S(1)} %maximum_select_fusion.refs_0_), channel_id=1, source_target_pairs={{0,128},{32,416},{64,192},{96,480},{128,256},{160,32},{192,320},{2... | collective-permute-start | bytes 1769480 | tf_op jit(solution)/shard_map/ppermute | solution.py:394
  85.9 7.9 %collective-permute-done.3.refs_1_ = bf16[2,192,768]{2,1,0:T(8,128)(2,1)} collective-permute-done((bf16[2,192,768]{2,1,0:T(8,128)(2,1)S(1)}, bf16[2,192,768]{2,1,0:T(8,128)(2,1)}, u32[]{:S(2)}, u32[]{:S(2)}) %collective-permute-start.3) | collective-permute-done | bytes 589856 | tf_op jit(solution)/shard_map/ppermute | solution.py:394
  93.8 4.7 %collective-permute-start.4 = (bf16[2,192,768]{2,1,0:T(8,128)(2,1)}, bf16[2,192,768]{2,1,0:T(8,128)(2,1)}, u32[]{:S(2)}, u32[]{:S(2)}) collective-permute-start(bf16[2,192,768]{2,1,0:T(8,128)(2,1)} %collective-permute-done.3.refs_1_), channel_id=1, source_target_pairs={{0,32},{32,0},{64,96},{96,64},{128,160},{160,128},{192,224},{224,1... | collective-permute-start | bytes 1769480 | tf_op jit(solution)/shard_map/ppermute | solution.py:389
  98.5 1.3 convolution_convert_fusion
  99.8 0.6 copy.14.up_ref
  100.4 1.6 %convolution_convert_fusion.1 = bf16[3,96,2,768]{3,1,2,0:T(8,128)(2,1)S(1)} fusion(bf16[3,2,96,768]{3,2,1,0:T(8,128)(2,1)} %constant.40.clone, bf16[2,96,96,96]{3,2,1,0:T(8,128)(2,1)} %constant.39.clone, s32[]{:T(128)S(6)} %select_n.31), kind=kOutput, calls=%fused_computation.1 | convolution fusion | flops 85377024 | bytes 1843204 | tf_op jit(solution)/shard_map/ilj,icjn->icln/dot_general | solution.py:436
  102.0 1.0 pad_maximum_fusion.down_ref
  103.0 0.7 collective-permute-done.2.refs_3_
  103.7 0.0 collective-permute-done.4.refs_2_
  103.7 3.0 %all-to-all-done.2.in_ref = bf16[32,112,128]{2,1,0:T(8,128)(2,1)S(1)} async-done(((bf16[32,112,128]{2,1,0:T(8,128)(2,1)}), bf16[32,112,128]{2,1,0:T(8,128)(2,1)S(1)}, u32[]{:S(2)}, u32[]{:S(2)}) %all-to-all-start.2) | async-done | bytes 917536 | tf_op jit(solution)/shard_map/all_to_all | solution.py:380
  106.7 2.2 %shard_map.122 = bf16[32,112,128]{2,1,0:T(8,128)(2,1)S(1)} custom-call(bf16[32,112,128]{2,1,0:T(8,128)(2,1)S(1)} %all-to-all-done.2.in_ref, bf16[672,768]{1,0:T(8,128)(2,1)S(1)} %pad_maximum_fusion.down_ref, bf16[768,576]{1,0:T(8,128)(2,1)S(1)} %copy.14.up_ref), custom_call_target="tpu_custom_call" | custom-call | flops 1358954496 | bytes 3751936 | tf_op jit(solution)/shard_map/pallas_call | solution.py:361
  108.9 0.9 copy-done
  109.8 6.4 %all-to-all-start.3 = ((bf16[32,112,128]{2,1,0:T(8,128)(2,1)}), bf16[32,112,128]{2,1,0:T(8,128)(2,1)}, u32[]{:S(2)}, u32[]{:S(2)}) async-start(bf16[32,112,128]{2,1,0:T(8,128)(2,1)} %copy-done), calls=%async_computation.3 | async-start | bytes 1835008 | tf_op jit(solution)/shard_map/all_to_all | solution.py:380
  116.2 5.7 %collective-permute-start.5 = (bf16[2,192,768]{2,1,0:T(8,128)(2,1)}, bf16[2,192,768]{2,1,0:T(8,128)(2,1)S(1)}, u32[]{:S(2)}, u32[]{:S(2)}) collective-permute-start(bf16[2,192,768]{2,1,0:T(8,128)(2,1)} %collective-permute-done.2.refs_3_), channel_id=1, source_target_pairs={{0,64},{32,480},{64,128},{96,32},{128,192},{160,96},{192,256},{224... | collective-permute-start | bytes 1769480 | tf_op jit(solution)/shard_map/ppermute | solution.py:394
  121.9 3.0 %collective-permute-start.6 = (bf16[2,192,768]{2,1,0:T(8,128)(2,1)}, bf16[2,192,768]{2,1,0:T(8,128)(2,1)S(1)}, u32[]{:S(2)}, u32[]{:S(2)}) collective-permute-start(bf16[2,192,768]{2,1,0:T(8,128)(2,1)} %collective-permute-done.2.refs_3_), channel_id=1, source_target_pairs={{0,32},{32,0},{64,96},{96,64},{128,160},{160,128},{192,224},{224,1... | collective-permute-start | bytes 1769480 | tf_op jit(solution)/shard_map/ppermute | solution.py:389
  124.9 1.1 slice_select_fusion
  126.0 2.2 %collective-permute-start.8 = (bf16[1,192,768]{2,1,0:T(8,128)(2,1)S(1)}, bf16[1,192,768]{2,1,0:T(8,128)(2,1)S(1)}, u32[]{:S(2)}, u32[]{:S(2)}) collective-permute-start(bf16[1,192,768]{2,1,0:T(8,128)(2,1)S(1)} %slice_select_fusion), channel_id=1, source_target_pairs={{0,128},{32,416},{64,192},{96,480},{128,256},{160,32},{192,320},{2... | collective-permute-start | bytes 884744 | tf_op jit(solution)/shard_map/ppermute | solution.py:394
  128.2 4.0 %collective-permute-done.5.refs_4_ = bf16[2,192,768]{2,1,0:T(8,128)(2,1)S(1)} collective-permute-done((bf16[2,192,768]{2,1,0:T(8,128)(2,1)}, bf16[2,192,768]{2,1,0:T(8,128)(2,1)S(1)}, u32[]{:S(2)}, u32[]{:S(2)}) %collective-permute-start.5) | collective-permute-done | bytes 589856 | tf_op jit(solution)/shard_map/ppermute | solution.py:394
  132.2 1.9 %collective-permute-start.7 = (bf16[2,192,768]{2,1,0:T(8,128)(2,1)S(1)}, bf16[2,192,768]{2,1,0:T(8,128)(2,1)S(1)}, u32[]{:S(2)}, u32[]{:S(2)}) collective-permute-start(bf16[2,192,768]{2,1,0:T(8,128)(2,1)S(1)} %collective-permute-done.5.refs_4_), channel_id=1, source_target_pairs={{0,32},{32,0},{64,96},{96,64},{128,160},{160,128},{192,224},{224,1... | collective-permute-start | bytes 1769480 | tf_op jit(solution)/shard_map/ppermute | solution.py:389
  134.1 3.3 %collective-permute-done.8.refs_7_ = bf16[1,192,768]{2,1,0:T(8,128)(2,1)S(1)} collective-permute-done((bf16[1,192,768]{2,1,0:T(8,128)(2,1)S(1)}, bf16[1,192,768]{2,1,0:T(8,128)(2,1)S(1)}, u32[]{:S(2)}, u32[]{:S(2)}) %collective-permute-start.8) | collective-permute-done | bytes 294944 | tf_op jit(solution)/shard_map/ppermute | solution.py:394
  137.4 3.2 %collective-permute-start.9 = (bf16[1,192,768]{2,1,0:T(8,128)(2,1)S(1)}, bf16[1,192,768]{2,1,0:T(8,128)(2,1)S(1)}, u32[]{:S(2)}, u32[]{:S(2)}) collective-permute-start(bf16[1,192,768]{2,1,0:T(8,128)(2,1)S(1)} %collective-permute-done.8.refs_7_), channel_id=1, source_target_pairs={{0,32},{32,0},{64,96},{96,64},{128,160},{160,128},{192,224},{224,1... | collective-permute-start | bytes 884744 | tf_op jit(solution)/shard_map/ppermute | solution.py:389
  140.6 0.0 collective-permute-done.6.refs_5_
  140.6 1.0 collective-permute-done.9.refs_8_
  141.6 0.0 collective-permute-done.7.refs_6_
  141.6 0.0 all-to-all-done.3.in_any
  141.6 8.0 %shard_map.123 = bf16[576,768]{1,0:T(8,128)(2,1)} custom-call(s32[1]{0:T(128)} %bitcast.frame_ref, f32[35,8,128]{2,1,0:T(8,128)S(1)} %copy-done.3, bf16[32,112,128]{2,1,0:T(8,128)(2,1)} %all-to-all-done.3.in_any, bf16[2,768,768]{2,1,0:T(8,128)(2,1)} %constant.38.clone.tables_any, bf16[2,576,768]{2,1,0:T(8,128)(2,1)} %get-tuple-element.36.carry_any, ...), custom_call_target="tpu_custom_call" | custom-call | flops 3397386240 | bytes 10792964 | tf_op jit(solution)/shard_map/pallas_call | solution.py:361
  (15 shorter events, 0.0 us)
Async XLA Ops:
  0.0 14.1 %copy-start.8 = (bf16[1,3,192,768]{3,2,1,0:T(8,128)(2,1)S(1)}, bf16[1,3,192,768]{3,2,1,0:T(8,128)(2,1)}, u32[]{:S(2)}) copy-start(bf16[1,3,192,768]{3,2,1,0:T(8,128)(2,1)} %param.12) | copy-start | bytes 2654212
  0.0 14.3 %copy-start.9 = (bf16[96,768]{1,0:T(8,128)(2,1)S(1)}, bf16[96,768]{1,0:T(8,128)(2,1)}, u32[]{:S(2)}) copy-start(bf16[96,768]{1,0:T(8,128)(2,1)} %param.20) | copy-start | bytes 442372
  0.0 14.3 %copy-start.10 = (bf16[96,768]{1,0:T(8,128)(2,1)S(1)}, bf16[96,768]{1,0:T(8,128)(2,1)}, u32[]{:S(2)}) copy-start(bf16[96,768]{1,0:T(8,128)(2,1)} %param.19) | copy-start | bytes 442372
  0.0 19.1 %copy-start.4 = (f32[3,768]{1,0:T(4,128)S(1)}, f32[3,768]{1,0:T(4,128)}, u32[]{:S(2)}) copy-start(f32[3,768]{1,0:T(4,128)} %gains_ref) | copy-start | bytes 27652
  0.0 19.1 %copy-start.5 = (f32[16]{0:T(128)S(1)}, f32[16]{0:T(128)}, u32[]{:S(2)}) copy-start(f32[16]{0:T(128)} %noise_ref.1) | copy-start | bytes 196
  0.0 19.1 %copy-start.6 = (f32[16]{0:T(128)S(1)}, f32[16]{0:T(128)}, u32[]{:S(2)}) copy-start(f32[16]{0:T(128)} %keep_ref.1) | copy-start | bytes 196
  2.3 36.5 %all-to-all-start = ((bf16[16,9,8,384]{3,2,1,0:T(8,128)(2,1)}), bf16[16,9,8,384]{3,2,1,0:T(8,128)(2,1)S(1)}, u32[]{:S(2)}, u32[]{:S(2)}) async-start(bf16[16,9,8,384]{3,2,1,0:T(8,128)(2,1)} %shard_map.118), calls=%async_computation | async-start | bytes 1769472 | tf_op jit(solution)/shard_map/all_to_all | solution.py:380
  14.1 31.1 %collective-permute-start = (bf16[576,768]{1,0:T(8,128)(2,1)S(1)}, bf16[576,768]{1,0:T(8,128)(2,1)}, u32[]{:S(2)}, u32[]{:S(2)}) collective-permute-start(bf16[576,768]{1,0:T(8,128)(2,1)S(1)} %bitcast.29), channel_id=1, source_target_pairs={{0,480},{32,0},{64,32},{96,64},{128,96},{160,128},{192,160},{224,1... | collective-permute-start | bytes 2654216 | tf_op jit(solution)/shard_map/ppermute | solution.py:385
  14.3 6.0 %collective-permute-start.1 = (bf16[1,192,768]{2,1,0:T(8,128)(2,1)S(1)}, bf16[1,192,768]{2,1,0:T(8,128)(2,1)S(1)}, u32[]{:S(2)}, u32[]{:S(2)}) collective-permute-start(bf16[1,192,768]{2,1,0:T(8,128)(2,1)S(1)} %maximum_bitcast_fusion), channel_id=1, source_target_pairs={{0,32},{32,0},{64,96},{96,64},{128,160},{160,128},{192,224},{224,1... | collective-permute-start | bytes 884744 | tf_op jit(solution)/shard_map/ppermute | solution.py:389
  19.7 47.4 %copy-start.2 = (f32[35,8,128]{2,1,0:T(8,128)}, f32[35,8,128]{2,1,0:T(8,128)S(1)}, u32[]{:S(2)}) copy-start(f32[35,8,128]{2,1,0:T(8,128)S(1)} %shard_map.119.params_ref) | copy-start | bytes 430084
  20.4 46.7 %copy-start.1 = (bf16[384,768]{1,0:T(8,128)(2,1)S(1)}, bf16[384,768]{1,0:T(8,128)(2,1)}, u32[]{:S(2)}) copy-start(bf16[384,768]{1,0:T(8,128)(2,1)} %w_any.3) | copy-start | bytes 1769476
  45.3 21.8 %all-to-all-start.1 = ((bf16[16,112,128]{2,1,0:T(8,128)(2,1)}), bf16[16,112,128]{2,1,0:T(8,128)(2,1)S(1)}, u32[]{:S(2)}, u32[]{:S(2)}) async-start(bf16[16,112,128]{2,1,0:T(8,128)(2,1)} %shard_map.120), calls=%async_computation.1 | async-start | bytes 917504 | tf_op jit(solution)/shard_map/all_to_all | solution.py:380
  71.7 26.8 %copy-start.7 = (bf16[3,2,96,768]{3,2,1,0:T(8,128)(2,1)S(1)}, bf16[3,2,96,768]{3,2,1,0:T(8,128)(2,1)}, u32[]{:S(2)}) copy-start(bf16[3,2,96,768]{3,2,1,0:T(8,128)(2,1)} %constant.40.clone) | copy-start | bytes 2654212
  71.7 35.0 %all-to-all-start.2 = ((bf16[32,112,128]{2,1,0:T(8,128)(2,1)}), bf16[32,112,128]{2,1,0:T(8,128)(2,1)S(1)}, u32[]{:S(2)}, u32[]{:S(2)}) async-start(bf16[32,112,128]{2,1,0:T(8,128)(2,1)} %get-tuple-element.30), calls=%async_computation.2 | async-start | bytes 1835008 | tf_op jit(solution)/shard_map/all_to_all | solution.py:380
  81.5 12.3 %collective-permute-start.3 = (bf16[2,192,768]{2,1,0:T(8,128)(2,1)S(1)}, bf16[2,192,768]{2,1,0:T(8,128)(2,1)}, u32[]{:S(2)}, u32[]{:S(2)}) collective-permute-start(bf16[2,192,768]{2,1,0:T(8,128)(2,1)S(1)} %maximum_select_fusion.refs_0_), channel_id=1, source_target_pairs={{0,64},{32,480},{64,128},{96,32},{128,192},{160,96},{192,256},{224... | collective-permute-start | bytes 1769480 | tf_op jit(solution)/shard_map/ppermute | solution.py:394
  83.5 20.3 %collective-permute-start.2 = (bf16[2,192,768]{2,1,0:T(8,128)(2,1)S(1)}, bf16[2,192,768]{2,1,0:T(8,128)(2,1)}, u32[]{:S(2)}, u32[]{:S(2)}) collective-permute-start(bf16[2,192,768]{2,1,0:T(8,128)(2,1)S(1)} %maximum_select_fusion.refs_0_), channel_id=1, source_target_pairs={{0,128},{32,416},{64,192},{96,480},{128,256},{160,32},{192,320},{2... | collective-permute-start | bytes 1769480 | tf_op jit(solution)/shard_map/ppermute | solution.py:394
  93.8 9.9 %collective-permute-start.4 = (bf16[2,192,768]{2,1,0:T(8,128)(2,1)}, bf16[2,192,768]{2,1,0:T(8,128)(2,1)}, u32[]{:S(2)}, u32[]{:S(2)}) collective-permute-start(bf16[2,192,768]{2,1,0:T(8,128)(2,1)} %collective-permute-done.3.refs_1_), channel_id=1, source_target_pairs={{0,32},{32,0},{64,96},{96,64},{128,160},{160,128},{192,224},{224,1... | collective-permute-start | bytes 1769480 | tf_op jit(solution)/shard_map/ppermute | solution.py:389
  108.9 0.9 copy-start
  109.8 31.8 %copy-start.3 = (f32[35,8,128]{2,1,0:T(8,128)S(1)}, f32[35,8,128]{2,1,0:T(8,128)}, u32[]{:S(2)}) copy-start(f32[35,8,128]{2,1,0:T(8,128)} %copy-done.2) | copy-start | bytes 430084
  109.8 31.8 %all-to-all-start.3 = ((bf16[32,112,128]{2,1,0:T(8,128)(2,1)}), bf16[32,112,128]{2,1,0:T(8,128)(2,1)}, u32[]{:S(2)}, u32[]{:S(2)}) async-start(bf16[32,112,128]{2,1,0:T(8,128)(2,1)} %copy-done), calls=%async_computation.3 | async-start | bytes 1835008 | tf_op jit(solution)/shard_map/all_to_all | solution.py:380
  116.2 16.0 %collective-permute-start.5 = (bf16[2,192,768]{2,1,0:T(8,128)(2,1)}, bf16[2,192,768]{2,1,0:T(8,128)(2,1)S(1)}, u32[]{:S(2)}, u32[]{:S(2)}) collective-permute-start(bf16[2,192,768]{2,1,0:T(8,128)(2,1)} %collective-permute-done.2.refs_3_), channel_id=1, source_target_pairs={{0,64},{32,480},{64,128},{96,32},{128,192},{160,96},{192,256},{224... | collective-permute-start | bytes 1769480 | tf_op jit(solution)/shard_map/ppermute | solution.py:394
  121.9 18.7 %collective-permute-start.6 = (bf16[2,192,768]{2,1,0:T(8,128)(2,1)}, bf16[2,192,768]{2,1,0:T(8,128)(2,1)S(1)}, u32[]{:S(2)}, u32[]{:S(2)}) collective-permute-start(bf16[2,192,768]{2,1,0:T(8,128)(2,1)} %collective-permute-done.2.refs_3_), channel_id=1, source_target_pairs={{0,32},{32,0},{64,96},{96,64},{128,160},{160,128},{192,224},{224,1... | collective-permute-start | bytes 1769480 | tf_op jit(solution)/shard_map/ppermute | solution.py:389
  126.0 11.4 %collective-permute-start.8 = (bf16[1,192,768]{2,1,0:T(8,128)(2,1)S(1)}, bf16[1,192,768]{2,1,0:T(8,128)(2,1)S(1)}, u32[]{:S(2)}, u32[]{:S(2)}) collective-permute-start(bf16[1,192,768]{2,1,0:T(8,128)(2,1)S(1)} %slice_select_fusion), channel_id=1, source_target_pairs={{0,128},{32,416},{64,192},{96,480},{128,256},{160,32},{192,320},{2... | collective-permute-start | bytes 884744 | tf_op jit(solution)/shard_map/ppermute | solution.py:394
  132.2 9.4 %collective-permute-start.7 = (bf16[2,192,768]{2,1,0:T(8,128)(2,1)S(1)}, bf16[2,192,768]{2,1,0:T(8,128)(2,1)S(1)}, u32[]{:S(2)}, u32[]{:S(2)}) collective-permute-start(bf16[2,192,768]{2,1,0:T(8,128)(2,1)S(1)} %collective-permute-done.5.refs_4_), channel_id=1, source_target_pairs={{0,32},{32,0},{64,96},{96,64},{128,160},{160,128},{192,224},{224,1... | collective-permute-start | bytes 1769480 | tf_op jit(solution)/shard_map/ppermute | solution.py:389
  137.4 4.2 %collective-permute-start.9 = (bf16[1,192,768]{2,1,0:T(8,128)(2,1)S(1)}, bf16[1,192,768]{2,1,0:T(8,128)(2,1)S(1)}, u32[]{:S(2)}, u32[]{:S(2)}) collective-permute-start(bf16[1,192,768]{2,1,0:T(8,128)(2,1)S(1)} %collective-permute-done.8.refs_7_), channel_id=1, source_target_pairs={{0,32},{32,0},{64,96},{96,64},{128,160},{160,128},{192,224},{224,1... | collective-permute-start | bytes 884744 | tf_op jit(solution)/shard_map/ppermute | solution.py:389

commit v4 on v3

--- a/solution.py
+++ b/solution.py
@@ -208,7 +208,7 @@
             out_ref[2 * i, at : at + 8, :] = odd[i].astype(BF16)
 
 
-def put_chunks(columns, out_ref, out_any, sems):
+def put_chunks(columns, out_ref, out_any=None, sems=None):
     slot = lax.broadcasted_iota(jnp.int32, (LATS, 8, 128), 1)
     tiles, copies = [None, None], []
     for q in range(3):
@@ -223,7 +223,8 @@
             for t in range(2):
                 out_ref[:, 96 + 8 * t : 104 + 8 * t, :] = tiles[t].astype(BF16)
         rows = slice(32 * q, 32 * q + (32 if q < 2 else 48))
-        copies.append(fetch(out_ref.at[:, rows, :], out_any.at[:, rows, :], sems.at[q]))
+        if out_any is not None:
+            copies.append(fetch(out_ref.at[:, rows, :], out_any.at[:, rows, :], sems.at[q]))
     return copies
 
 
@@ -284,7 +285,7 @@
         copy.wait()
 
 
-def filter_orders(in_ref, down_ref, up_ref, out_any, out_ref, rows_ref, coeffs_ref, sems):
+def filter_orders(in_ref, down_ref, up_ref, out_ref, rows_ref, coeffs_ref):
     get_chunks(in_ref, rows_ref)
     degrees = 2 * ORDERS * LMAX
     factor = down_ref[degrees : degrees + LMAX, :].astype(F32)
@@ -293,8 +294,7 @@
         rows = slice(LMAX * b, LMAX * (b + 1))
         coeffs_ref[rows, :] = (coeffs[rows] * factor).astype(BF16)
     values = jnp.dot(up_ref[...], coeffs_ref[...], preferred_element_type=F32)
-    for copy in put_chunks(lambda q: values[:, 256 * q : 256 * q + 256], out_ref, out_any, sems):
-        copy.wait()
+    put_chunks(lambda q: values[:, 256 * q : 256 * q + 256], out_ref)
 
 
 def gelu(x):
@@ -478,13 +478,8 @@
     (back,) = call(
         filter_orders,
         [shape((LATS, 112, 128), BF16)],
-        "vvvh",
-        [
-            ((LATS, 112, 128), BF16),
-            ((768, WIDTH), BF16),
-            ((2 * ORDERS * LMAX, WIDTH), BF16),
-            3,
-        ],
+        "vvvv",
+        [((768, WIDTH), BF16), ((2 * ORDERS * LMAX, WIDTH), BF16)],
         [by_order, down, up],
         4 * POINTS * WIDTH * 768,
         LIMITS[3],

time: 151 us -> 151 us (level)
  no operation moved by 1% of the time
where the time goes in v4:
time: 151 us; the launch traced here: 150 us
  starting transfers between devices  63.9 us (42%)
  waiting for transfers between devices  56.5 us (37%)
  Pallas kernels  22.2 us (15%)
  matrix products  2.87 us (2%)
  other arithmetic  2.18 us (1%)
  local copies, waits for them, and re-layouts  1.59 us (1%)
    all_to_all x4, waiting for transfers between devices, exchange(): return lax.all_to_all(chunks, axis, split_axis=0, concat_axis=0, tiled=True)  37.3 us
    all_to_all x4, starting transfers between devices, exchange(): return lax.all_to_all(chunks, axis, split_axis=0, concat_axis=0, tiled=True)  33.8 us
    pallas_call x6, Pallas kernels, call(): pl.pallas_call(kernel, out_shape=outs, in_specs=specs[:len(args)], out_sp...  22.2 us
    ppermute x5, starting transfers between devices, swap_cores(): lax.ppermute(value, 'lead', [(source, source ^ 1) for source in range(FRA...  17.7 us
    ppermute x4, waiting for transfers between devices, round_chips(): return lax.ppermute(value, 'lead', hops)  15.9 us
    ppermute x4, starting transfers between devices, round_chips(): return lax.ppermute(value, 'lead', hops)  12.2 us
  transfers between devices with their start and end apart: 14, of which 10 were waited for; matrix products, arithmetic and copies ran while one was open for 4% of the time, Pallas kernels for 4%

profile of v4, /device:TPU:1, one launch (start us, length us, event | category | flops | bytes accessed | tf_op | source)
XLA Modules:
  0.0 149.6 jit_solution(7835611594613963568)
XLA Ops:
  0.0 0.0 copy-start.4
  0.0 0.0 copy-start.5
  0.0 2.3 %shard_map.118 = bf16[16,9,8,384]{3,2,1,0:T(8,128)(2,1)} custom-call(bf16[18,4,8,768]{3,2,1,0:T(8,128)(2,1)} %bitcast.28), custom_call_target="tpu_custom_call" | custom-call | bytes 1769472 | tf_op jit(solution)/shard_map/pallas_call | solution.py:361
  2.3 11.8 %all-to-all-start = ((bf16[16,9,8,384]{3,2,1,0:T(8,128)(2,1)}), bf16[16,9,8,384]{3,2,1,0:T(8,128)(2,1)S(1)}, u32[]{:S(2)}, u32[]{:S(2)}) async-start(bf16[16,9,8,384]{3,2,1,0:T(8,128)(2,1)} %shard_map.118), calls=%async_computation | async-start | bytes 1769472 | tf_op jit(solution)/shard_map/all_to_all | solution.py:380
  14.1 0.0 copy-done.8
  14.1 0.1 collective-permute-start
  14.3 0.0 copy-done.9
  14.3 4.8 %collective-permute-start.1 = (bf16[1,192,768]{2,1,0:T(8,128)(2,1)S(1)}, bf16[1,192,768]{2,1,0:T(8,128)(2,1)S(1)}, u32[]{:S(2)}, u32[]{:S(2)}) collective-permute-start(bf16[1,192,768]{2,1,0:T(8,128)(2,1)S(1)} %maximum_bitcast_fusion), channel_id=1, source_target_pairs={{0,32},{32,0},{64,96},{96,64},{128,160},{160,128},{192,224},{224,1... | collective-permute-start | bytes 884744 | tf_op jit(solution)/shard_map/ppermute | solution.py:389
  19.1 0.6 shard_map.119.params_ref
  19.7 0.6 collective-permute-done.1
  20.3 0.1 maximum_select_fusion.refs_0_
  20.4 0.0 copy-start.1
  20.4 18.4 %all-to-all-done.in_ref = bf16[16,9,8,384]{3,2,1,0:T(8,128)(2,1)S(1)} async-done(((bf16[16,9,8,384]{3,2,1,0:T(8,128)(2,1)}), bf16[16,9,8,384]{3,2,1,0:T(8,128)(2,1)S(1)}, u32[]{:S(2)}, u32[]{:S(2)}) %all-to-all-start) | async-done | bytes 884768 | tf_op jit(solution)/shard_map/all_to_all | solution.py:380
  38.8 4.8 %shard_map.120 = bf16[16,112,128]{2,1,0:T(8,128)(2,1)} custom-call(f32[35,8,128]{2,1,0:T(8,128)S(1)} %shard_map.119.params_ref, bf16[16,9,8,384]{3,2,1,0:T(8,128)(2,1)S(1)} %all-to-all-done.in_ref, bf16[768,1152]{1,0:T(8,128)(2,1)} %w_any.2), custom_call_target="tpu_custom_call" | custom-call | flops 1019215872 | bytes 3256320 | tf_op jit(solution)/shard_map/pallas_call | solution.py:361
  43.6 1.7 %collective-permute-done.window_any = bf16[576,768]{1,0:T(8,128)(2,1)} collective-permute-done((bf16[576,768]{1,0:T(8,128)(2,1)S(1)}, bf16[576,768]{1,0:T(8,128)(2,1)}, u32[]{:S(2)}, u32[]{:S(2)}) %collective-permute-start) | collective-permute-done | bytes 884768 | tf_op jit(solution)/shard_map/ppermute | solution.py:385
  45.3 5.8 %all-to-all-start.1 = ((bf16[16,112,128]{2,1,0:T(8,128)(2,1)}), bf16[16,112,128]{2,1,0:T(8,128)(2,1)S(1)}, u32[]{:S(2)}, u32[]{:S(2)}) async-start(bf16[16,112,128]{2,1,0:T(8,128)(2,1)} %shard_map.120), calls=%async_computation.1 | async-start | bytes 917504 | tf_op jit(solution)/shard_map/all_to_all | solution.py:380
  51.1 16.0 %all-to-all-done.1.mixed_ref = bf16[16,112,128]{2,1,0:T(8,128)(2,1)S(1)} async-done(((bf16[16,112,128]{2,1,0:T(8,128)(2,1)}), bf16[16,112,128]{2,1,0:T(8,128)(2,1)S(1)}, u32[]{:S(2)}, u32[]{:S(2)}) %all-to-all-start.1) | async-done | bytes 458784 | tf_op jit(solution)/shard_map/all_to_all | solution.py:380
  67.1 4.6 %shard_map.121 = (bf16[2,576,768]{2,1,0:T(8,128)(2,1)}, bf16[32,112,128]{2,1,0:T(8,128)(2,1)}) custom-call(s32[1]{0:T(128)} %bitcast.frame_ref, f32[35,8,128]{2,1,0:T(8,128)S(1)} %shard_map.119.params_ref, bf16[16,112,128]{2,1,0:T(8,128)(2,1)S(1)} %all-to-all-done.1.mixed_ref, bf16[576,768]{1,0:T(8,128)(2,1)} %collective-permute-done.window_any, ...), custom_call_target="tpu_custom_call" | custom-call | flops 1019215872 | bytes 7122948 | tf_op jit(solution)/shard_map/pallas_call | solution.py:361
  71.7 0.0 copy-start.7
  71.7 9.8 %all-to-all-start.2 = ((bf16[32,112,128]{2,1,0:T(8,128)(2,1)}), bf16[32,112,128]{2,1,0:T(8,128)(2,1)S(1)}, u32[]{:S(2)}, u32[]{:S(2)}) async-start(bf16[32,112,128]{2,1,0:T(8,128)(2,1)} %get-tuple-element.30), calls=%async_computation.2 | async-start | bytes 1835008 | tf_op jit(solution)/shard_map/all_to_all | solution.py:380
  81.5 1.9 %collective-permute-start.3 = (bf16[2,192,768]{2,1,0:T(8,128)(2,1)S(1)}, bf16[2,192,768]{2,1,0:T(8,128)(2,1)}, u32[]{:S(2)}, u32[]{:S(2)}) collective-permute-start(bf16[2,192,768]{2,1,0:T(8,128)(2,1)S(1)} %maximum_select_fusion.refs_0_), channel_id=1, source_target_pairs={{0,64},{32,480},{64,128},{96,32},{128,192},{160,96},{192,256},{224... | collective-permute-start | bytes 1769480 | tf_op jit(solution)/shard_map/ppermute | solution.py:394
  83.5 2.4 %collective-permute-start.2 = (bf16[2,192,768]{2,1,0:T(8,128)(2,1)S(1)}, bf16[2,192,768]{2,1,0:T(8,128)(2,1)}, u32[]{:S(2)}, u32[]{:S(2)}) collective-permute-start(bf16[2,192,768]{2,1,0:T(8,128)(2,1)S(1)} %maximum_select_fusion.refs_0_), channel_id=1, source_target_pairs={{0,128},{32,416},{64,192},{96,480},{128,256},{160,32},{192,320},{2... | collective-permute-start | bytes 1769480 | tf_op jit(solution)/shard_map/ppermute | solution.py:394
  85.9 7.9 %collective-permute-done.3.refs_1_ = bf16[2,192,768]{2,1,0:T(8,128)(2,1)} collective-permute-done((bf16[2,192,768]{2,1,0:T(8,128)(2,1)S(1)}, bf16[2,192,768]{2,1,0:T(8,128)(2,1)}, u32[]{:S(2)}, u32[]{:S(2)}) %collective-permute-start.3) | collective-permute-done | bytes 589856 | tf_op jit(solution)/shard_map/ppermute | solution.py:394
  93.8 4.7 %collective-permute-start.4 = (bf16[2,192,768]{2,1,0:T(8,128)(2,1)}, bf16[2,192,768]{2,1,0:T(8,128)(2,1)}, u32[]{:S(2)}, u32[]{:S(2)}) collective-permute-start(bf16[2,192,768]{2,1,0:T(8,128)(2,1)} %collective-permute-done.3.refs_1_), channel_id=1, source_target_pairs={{0,32},{32,0},{64,96},{96,64},{128,160},{160,128},{192,224},{224,1... | collective-permute-start | bytes 1769480 | tf_op jit(solution)/shard_map/ppermute | solution.py:389
  98.5 0.0 copy-done.7
  98.5 1.3 convolution_convert_fusion
  99.8 0.6 copy.14.up_ref
  100.4 1.6 %convolution_convert_fusion.1 = bf16[3,96,2,768]{3,1,2,0:T(8,128)(2,1)S(1)} fusion(bf16[3,2,96,768]{3,2,1,0:T(8,128)(2,1)} %constant.40.clone, bf16[2,96,96,96]{3,2,1,0:T(8,128)(2,1)} %constant.39.clone, s32[]{:T(128)S(6)} %select_n.31), kind=kOutput, calls=%fused_computation.1 | convolution fusion | flops 85377024 | bytes 1843204 | tf_op jit(solution)/shard_map/ilj,icjn->icln/dot_general | solution.py:436
  102.0 1.0 pad_maximum_fusion.down_ref
  103.0 0.7 collective-permute-done.2.refs_3_
  103.7 0.0 collective-permute-done.4.refs_2_
  103.7 3.0 %all-to-all-done.2.in_ref = bf16[32,112,128]{2,1,0:T(8,128)(2,1)S(1)} async-done(((bf16[32,112,128]{2,1,0:T(8,128)(2,1)}), bf16[32,112,128]{2,1,0:T(8,128)(2,1)S(1)}, u32[]{:S(2)}, u32[]{:S(2)}) %all-to-all-start.2) | async-done | bytes 917536 | tf_op jit(solution)/shard_map/all_to_all | solution.py:380
  106.7 2.0 %shard_map.122 = bf16[32,112,128]{2,1,0:T(8,128)(2,1)S(1)} custom-call(bf16[32,112,128]{2,1,0:T(8,128)(2,1)S(1)} %all-to-all-done.2.in_ref, bf16[672,768]{1,0:T(8,128)(2,1)S(1)} %pad_maximum_fusion.down_ref, bf16[768,576]{1,0:T(8,128)(2,1)S(1)} %copy.14.up_ref), custom_call_target="tpu_custom_call" | custom-call | flops 1358954496 | bytes 3751936 | tf_op jit(solution)/shard_map/pallas_call | solution.py:361
  108.7 0.9 copy-done
  109.6 6.4 %all-to-all-start.3 = ((bf16[32,112,128]{2,1,0:T(8,128)(2,1)}), bf16[32,112,128]{2,1,0:T(8,128)(2,1)}, u32[]{:S(2)}, u32[]{:S(2)}) async-start(bf16[32,112,128]{2,1,0:T(8,128)(2,1)} %copy-done), calls=%async_computation.3 | async-start | bytes 1835008 | tf_op jit(solution)/shard_map/all_to_all | solution.py:380
  116.0 5.7 %collective-permute-start.5 = (bf16[2,192,768]{2,1,0:T(8,128)(2,1)}, bf16[2,192,768]{2,1,0:T(8,128)(2,1)S(1)}, u32[]{:S(2)}, u32[]{:S(2)}) collective-permute-start(bf16[2,192,768]{2,1,0:T(8,128)(2,1)} %collective-permute-done.2.refs_3_), channel_id=1, source_target_pairs={{0,64},{32,480},{64,128},{96,32},{128,192},{160,96},{192,256},{224... | collective-permute-start | bytes 1769480 | tf_op jit(solution)/shard_map/ppermute | solution.py:394
  121.7 3.0 %collective-permute-start.6 = (bf16[2,192,768]{2,1,0:T(8,128)(2,1)}, bf16[2,192,768]{2,1,0:T(8,128)(2,1)S(1)}, u32[]{:S(2)}, u32[]{:S(2)}) collective-permute-start(bf16[2,192,768]{2,1,0:T(8,128)(2,1)} %collective-permute-done.2.refs_3_), channel_id=1, source_target_pairs={{0,32},{32,0},{64,96},{96,64},{128,160},{160,128},{192,224},{224,1... | collective-permute-start | bytes 1769480 | tf_op jit(solution)/shard_map/ppermute | solution.py:389
  124.7 1.1 slice_select_fusion
  125.8 2.2 %collective-permute-start.8 = (bf16[1,192,768]{2,1,0:T(8,128)(2,1)S(1)}, bf16[1,192,768]{2,1,0:T(8,128)(2,1)S(1)}, u32[]{:S(2)}, u32[]{:S(2)}) collective-permute-start(bf16[1,192,768]{2,1,0:T(8,128)(2,1)S(1)} %slice_select_fusion), channel_id=1, source_target_pairs={{0,128},{32,416},{64,192},{96,480},{128,256},{160,32},{192,320},{2... | collective-permute-start | bytes 884744 | tf_op jit(solution)/shard_map/ppermute | solution.py:394
  128.0 4.0 %collective-permute-done.5.refs_4_ = bf16[2,192,768]{2,1,0:T(8,128)(2,1)S(1)} collective-permute-done((bf16[2,192,768]{2,1,0:T(8,128)(2,1)}, bf16[2,192,768]{2,1,0:T(8,128)(2,1)S(1)}, u32[]{:S(2)}, u32[]{:S(2)}) %collective-permute-start.5) | collective-permute-done | bytes 589856 | tf_op jit(solution)/shard_map/ppermute | solution.py:394
  132.0 1.9 %collective-permute-start.7 = (bf16[2,192,768]{2,1,0:T(8,128)(2,1)S(1)}, bf16[2,192,768]{2,1,0:T(8,128)(2,1)S(1)}, u32[]{:S(2)}, u32[]{:S(2)}) collective-permute-start(bf16[2,192,768]{2,1,0:T(8,128)(2,1)S(1)} %collective-permute-done.5.refs_4_), channel_id=1, source_target_pairs={{0,32},{32,0},{64,96},{96,64},{128,160},{160,128},{192,224},{224,1... | collective-permute-start | bytes 1769480 | tf_op jit(solution)/shard_map/ppermute | solution.py:389
  133.9 3.3 %collective-permute-done.8.refs_7_ = bf16[1,192,768]{2,1,0:T(8,128)(2,1)S(1)} collective-permute-done((bf16[1,192,768]{2,1,0:T(8,128)(2,1)S(1)}, bf16[1,192,768]{2,1,0:T(8,128)(2,1)S(1)}, u32[]{:S(2)}, u32[]{:S(2)}) %collective-permute-start.8) | collective-permute-done | bytes 294944 | tf_op jit(solution)/shard_map/ppermute | solution.py:394
  137.2 3.2 %collective-permute-start.9 = (bf16[1,192,768]{2,1,0:T(8,128)(2,1)S(1)}, bf16[1,192,768]{2,1,0:T(8,128)(2,1)S(1)}, u32[]{:S(2)}, u32[]{:S(2)}) collective-permute-start(bf16[1,192,768]{2,1,0:T(8,128)(2,1)S(1)} %collective-permute-done.8.refs_7_), channel_id=1, source_target_pairs={{0,32},{32,0},{64,96},{96,64},{128,160},{160,128},{192,224},{224,1... | collective-permute-start | bytes 884744 | tf_op jit(solution)/shard_map/ppermute | solution.py:389
  140.4 0.0 collective-permute-done.6.refs_5_
  140.4 1.0 collective-permute-done.9.refs_8_
  141.4 0.0 collective-permute-done.7.refs_6_
  141.4 0.0 all-to-all-done.3.in_any
  141.5 8.0 %shard_map.123 = bf16[576,768]{1,0:T(8,128)(2,1)} custom-call(s32[1]{0:T(128)} %bitcast.frame_ref, f32[35,8,128]{2,1,0:T(8,128)S(1)} %copy-done.3, bf16[32,112,128]{2,1,0:T(8,128)(2,1)} %all-to-all-done.3.in_any, bf16[2,768,768]{2,1,0:T(8,128)(2,1)} %constant.38.clone.tables_any, bf16[2,576,768]{2,1,0:T(8,128)(2,1)} %get-tuple-element.36.carry_any, ...), custom_call_target="tpu_custom_call" | custom-call | flops 3397386240 | bytes 10792964 | tf_op jit(solution)/shard_map/pallas_call | solution.py:361
  (15 shorter events, 0.0 us)
Async XLA Ops:
  0.0 14.1 %copy-start.8 = (bf16[1,3,192,768]{3,2,1,0:T(8,128)(2,1)S(1)}, bf16[1,3,192,768]{3,2,1,0:T(8,128)(2,1)}, u32[]{:S(2)}) copy-start(bf16[1,3,192,768]{3,2,1,0:T(8,128)(2,1)} %param.12) | copy-start | bytes 2654212
  0.0 14.3 %copy-start.9 = (bf16[96,768]{1,0:T(8,128)(2,1)S(1)}, bf16[96,768]{1,0:T(8,128)(2,1)}, u32[]{:S(2)}) copy-start(bf16[96,768]{1,0:T(8,128)(2,1)} %param.20) | copy-start | bytes 442372
  0.0 14.3 %copy-start.10 = (bf16[96,768]{1,0:T(8,128)(2,1)S(1)}, bf16[96,768]{1,0:T(8,128)(2,1)}, u32[]{:S(2)}) copy-start(bf16[96,768]{1,0:T(8,128)(2,1)} %param.19) | copy-start | bytes 442372
  0.0 19.1 %copy-start.4 = (f32[3,768]{1,0:T(4,128)S(1)}, f32[3,768]{1,0:T(4,128)}, u32[]{:S(2)}) copy-start(f32[3,768]{1,0:T(4,128)} %gains_ref) | copy-start | bytes 27652
  0.0 19.1 %copy-start.5 = (f32[16]{0:T(128)S(1)}, f32[16]{0:T(128)}, u32[]{:S(2)}) copy-start(f32[16]{0:T(128)} %noise_ref.1) | copy-start | bytes 196
  0.0 19.1 %copy-start.6 = (f32[16]{0:T(128)S(1)}, f32[16]{0:T(128)}, u32[]{:S(2)}) copy-start(f32[16]{0:T(128)} %keep_ref.1) | copy-start | bytes 196
  2.3 36.5 %all-to-all-start = ((bf16[16,9,8,384]{3,2,1,0:T(8,128)(2,1)}), bf16[16,9,8,384]{3,2,1,0:T(8,128)(2,1)S(1)}, u32[]{:S(2)}, u32[]{:S(2)}) async-start(bf16[16,9,8,384]{3,2,1,0:T(8,128)(2,1)} %shard_map.118), calls=%async_computation | async-start | bytes 1769472 | tf_op jit(solution)/shard_map/all_to_all | solution.py:380
  14.1 31.1 %collective-permute-start = (bf16[576,768]{1,0:T(8,128)(2,1)S(1)}, bf16[576,768]{1,0:T(8,128)(2,1)}, u32[]{:S(2)}, u32[]{:S(2)}) collective-permute-start(bf16[576,768]{1,0:T(8,128)(2,1)S(1)} %bitcast.29), channel_id=1, source_target_pairs={{0,480},{32,0},{64,32},{96,64},{128,96},{160,128},{192,160},{224,1... | collective-permute-start | bytes 2654216 | tf_op jit(solution)/shard_map/ppermute | solution.py:385
  14.3 6.0 %collective-permute-start.1 = (bf16[1,192,768]{2,1,0:T(8,128)(2,1)S(1)}, bf16[1,192,768]{2,1,0:T(8,128)(2,1)S(1)}, u32[]{:S(2)}, u32[]{:S(2)}) collective-permute-start(bf16[1,192,768]{2,1,0:T(8,128)(2,1)S(1)} %maximum_bitcast_fusion), channel_id=1, source_target_pairs={{0,32},{32,0},{64,96},{96,64},{128,160},{160,128},{192,224},{224,1... | collective-permute-start | bytes 884744 | tf_op jit(solution)/shard_map/ppermute | solution.py:389
  19.7 47.4 %copy-start.2 = (f32[35,8,128]{2,1,0:T(8,128)}, f32[35,8,128]{2,1,0:T(8,128)S(1)}, u32[]{:S(2)}) copy-start(f32[35,8,128]{2,1,0:T(8,128)S(1)} %shard_map.119.params_ref) | copy-start | bytes 430084
  20.4 46.7 %copy-start.1 = (bf16[384,768]{1,0:T(8,128)(2,1)S(1)}, bf16[384,768]{1,0:T(8,128)(2,1)}, u32[]{:S(2)}) copy-start(bf16[384,768]{1,0:T(8,128)(2,1)} %w_any.3) | copy-start | bytes 1769476
  45.3 21.8 %all-to-all-start.1 = ((bf16[16,112,128]{2,1,0:T(8,128)(2,1)}), bf16[16,112,128]{2,1,0:T(8,128)(2,1)S(1)}, u32[]{:S(2)}, u32[]{:S(2)}) async-start(bf16[16,112,128]{2,1,0:T(8,128)(2,1)} %shard_map.120), calls=%async_computation.1 | async-start | bytes 917504 | tf_op jit(solution)/shard_map/all_to_all | solution.py:380
  71.7 26.8 %copy-start.7 = (bf16[3,2,96,768]{3,2,1,0:T(8,128)(2,1)S(1)}, bf16[3,2,96,768]{3,2,1,0:T(8,128)(2,1)}, u32[]{:S(2)}) copy-start(bf16[3,2,96,768]{3,2,1,0:T(8,128)(2,1)} %constant.40.clone) | copy-start | bytes 2654212
  71.7 35.0 %all-to-all-start.2 = ((bf16[32,112,128]{2,1,0:T(8,128)(2,1)}), bf16[32,112,128]{2,1,0:T(8,128)(2,1)S(1)}, u32[]{:S(2)}, u32[]{:S(2)}) async-start(bf16[32,112,128]{2,1,0:T(8,128)(2,1)} %get-tuple-element.30), calls=%async_computation.2 | async-start | bytes 1835008 | tf_op jit(solution)/shard_map/all_to_all | solution.py:380
  81.5 12.3 %collective-permute-start.3 = (bf16[2,192,768]{2,1,0:T(8,128)(2,1)S(1)}, bf16[2,192,768]{2,1,0:T(8,128)(2,1)}, u32[]{:S(2)}, u32[]{:S(2)}) collective-permute-start(bf16[2,192,768]{2,1,0:T(8,128)(2,1)S(1)} %maximum_select_fusion.refs_0_), channel_id=1, source_target_pairs={{0,64},{32,480},{64,128},{96,32},{128,192},{160,96},{192,256},{224... | collective-permute-start | bytes 1769480 | tf_op jit(solution)/shard_map/ppermute | solution.py:394
  83.5 20.3 %collective-permute-start.2 = (bf16[2,192,768]{2,1,0:T(8,128)(2,1)S(1)}, bf16[2,192,768]{2,1,0:T(8,128)(2,1)}, u32[]{:S(2)}, u32[]{:S(2)}) collective-permute-start(bf16[2,192,768]{2,1,0:T(8,128)(2,1)S(1)} %maximum_select_fusion.refs_0_), channel_id=1, source_target_pairs={{0,128},{32,416},{64,192},{96,480},{128,256},{160,32},{192,320},{2... | collective-permute-start | bytes 1769480 | tf_op jit(solution)/shard_map/ppermute | solution.py:394
  93.8 9.9 %collective-permute-start.4 = (bf16[2,192,768]{2,1,0:T(8,128)(2,1)}, bf16[2,192,768]{2,1,0:T(8,128)(2,1)}, u32[]{:S(2)}, u32[]{:S(2)}) collective-permute-start(bf16[2,192,768]{2,1,0:T(8,128)(2,1)} %collective-permute-done.3.refs_1_), channel_id=1, source_target_pairs={{0,32},{32,0},{64,96},{96,64},{128,160},{160,128},{192,224},{224,1... | collective-permute-start | bytes 1769480 | tf_op jit(solution)/shard_map/ppermute | solution.py:389
  108.7 0.9 copy-start
  109.6 31.8 %copy-start.3 = (f32[35,8,128]{2,1,0:T(8,128)S(1)}, f32[35,8,128]{2,1,0:T(8,128)}, u32[]{:S(2)}) copy-start(f32[35,8,128]{2,1,0:T(8,128)} %copy-done.2) | copy-start | bytes 430084
  109.6 31.8 %all-to-all-start.3 = ((bf16[32,112,128]{2,1,0:T(8,128)(2,1)}), bf16[32,112,128]{2,1,0:T(8,128)(2,1)}, u32[]{:S(2)}, u32[]{:S(2)}) async-start(bf16[32,112,128]{2,1,0:T(8,128)(2,1)} %copy-done), calls=%async_computation.3 | async-start | bytes 1835008 | tf_op jit(solution)/shard_map/all_to_all | solution.py:380
  116.0 16.0 %collective-permute-start.5 = (bf16[2,192,768]{2,1,0:T(8,128)(2,1)}, bf16[2,192,768]{2,1,0:T(8,128)(2,1)S(1)}, u32[]{:S(2)}, u32[]{:S(2)}) collective-permute-start(bf16[2,192,768]{2,1,0:T(8,128)(2,1)} %collective-permute-done.2.refs_3_), channel_id=1, source_target_pairs={{0,64},{32,480},{64,128},{96,32},{128,192},{160,96},{192,256},{224... | collective-permute-start | bytes 1769480 | tf_op jit(solution)/shard_map/ppermute | solution.py:394
  121.7 18.7 %collective-permute-start.6 = (bf16[2,192,768]{2,1,0:T(8,128)(2,1)}, bf16[2,192,768]{2,1,0:T(8,128)(2,1)S(1)}, u32[]{:S(2)}, u32[]{:S(2)}) collective-permute-start(bf16[2,192,768]{2,1,0:T(8,128)(2,1)} %collective-permute-done.2.refs_3_), channel_id=1, source_target_pairs={{0,32},{32,0},{64,96},{96,64},{128,160},{160,128},{192,224},{224,1... | collective-permute-start | bytes 1769480 | tf_op jit(solution)/shard_map/ppermute | solution.py:389
  125.8 11.4 %collective-permute-start.8 = (bf16[1,192,768]{2,1,0:T(8,128)(2,1)S(1)}, bf16[1,192,768]{2,1,0:T(8,128)(2,1)S(1)}, u32[]{:S(2)}, u32[]{:S(2)}) collective-permute-start(bf16[1,192,768]{2,1,0:T(8,128)(2,1)S(1)} %slice_select_fusion), channel_id=1, source_target_pairs={{0,128},{32,416},{64,192},{96,480},{128,256},{160,32},{192,320},{2... | collective-permute-start | bytes 884744 | tf_op jit(solution)/shard_map/ppermute | solution.py:394
  132.0 9.4 %collective-permute-start.7 = (bf16[2,192,768]{2,1,0:T(8,128)(2,1)S(1)}, bf16[2,192,768]{2,1,0:T(8,128)(2,1)S(1)}, u32[]{:S(2)}, u32[]{:S(2)}) collective-permute-start(bf16[2,192,768]{2,1,0:T(8,128)(2,1)S(1)} %collective-permute-done.5.refs_4_), channel_id=1, source_target_pairs={{0,32},{32,0},{64,96},{96,64},{128,160},{160,128},{192,224},{224,1... | collective-permute-start | bytes 1769480 | tf_op jit(solution)/shard_map/ppermute | solution.py:389
  137.2 4.2 %collective-permute-start.9 = (bf16[1,192,768]{2,1,0:T(8,128)(2,1)S(1)}, bf16[1,192,768]{2,1,0:T(8,128)(2,1)S(1)}, u32[]{:S(2)}, u32[]{:S(2)}) collective-permute-start(bf16[1,192,768]{2,1,0:T(8,128)(2,1)S(1)} %collective-permute-done.8.refs_7_), channel_id=1, source_target_pairs={{0,32},{32,0},{64,96},{96,64},{128,160},{160,128},{192,224},{224,1... | collective-permute-start | bytes 884744 | tf_op jit(solution)/shard_map/ppermute | solution.py:389

commit v5 on v4

--- a/solution.py
+++ b/solution.py
@@ -428,10 +428,7 @@
         4,
     )
     own = jnp.concatenate([w_in, w_down], 0)[None]
-    other = swap_cores(own)
-    pair = jnp.where(
-        lead % 2 == 0, jnp.concatenate([own, other], 0), jnp.concatenate([other, own], 0)
-    )
+    pair = jnp.concatenate([own, swap_cores(own)], 0)
     local = lax.dynamic_slice_in_dim(legendre, ORDERS * lat, ORDERS, 1)
     down = jnp.einsum("ilj,icjn->icln", local[0], placement, preferred_element_type=F32)
     down = down.astype(BF16).reshape(2 * ORDERS * LMAX, 768)
@@ -486,7 +483,7 @@
     )
     back, second_pair = lax.optimization_barrier((back, second_pair))
     third_pair = round_chips(second_pair, 1)
-    last = round_chips(jnp.where(lead % 2 == 0, second_pair[0:1], second_pair[1:2]), 2)
+    last = round_chips(second_pair[0:1], 2)
     shards += [third_pair, swap_cores(second_pair), swap_cores(third_pair), last, swap_cores(last)]
     (stepped,) = call(
         feed_forward,

time: 151 us -> 151 us (level)
  no operation moved by 1% of the time
where the time goes in v5:
time: 151 us; the launch traced here: 150 us
  starting transfers between devices  64 us (42%)
  waiting for transfers between devices  56.5 us (37%)
  Pallas kernels  22.2 us (15%)
  matrix products  2.87 us (2%)
  local copies, waits for them, and re-layouts  2.59 us (2%)
    all_to_all x4, waiting for transfers between devices, exchange(): return lax.all_to_all(chunks, axis, split_axis=0, concat_axis=0, tiled=True)  37.4 us
    all_to_all x4, starting transfers between devices, exchange(): return lax.all_to_all(chunks, axis, split_axis=0, concat_axis=0, tiled=True)  33.9 us
    pallas_call x6, Pallas kernels, call(): pl.pallas_call(kernel, out_shape=outs, in_specs=specs[:len(args)], out_sp...  22.2 us
    ppermute x5, starting transfers between devices, swap_cores(): lax.ppermute(value, 'lead', [(source, source ^ 1) for source in range(FRA...  17.8 us
    ppermute x4, waiting for transfers between devices, round_chips(): return lax.ppermute(value, 'lead', hops)  15.9 us
    ppermute x4, starting transfers between devices, round_chips(): return lax.ppermute(value, 'lead', hops)  12.2 us
  transfers between devices with their start and end apart: 14, of which 10 were waited for; matrix products, arithmetic and copies ran while one was open for 4% of the time, Pallas kernels for 4%

profile of v5, /device:TPU:1, one launch (start us, length us, event | category | flops | bytes accessed | tf_op | source)
XLA Modules:
  0.0 149.6 jit_solution(10891727652094174374)
XLA Ops:
  0.0 2.3 %shard_map.118 = bf16[16,9,8,384]{3,2,1,0:T(8,128)(2,1)} custom-call(bf16[18,4,8,768]{3,2,1,0:T(8,128)(2,1)} %bitcast.28), custom_call_target="tpu_custom_call" | custom-call | bytes 1769472 | tf_op jit(solution)/shard_map/pallas_call | solution.py:361
  2.3 11.8 %all-to-all-start = ((bf16[16,9,8,384]{3,2,1,0:T(8,128)(2,1)}), bf16[16,9,8,384]{3,2,1,0:T(8,128)(2,1)S(1)}, u32[]{:S(2)}, u32[]{:S(2)}) async-start(bf16[16,9,8,384]{3,2,1,0:T(8,128)(2,1)} %shard_map.118), calls=%async_computation | async-start | bytes 1769472 | tf_op jit(solution)/shard_map/all_to_all | solution.py:380
  14.1 0.1 collective-permute-start
  14.3 4.8 %collective-permute-start.1 = (bf16[1,192,768]{2,1,0:T(8,128)(2,1)S(1)}, bf16[1,192,768]{2,1,0:T(8,128)(2,1)S(1)}, u32[]{:S(2)}, u32[]{:S(2)}) collective-permute-start(bf16[1,192,768]{2,1,0:T(8,128)(2,1)S(1)} %maximum_bitcast_fusion), channel_id=1, source_target_pairs={{0,32},{32,0},{64,96},{96,64},{128,160},{160,128},{192,224},{224,1... | collective-permute-start | bytes 884744 | tf_op jit(solution)/shard_map/ppermute | solution.py:389
  19.1 0.0 copy-done.4
  19.1 0.0 copy-done.5
  19.1 0.0 copy-done.6
  19.1 0.6 shard_map.119.params_ref
  19.7 0.6 collective-permute-done.1
  20.3 0.1 pad_maximum_fusion.1.refs_0_
  20.3 0.0 copy-start.1
  20.4 18.4 %all-to-all-done.in_ref = bf16[16,9,8,384]{3,2,1,0:T(8,128)(2,1)S(1)} async-done(((bf16[16,9,8,384]{3,2,1,0:T(8,128)(2,1)}), bf16[16,9,8,384]{3,2,1,0:T(8,128)(2,1)S(1)}, u32[]{:S(2)}, u32[]{:S(2)}) %all-to-all-start) | async-done | bytes 884768 | tf_op jit(solution)/shard_map/all_to_all | solution.py:380
  38.8 4.8 %shard_map.120 = bf16[16,112,128]{2,1,0:T(8,128)(2,1)} custom-call(f32[35,8,128]{2,1,0:T(8,128)S(1)} %shard_map.119.params_ref, bf16[16,9,8,384]{3,2,1,0:T(8,128)(2,1)S(1)} %all-to-all-done.in_ref, bf16[768,1152]{1,0:T(8,128)(2,1)} %w_any.2), custom_call_target="tpu_custom_call" | custom-call | flops 1019215872 | bytes 3256320 | tf_op jit(solution)/shard_map/pallas_call | solution.py:361
  43.6 1.7 %collective-permute-done.window_any = bf16[576,768]{1,0:T(8,128)(2,1)} collective-permute-done((bf16[576,768]{1,0:T(8,128)(2,1)S(1)}, bf16[576,768]{1,0:T(8,128)(2,1)}, u32[]{:S(2)}, u32[]{:S(2)}) %collective-permute-start) | collective-permute-done | bytes 884768 | tf_op jit(solution)/shard_map/ppermute | solution.py:385
  45.3 5.8 %all-to-all-start.1 = ((bf16[16,112,128]{2,1,0:T(8,128)(2,1)}), bf16[16,112,128]{2,1,0:T(8,128)(2,1)S(1)}, u32[]{:S(2)}, u32[]{:S(2)}) async-start(bf16[16,112,128]{2,1,0:T(8,128)(2,1)} %shard_map.120), calls=%async_computation.1 | async-start | bytes 917504 | tf_op jit(solution)/shard_map/all_to_all | solution.py:380
  51.1 16.0 %all-to-all-done.1.mixed_ref = bf16[16,112,128]{2,1,0:T(8,128)(2,1)S(1)} async-done(((bf16[16,112,128]{2,1,0:T(8,128)(2,1)}), bf16[16,112,128]{2,1,0:T(8,128)(2,1)S(1)}, u32[]{:S(2)}, u32[]{:S(2)}) %all-to-all-start.1) | async-done | bytes 458784 | tf_op jit(solution)/shard_map/all_to_all | solution.py:380
  67.1 0.0 copy-done.2
  67.1 4.6 %shard_map.121 = (bf16[2,576,768]{2,1,0:T(8,128)(2,1)}, bf16[32,112,128]{2,1,0:T(8,128)(2,1)}) custom-call(s32[1]{0:T(128)} %bitcast.frame_ref, f32[35,8,128]{2,1,0:T(8,128)S(1)} %shard_map.119.params_ref, bf16[16,112,128]{2,1,0:T(8,128)(2,1)S(1)} %all-to-all-done.1.mixed_ref, bf16[576,768]{1,0:T(8,128)(2,1)} %collective-permute-done.window_any, ...), custom_call_target="tpu_custom_call" | custom-call | flops 1019215872 | bytes 7122948 | tf_op jit(solution)/shard_map/pallas_call | solution.py:361
  71.7 0.0 copy-start.7
  71.7 9.8 %all-to-all-start.2 = ((bf16[32,112,128]{2,1,0:T(8,128)(2,1)}), bf16[32,112,128]{2,1,0:T(8,128)(2,1)S(1)}, u32[]{:S(2)}, u32[]{:S(2)}) async-start(bf16[32,112,128]{2,1,0:T(8,128)(2,1)} %get-tuple-element.30), calls=%async_computation.2 | async-start | bytes 1835008 | tf_op jit(solution)/shard_map/all_to_all | solution.py:380
  81.5 1.9 %collective-permute-start.3 = (bf16[2,192,768]{2,1,0:T(8,128)(2,1)S(1)}, bf16[2,192,768]{2,1,0:T(8,128)(2,1)}, u32[]{:S(2)}, u32[]{:S(2)}) collective-permute-start(bf16[2,192,768]{2,1,0:T(8,128)(2,1)S(1)} %pad_maximum_fusion.1.refs_0_), channel_id=1, source_target_pairs={{0,64},{32,480},{64,128},{96,32},{128,192},{160,96},{192,256},{224... | collective-permute-start | bytes 1769480 | tf_op jit(solution)/shard_map/ppermute | solution.py:394
  83.5 2.4 %collective-permute-start.2 = (bf16[2,192,768]{2,1,0:T(8,128)(2,1)S(1)}, bf16[2,192,768]{2,1,0:T(8,128)(2,1)}, u32[]{:S(2)}, u32[]{:S(2)}) collective-permute-start(bf16[2,192,768]{2,1,0:T(8,128)(2,1)S(1)} %pad_maximum_fusion.1.refs_0_), channel_id=1, source_target_pairs={{0,128},{32,416},{64,192},{96,480},{128,256},{160,32},{192,320},{2... | collective-permute-start | bytes 1769480 | tf_op jit(solution)/shard_map/ppermute | solution.py:394
  85.9 7.9 %collective-permute-done.3.refs_1_ = bf16[2,192,768]{2,1,0:T(8,128)(2,1)} collective-permute-done((bf16[2,192,768]{2,1,0:T(8,128)(2,1)S(1)}, bf16[2,192,768]{2,1,0:T(8,128)(2,1)}, u32[]{:S(2)}, u32[]{:S(2)}) %collective-permute-start.3) | collective-permute-done | bytes 589856 | tf_op jit(solution)/shard_map/ppermute | solution.py:394
  93.8 4.7 %collective-permute-start.4 = (bf16[2,192,768]{2,1,0:T(8,128)(2,1)}, bf16[2,192,768]{2,1,0:T(8,128)(2,1)}, u32[]{:S(2)}, u32[]{:S(2)}) collective-permute-start(bf16[2,192,768]{2,1,0:T(8,128)(2,1)} %collective-permute-done.3.refs_1_), channel_id=1, source_target_pairs={{0,32},{32,0},{64,96},{96,64},{128,160},{160,128},{192,224},{224,1... | collective-permute-start | bytes 1769480 | tf_op jit(solution)/shard_map/ppermute | solution.py:389
  98.5 1.3 convolution_convert_fusion
  99.8 0.6 copy.14.up_ref
  100.4 1.6 %convolution_convert_fusion.1 = bf16[3,96,2,768]{3,1,2,0:T(8,128)(2,1)S(1)} fusion(bf16[3,2,96,768]{3,2,1,0:T(8,128)(2,1)} %constant.27.clone, bf16[2,96,96,96]{3,2,1,0:T(8,128)(2,1)} %constant.26.clone, s32[]{:T(128)S(6)} %select_n.3), kind=kOutput, calls=%fused_computation.1 | convolution fusion | flops 85377024 | bytes 1843204 | tf_op jit(solution)/shard_map/ilj,icjn->icln/dot_general | solution.py:433
  102.0 1.0 pad_maximum_fusion.down_ref
  103.0 0.7 collective-permute-done.2.refs_3_
  103.7 0.0 collective-permute-done.4.refs_2_
  103.7 3.0 %all-to-all-done.2.in_ref = bf16[32,112,128]{2,1,0:T(8,128)(2,1)S(1)} async-done(((bf16[32,112,128]{2,1,0:T(8,128)(2,1)}), bf16[32,112,128]{2,1,0:T(8,128)(2,1)S(1)}, u32[]{:S(2)}, u32[]{:S(2)}) %all-to-all-start.2) | async-done | bytes 917536 | tf_op jit(solution)/shard_map/all_to_all | solution.py:380
  106.7 2.0 %shard_map.122 = bf16[32,112,128]{2,1,0:T(8,128)(2,1)S(1)} custom-call(bf16[32,112,128]{2,1,0:T(8,128)(2,1)S(1)} %all-to-all-done.2.in_ref, bf16[672,768]{1,0:T(8,128)(2,1)S(1)} %pad_maximum_fusion.down_ref, bf16[768,576]{1,0:T(8,128)(2,1)S(1)} %copy.14.up_ref), custom_call_target="tpu_custom_call" | custom-call | flops 1358954496 | bytes 3751936 | tf_op jit(solution)/shard_map/pallas_call | solution.py:361
  108.7 0.0 copy-start
  108.7 0.9 copy-done
  109.6 6.4 %all-to-all-start.3 = ((bf16[32,112,128]{2,1,0:T(8,128)(2,1)}), bf16[32,112,128]{2,1,0:T(8,128)(2,1)}, u32[]{:S(2)}, u32[]{:S(2)}) async-start(bf16[32,112,128]{2,1,0:T(8,128)(2,1)} %copy-done), calls=%async_computation.3 | async-start | bytes 1835008 | tf_op jit(solution)/shard_map/all_to_all | solution.py:380
  116.0 5.7 %collective-permute-start.5 = (bf16[2,192,768]{2,1,0:T(8,128)(2,1)}, bf16[2,192,768]{2,1,0:T(8,128)(2,1)S(1)}, u32[]{:S(2)}, u32[]{:S(2)}) collective-permute-start(bf16[2,192,768]{2,1,0:T(8,128)(2,1)} %collective-permute-done.2.refs_3_), channel_id=1, source_target_pairs={{0,64},{32,480},{64,128},{96,32},{128,192},{160,96},{192,256},{224... | collective-permute-start | bytes 1769480 | tf_op jit(solution)/shard_map/ppermute | solution.py:394
  121.7 1.0 slice.11
  122.7 3.0 %collective-permute-start.6 = (bf16[2,192,768]{2,1,0:T(8,128)(2,1)}, bf16[2,192,768]{2,1,0:T(8,128)(2,1)S(1)}, u32[]{:S(2)}, u32[]{:S(2)}) collective-permute-start(bf16[2,192,768]{2,1,0:T(8,128)(2,1)} %collective-permute-done.2.refs_3_), channel_id=1, source_target_pairs={{0,32},{32,0},{64,96},{96,64},{128,160},{160,128},{192,224},{224,1... | collective-permute-start | bytes 1769480 | tf_op jit(solution)/shard_map/ppermute | solution.py:389
  125.7 2.2 %collective-permute-start.8 = (bf16[1,192,768]{2,1,0:T(8,128)(2,1)S(1)}, bf16[1,192,768]{2,1,0:T(8,128)(2,1)S(1)}, u32[]{:S(2)}, u32[]{:S(2)}) collective-permute-start(bf16[1,192,768]{2,1,0:T(8,128)(2,1)S(1)} %slice.11), channel_id=1, source_target_pairs={{0,128},{32,416},{64,192},{96,480},{128,256},{160,32},{192,320},{2... | collective-permute-start | bytes 884744 | tf_op jit(solution)/shard_map/ppermute | solution.py:394
  127.9 4.1 %collective-permute-done.5.refs_4_ = bf16[2,192,768]{2,1,0:T(8,128)(2,1)S(1)} collective-permute-done((bf16[2,192,768]{2,1,0:T(8,128)(2,1)}, bf16[2,192,768]{2,1,0:T(8,128)(2,1)S(1)}, u32[]{:S(2)}, u32[]{:S(2)}) %collective-permute-start.5) | collective-permute-done | bytes 589856 | tf_op jit(solution)/shard_map/ppermute | solution.py:394
  132.0 1.9 %collective-permute-start.7 = (bf16[2,192,768]{2,1,0:T(8,128)(2,1)S(1)}, bf16[2,192,768]{2,1,0:T(8,128)(2,1)S(1)}, u32[]{:S(2)}, u32[]{:S(2)}) collective-permute-start(bf16[2,192,768]{2,1,0:T(8,128)(2,1)S(1)} %collective-permute-done.5.refs_4_), channel_id=1, source_target_pairs={{0,32},{32,0},{64,96},{96,64},{128,160},{160,128},{192,224},{224,1... | collective-permute-start | bytes 1769480 | tf_op jit(solution)/shard_map/ppermute | solution.py:389
  133.9 3.2 %collective-permute-done.8.refs_7_ = bf16[1,192,768]{2,1,0:T(8,128)(2,1)S(1)} collective-permute-done((bf16[1,192,768]{2,1,0:T(8,128)(2,1)S(1)}, bf16[1,192,768]{2,1,0:T(8,128)(2,1)S(1)}, u32[]{:S(2)}, u32[]{:S(2)}) %collective-permute-start.8) | collective-permute-done | bytes 294944 | tf_op jit(solution)/shard_map/ppermute | solution.py:394
  137.1 3.3 %collective-permute-start.9 = (bf16[1,192,768]{2,1,0:T(8,128)(2,1)S(1)}, bf16[1,192,768]{2,1,0:T(8,128)(2,1)S(1)}, u32[]{:S(2)}, u32[]{:S(2)}) collective-permute-start(bf16[1,192,768]{2,1,0:T(8,128)(2,1)S(1)} %collective-permute-done.8.refs_7_), channel_id=1, source_target_pairs={{0,32},{32,0},{64,96},{96,64},{128,160},{160,128},{192,224},{224,1... | collective-permute-start | bytes 884744 | tf_op jit(solution)/shard_map/ppermute | solution.py:389
  140.4 0.0 collective-permute-done.6.refs_5_
  140.4 1.0 collective-permute-done.9.refs_8_
  141.4 0.0 collective-permute-done.7.refs_6_
  141.4 0.0 all-to-all-done.3.in_any
  141.5 8.0 %shard_map.123 = bf16[576,768]{1,0:T(8,128)(2,1)} custom-call(s32[1]{0:T(128)} %bitcast.frame_ref, f32[35,8,128]{2,1,0:T(8,128)S(1)} %copy-done.3, bf16[32,112,128]{2,1,0:T(8,128)(2,1)} %all-to-all-done.3.in_any, bf16[2,768,768]{2,1,0:T(8,128)(2,1)} %constant.25.clone.tables_any, bf16[2,576,768]{2,1,0:T(8,128)(2,1)} %get-tuple-element.36.carry_any, ...), custom_call_target="tpu_custom_call" | custom-call | flops 3397386240 | bytes 10792964 | tf_op jit(solution)/shard_map/pallas_call | solution.py:361
  (15 shorter events, 0.0 us)
Async XLA Ops:
  0.0 14.1 %copy-start.8 = (bf16[1,3,192,768]{3,2,1,0:T(8,128)(2,1)S(1)}, bf16[1,3,192,768]{3,2,1,0:T(8,128)(2,1)}, u32[]{:S(2)}) copy-start(bf16[1,3,192,768]{3,2,1,0:T(8,128)(2,1)} %param.12) | copy-start | bytes 2654212
  0.0 14.3 %copy-start.9 = (bf16[96,768]{1,0:T(8,128)(2,1)S(1)}, bf16[96,768]{1,0:T(8,128)(2,1)}, u32[]{:S(2)}) copy-start(bf16[96,768]{1,0:T(8,128)(2,1)} %param.20) | copy-start | bytes 442372
  0.0 14.3 %copy-start.10 = (bf16[96,768]{1,0:T(8,128)(2,1)S(1)}, bf16[96,768]{1,0:T(8,128)(2,1)}, u32[]{:S(2)}) copy-start(bf16[96,768]{1,0:T(8,128)(2,1)} %param.19) | copy-start | bytes 442372
  0.0 19.1 %copy-start.4 = (f32[3,768]{1,0:T(4,128)S(1)}, f32[3,768]{1,0:T(4,128)}, u32[]{:S(2)}) copy-start(f32[3,768]{1,0:T(4,128)} %gains_ref) | copy-start | bytes 27652
  0.0 19.1 %copy-start.5 = (f32[16]{0:T(128)S(1)}, f32[16]{0:T(128)}, u32[]{:S(2)}) copy-start(f32[16]{0:T(128)} %noise_ref.1) | copy-start | bytes 196
  0.0 19.1 %copy-start.6 = (f32[16]{0:T(128)S(1)}, f32[16]{0:T(128)}, u32[]{:S(2)}) copy-start(f32[16]{0:T(128)} %keep_ref.1) | copy-start | bytes 196
  2.3 36.5 %all-to-all-start = ((bf16[16,9,8,384]{3,2,1,0:T(8,128)(2,1)}), bf16[16,9,8,384]{3,2,1,0:T(8,128)(2,1)S(1)}, u32[]{:S(2)}, u32[]{:S(2)}) async-start(bf16[16,9,8,384]{3,2,1,0:T(8,128)(2,1)} %shard_map.118), calls=%async_computation | async-start | bytes 1769472 | tf_op jit(solution)/shard_map/all_to_all | solution.py:380
  14.1 31.1 %collective-permute-start = (bf16[576,768]{1,0:T(8,128)(2,1)S(1)}, bf16[576,768]{1,0:T(8,128)(2,1)}, u32[]{:S(2)}, u32[]{:S(2)}) collective-permute-start(bf16[576,768]{1,0:T(8,128)(2,1)S(1)} %bitcast.29), channel_id=1, source_target_pairs={{0,480},{32,0},{64,32},{96,64},{128,96},{160,128},{192,160},{224,1... | collective-permute-start | bytes 2654216 | tf_op jit(solution)/shard_map/ppermute | solution.py:385
  14.3 6.0 %collective-permute-start.1 = (bf16[1,192,768]{2,1,0:T(8,128)(2,1)S(1)}, bf16[1,192,768]{2,1,0:T(8,128)(2,1)S(1)}, u32[]{:S(2)}, u32[]{:S(2)}) collective-permute-start(bf16[1,192,768]{2,1,0:T(8,128)(2,1)S(1)} %maximum_bitcast_fusion), channel_id=1, source_target_pairs={{0,32},{32,0},{64,96},{96,64},{128,160},{160,128},{192,224},{224,1... | collective-permute-start | bytes 884744 | tf_op jit(solution)/shard_map/ppermute | solution.py:389
  19.7 47.4 %copy-start.2 = (f32[35,8,128]{2,1,0:T(8,128)}, f32[35,8,128]{2,1,0:T(8,128)S(1)}, u32[]{:S(2)}) copy-start(f32[35,8,128]{2,1,0:T(8,128)S(1)} %shard_map.119.params_ref) | copy-start | bytes 430084
  20.3 46.7 %copy-start.1 = (bf16[384,768]{1,0:T(8,128)(2,1)S(1)}, bf16[384,768]{1,0:T(8,128)(2,1)}, u32[]{:S(2)}) copy-start(bf16[384,768]{1,0:T(8,128)(2,1)} %w_any.3) | copy-start | bytes 1769476
  45.3 21.8 %all-to-all-start.1 = ((bf16[16,112,128]{2,1,0:T(8,128)(2,1)}), bf16[16,112,128]{2,1,0:T(8,128)(2,1)S(1)}, u32[]{:S(2)}, u32[]{:S(2)}) async-start(bf16[16,112,128]{2,1,0:T(8,128)(2,1)} %shard_map.120), calls=%async_computation.1 | async-start | bytes 917504 | tf_op jit(solution)/shard_map/all_to_all | solution.py:380
  71.7 26.8 %copy-start.7 = (bf16[3,2,96,768]{3,2,1,0:T(8,128)(2,1)S(1)}, bf16[3,2,96,768]{3,2,1,0:T(8,128)(2,1)}, u32[]{:S(2)}) copy-start(bf16[3,2,96,768]{3,2,1,0:T(8,128)(2,1)} %constant.27.clone) | copy-start | bytes 2654212
  71.7 35.0 %all-to-all-start.2 = ((bf16[32,112,128]{2,1,0:T(8,128)(2,1)}), bf16[32,112,128]{2,1,0:T(8,128)(2,1)S(1)}, u32[]{:S(2)}, u32[]{:S(2)}) async-start(bf16[32,112,128]{2,1,0:T(8,128)(2,1)} %get-tuple-element.30), calls=%async_computation.2 | async-start | bytes 1835008 | tf_op jit(solution)/shard_map/all_to_all | solution.py:380
  81.5 12.3 %collective-permute-start.3 = (bf16[2,192,768]{2,1,0:T(8,128)(2,1)S(1)}, bf16[2,192,768]{2,1,0:T(8,128)(2,1)}, u32[]{:S(2)}, u32[]{:S(2)}) collective-permute-start(bf16[2,192,768]{2,1,0:T(8,128)(2,1)S(1)} %pad_maximum_fusion.1.refs_0_), channel_id=1, source_target_pairs={{0,64},{32,480},{64,128},{96,32},{128,192},{160,96},{192,256},{224... | collective-permute-start | bytes 1769480 | tf_op jit(solution)/shard_map/ppermute | solution.py:394
  83.5 20.3 %collective-permute-start.2 = (bf16[2,192,768]{2,1,0:T(8,128)(2,1)S(1)}, bf16[2,192,768]{2,1,0:T(8,128)(2,1)}, u32[]{:S(2)}, u32[]{:S(2)}) collective-permute-start(bf16[2,192,768]{2,1,0:T(8,128)(2,1)S(1)} %pad_maximum_fusion.1.refs_0_), channel_id=1, source_target_pairs={{0,128},{32,416},{64,192},{96,480},{128,256},{160,32},{192,320},{2... | collective-permute-start | bytes 1769480 | tf_op jit(solution)/shard_map/ppermute | solution.py:394
  93.8 9.9 %collective-permute-start.4 = (bf16[2,192,768]{2,1,0:T(8,128)(2,1)}, bf16[2,192,768]{2,1,0:T(8,128)(2,1)}, u32[]{:S(2)}, u32[]{:S(2)}) collective-permute-start(bf16[2,192,768]{2,1,0:T(8,128)(2,1)} %collective-permute-done.3.refs_1_), channel_id=1, source_target_pairs={{0,32},{32,0},{64,96},{96,64},{128,160},{160,128},{192,224},{224,1... | collective-permute-start | bytes 1769480 | tf_op jit(solution)/shard_map/ppermute | solution.py:389
  108.7 0.9 copy-start
  109.6 31.8 %copy-start.3 = (f32[35,8,128]{2,1,0:T(8,128)S(1)}, f32[35,8,128]{2,1,0:T(8,128)}, u32[]{:S(2)}) copy-start(f32[35,8,128]{2,1,0:T(8,128)} %copy-done.2) | copy-start | bytes 430084
  109.6 31.8 %all-to-all-start.3 = ((bf16[32,112,128]{2,1,0:T(8,128)(2,1)}), bf16[32,112,128]{2,1,0:T(8,128)(2,1)}, u32[]{:S(2)}, u32[]{:S(2)}) async-start(bf16[32,112,128]{2,1,0:T(8,128)(2,1)} %copy-done), calls=%async_computation.3 | async-start | bytes 1835008 | tf_op jit(solution)/shard_map/all_to_all | solution.py:380
  116.0 16.0 %collective-permute-start.5 = (bf16[2,192,768]{2,1,0:T(8,128)(2,1)}, bf16[2,192,768]{2,1,0:T(8,128)(2,1)S(1)}, u32[]{:S(2)}, u32[]{:S(2)}) collective-permute-start(bf16[2,192,768]{2,1,0:T(8,128)(2,1)} %collective-permute-done.2.refs_3_), channel_id=1, source_target_pairs={{0,64},{32,480},{64,128},{96,32},{128,192},{160,96},{192,256},{224... | collective-permute-start | bytes 1769480 | tf_op jit(solution)/shard_map/ppermute | solution.py:394
  122.7 17.7 %collective-permute-start.6 = (bf16[2,192,768]{2,1,0:T(8,128)(2,1)}, bf16[2,192,768]{2,1,0:T(8,128)(2,1)S(1)}, u32[]{:S(2)}, u32[]{:S(2)}) collective-permute-start(bf16[2,192,768]{2,1,0:T(8,128)(2,1)} %collective-permute-done.2.refs_3_), channel_id=1, source_target_pairs={{0,32},{32,0},{64,96},{96,64},{128,160},{160,128},{192,224},{224,1... | collective-permute-start | bytes 1769480 | tf_op jit(solution)/shard_map/ppermute | solution.py:389
  125.7 11.4 %collective-permute-start.8 = (bf16[1,192,768]{2,1,0:T(8,128)(2,1)S(1)}, bf16[1,192,768]{2,1,0:T(8,128)(2,1)S(1)}, u32[]{:S(2)}, u32[]{:S(2)}) collective-permute-start(bf16[1,192,768]{2,1,0:T(8,128)(2,1)S(1)} %slice.11), channel_id=1, source_target_pairs={{0,128},{32,416},{64,192},{96,480},{128,256},{160,32},{192,320},{2... | collective-permute-start | bytes 884744 | tf_op jit(solution)/shard_map/ppermute | solution.py:394
  132.0 9.4 %collective-permute-start.7 = (bf16[2,192,768]{2,1,0:T(8,128)(2,1)S(1)}, bf16[2,192,768]{2,1,0:T(8,128)(2,1)S(1)}, u32[]{:S(2)}, u32[]{:S(2)}) collective-permute-start(bf16[2,192,768]{2,1,0:T(8,128)(2,1)S(1)} %collective-permute-done.5.refs_4_), channel_id=1, source_target_pairs={{0,32},{32,0},{64,96},{96,64},{128,160},{160,128},{192,224},{224,1... | collective-permute-start | bytes 1769480 | tf_op jit(solution)/shard_map/ppermute | solution.py:389
  137.1 4.3 %collective-permute-start.9 = (bf16[1,192,768]{2,1,0:T(8,128)(2,1)S(1)}, bf16[1,192,768]{2,1,0:T(8,128)(2,1)S(1)}, u32[]{:S(2)}, u32[]{:S(2)}) collective-permute-start(bf16[1,192,768]{2,1,0:T(8,128)(2,1)S(1)} %collective-permute-done.8.refs_7_), channel_id=1, source_target_pairs={{0,32},{32,0},{64,96},{96,64},{128,160},{160,128},{192,224},{224,1... | collective-permute-start | bytes 884744 | tf_op jit(solution)/shard_map/ppermute | solution.py:389
